TPU v7x, 32 devices: a whole 2x2x4 slice. The times are simulated.
32 devices in a mesh: row: 8 (over z, x), col: 4 (over y, core).
Axes of the slice: x: 2, y: 2, z: 4, core: 2. Of those that a mesh axis runs over, the one named last changes fastest.
Arguments:
- tile_values: bfloat16 [8, 4, 360, 128, 128], P('row', 'col')
- tile_places: int32 [8, 4, 2, 360], P('row', 'col'), may hold values from 0 to 47, as said below
- tile_counts: int32 [8, 4], P('row', 'col'), may hold values from 90 to 360, as said below
- sketch: bfloat16 [24576, 512], P('col'), may hold values from -6 to 6
Outputs:
- range_basis: float32 [24576, 512], P(('row', 'col'))
- triangle: float32 [512, 512], replicated
Inputs may be any that keep to these rules, and one draw needn't show every extreme that they name: `tile_places`: entry [r, c, 0, t] is the slot's tile row among the 24 tile rows of row block r and entry [r, c, 1, t] its tile column among the 48 tile columns of column block c; the 360 slots of one block pair name distinct positions, padded slots included. Slots t < tile_counts[r, c] hold the live tiles of block pair (r, c); later slots are padding and contribute nothing. Some block pair holds exactly 360 live tiles.
All inputs are finite; a program needn't handle non-finite values.
Results may differ from a plain program's by a relative error of at most 0.0003.
Values sent between devices are 32-bit elements; how exact they have to be, the bound alone decides.
No kernel may reach another device: no remote copies, remote signals or barrier semaphores. Data moves between devices by JAX's collectives and lax.ppermute only.
A program may use at most 192 MiB of HBM per device.

v0:
```python
import functools
import math

import jax
import jax.numpy as jnp
from jax import lax
from jax.experimental import pallas as pl
from jax.experimental.pallas import tpu as pltpu
from jax.sharding import PartitionSpec as P

BF16 = jnp.bfloat16
F32 = jnp.float32
PAIR = 2
TURN = 8
CHUNKS = 3
BLOCK = 128
SMEM = pl.BlockSpec(memory_space=pltpu.SMEM)
VMEM = pl.BlockSpec(memory_space=pltpu.VMEM)
ANY = pl.BlockSpec(memory_space=pl.ANY)


def params(size):
    return pltpu.CompilerParams(vmem_limit_bytes=size)


def halves(x):
    high = x.astype(BF16)
    return high, (x - high.astype(F32)).astype(BF16)


def tile_kernel(resident, span, chunks, flip, stride, counts, places, tiles, panels, *refs):
    outs = refs[: 2 * chunks]
    refs = refs[2 * chunks :]
    acc, tile_buf, panel_buf, key, fill, slot, column, first_of, key_of = refs[:9]
    tile_sem, panel_sem, out_sem = refs[9:]
    slots = tiles.shape[0]
    blocks = acc.shape[0]
    per_owner = key.shape[0] // lax.axis_size("col")
    here = blocks // 2
    bulk_copy = pltpu.make_async_copy(tiles, tile_buf.at[pl.ds(0, slots)], tile_sem.at[0])
    bulk_copy.start()
    if resident:
        panel_copy = pltpu.make_async_copy(panels, panel_buf, panel_sem.at[0])
        panel_copy.start()
    live = counts[0, 0]
    own = lax.axis_index("col")

    for owner in range(key.shape[0] // per_owner):
        base = jnp.where((owner & 1) == (own & 1), here, 0)
        wanted = (owner >> 1) == ((own >> 1) ^ flip)
        for inside in range(per_owner):
            name = jnp.where(wanted, base + inside - span[0], blocks)
            key[owner * per_owner + inside] = name if span[0] <= inside < span[1] else blocks
    for k in range(blocks + 1):
        fill[k] = k * stride

    unroll = math.gcd(slots, 8)

    def put(g, carry):
        for i in range(unroll):
            t = g * unroll + i
            k = jnp.where(t < live, key[places[0, t]], blocks)
            p = fill[k]
            fill[k] = p + 1
            slot[p] = t
            column[p] = places[1, t]
        return carry

    lax.fori_loop(0, (live + unroll - 1) // unroll, put, 0)

    empty = blocks * stride + slots
    for i in range(PAIR):
        slot[empty + i] = slots
        column[empty + i] = 0
    number, bounds = 0, [0]
    for k in range(blocks):
        size = fill[k] - k * stride
        for i in range(PAIR - 1):
            slot[fill[k] + i] = slots
            column[fill[k] + i] = 0

        def add_pair(j, at, k=k):
            first_of[at + j] = k * stride + j * PAIR
            key_of[at + j] = k
            return at

        pairs = (size + PAIR - 1) // PAIR
        lax.fori_loop(0, pairs, add_pair, number)
        number += pairs
        if (k + 1) % here == 0:
            for i in range(TURN - 1):
                first_of[number + i] = empty
                key_of[number + i] = k
            number = (number + TURN - 1) // TURN * TURN
            bounds.append(number // TURN)
    acc[...] = jnp.zeros_like(acc)
    tile_buf[slots] = jnp.zeros_like(tile_buf[slots])
    bulk_copy.wait()
    if resident:
        panel_copy.wait()

    def turn(g, carry):
        firsts = [first_of[g * TURN + i] for i in range(TURN)]
        if not resident:
            copies = [
                pltpu.make_async_copy(
                    panels.at[column[firsts[i] + j]],
                    panel_buf.at[i * PAIR + j],
                    panel_sem.at[i * PAIR + j],
                )
                for i in range(TURN)
                for j in range(PAIR)
            ]
            for copy in copies:
                copy.start()
            for copy in copies:
                copy.wait()
        for i, at in enumerate(firsts):
            left = jnp.concatenate([tile_buf[slot[at + j]] for j in range(PAIR)], axis=1)
            right = jnp.concatenate(
                [
                    panel_buf[column[at + j] if resident else i * PAIR + j]
                    for j in range(PAIR)
                ],
                axis=0,
            )
            acc[key_of[g * TURN + i]] += jnp.dot(left, right, preferred_element_type=F32)
        return carry

    size = here // chunks
    copies = []
    for half in range(2):
        lax.fori_loop(bounds[half], bounds[half + 1], turn, 0)
        for n in range(half * chunks, (half + 1) * chunks):
            copy = pltpu.make_async_copy(acc.at[pl.ds(n * size, size)], outs[n], out_sem.at[n])
            copy.start()
            copies.append(copy)
    for copy in copies:
        copy.wait()


def tile_products(counts, places, tiles, panels, tile_rows, span, chunks, flip, limit):
    slots, size, _ = tiles.shape
    width = panels.shape[2]
    blocks = (span[1] - span[0]) * 2
    stride = (min(slots, panels.shape[0]) // PAIR + 1) * PAIR
    entries = blocks * stride + slots + PAIR
    pairs = blocks * stride // PAIR + 2 * TURN
    resident = panels.size * 2 <= 16 << 20
    panel_shape = (panels.shape[0] if resident else PAIR * TURN, size, width)
    used = blocks * size * width * 4 + (slots + 1) * size * size * 2 + math.prod(panel_shape) * 2
    piece = jax.ShapeDtypeStruct((blocks // 2 // chunks, size, width), F32)
    return pl.pallas_call(
        functools.partial(tile_kernel, resident, span, chunks, flip, stride),
        out_shape=[piece] * (2 * chunks),
        in_specs=[SMEM, SMEM, ANY, ANY],
        out_specs=[ANY] * (2 * chunks),
        scratch_shapes=[
            pltpu.VMEM((blocks, size, width), F32),
            pltpu.VMEM((slots + 1, size, size), BF16),
            pltpu.VMEM(panel_shape, BF16),
            pltpu.SMEM((tile_rows,), jnp.int32),
            pltpu.SMEM((blocks + 1,), jnp.int32),
            pltpu.SMEM((entries,), jnp.int32),
            pltpu.SMEM((entries,), jnp.int32),
            pltpu.SMEM((pairs,), jnp.int32),
            pltpu.SMEM((pairs,), jnp.int32),
            pltpu.SemaphoreType.DMA((1,)),
            pltpu.SemaphoreType.DMA((1 if resident else PAIR * TURN,)),
            pltpu.SemaphoreType.DMA((2 * chunks,)),
        ],
        compiler_params=params(max(limit, used + (6 << 20))),
        cost_estimate=pl.CostEstimate(
            flops=slots * size * size * width,
            bytes_accessed=tiles.size + panels.size * 2,
            transcendentals=0,
        ),
    )(counts, places, tiles, panels)


def block_list(order):
    return [(i, j) for i in range(order) for j in range(i + 1)]


def gram_kernel(last, *refs):
    if last:
        keep, core, across, *earlier, rows, own, send, acc = refs
    else:
        keep, core, across, rows, acc = refs
    total = (keep[...] + core[...]) + across[...]
    total = total.reshape(rows.shape)
    rows[...] = total
    high, low = halves(total)
    left = jnp.concatenate([high, high, low], axis=0)
    right = jnp.concatenate([high, low, high], axis=0)
    order = rows.shape[1] // BLOCK
    for i in range(order):
        strip = lax.dot_general(
            left[:, i * BLOCK : (i + 1) * BLOCK],
            right[:, : (i + 1) * BLOCK],
            (((0,), (0,)), ((), ())),
            preferred_element_type=F32,
        )
        for j in range(i + 1):
            at = pl.ds((i * (i + 1) // 2 + j) * BLOCK, BLOCK)
            part = strip[:, j * BLOCK : (j + 1) * BLOCK]
            if last:
                for gram in earlier:
                    part = part + gram[at]
            acc[at] = part
    if last:
        core_bit, me = place()
        size = own.shape[1]
        half = acc.shape[0] // 2
        for d in range(own.shape[0]):
            at = (me ^ d) * size
            own[d] = acc[pl.ds(pl.multiple_of(core_bit * half + at, 8), size)]
            send[d] = acc[pl.ds(pl.multiple_of((1 - core_bit) * half + at, 8), size)]


def place():
    row, col = lax.axis_index("row"), lax.axis_index("col")
    return col & 1, (row & 1) | (col & 2)


def gram_chunk(keep, core, across, earlier, last):
    width = keep.shape[2]
    rows = keep.shape[0] * keep.shape[1]
    number = len(block_list(width // BLOCK)) * BLOCK
    whole = jax.ShapeDtypeStruct((number, BLOCK), F32)
    pieces = jax.ShapeDtypeStruct((4, number // 8, BLOCK), F32)
    row_shape = jax.ShapeDtypeStruct((rows, width), F32)
    args = [keep, core, across] + (list(earlier) if last else [])
    outs = [row_shape] + ([pieces, pieces] if last else [whole])
    return pl.pallas_call(
        functools.partial(gram_kernel, last),
        out_shape=outs,
        in_specs=[VMEM] * len(args),
        out_specs=[VMEM] * len(outs),
        scratch_shapes=[pltpu.VMEM(whole.shape, F32)] if last else [],
        compiler_params=params(16 << 20),
        cost_estimate=pl.CostEstimate(
            flops=4 * rows * width * width, bytes_accessed=rows * width * 16, transcendentals=0
        ),
    )(*args)


def swapped(x, row_flip, col_flip):
    rows, cols = lax.axis_size("row"), lax.axis_size("col")
    if not row_flip:
        return lax.ppermute(x, "col", [(c, c ^ col_flip) for c in range(cols)])
    if not col_flip:
        return lax.ppermute(x, "row", [(r, r ^ row_flip) for r in range(rows)])
    route = [
        (r * cols + c, (r ^ row_flip) * cols + (c ^ col_flip))
        for r in range(rows)
        for c in range(cols)
    ]
    return lax.ppermute(x, ("row", "col"), route)


FLIPS = ((1, 0), (0, 2), (1, 2))


def gram_sum(own, send):
    theirs = swapped(send, 0, 1)
    part = [own[d] + theirs[d] for d in range(4)]
    got = [swapped(x, *flip) for x, flip in zip(part[1:], FLIPS)]
    piece = (part[0] + got[0]) + (got[1] + got[2])
    bits = lax.axis_size("row").bit_length() - 1
    bit = 1
    while bit < bits:
        if bit + 1 < bits:
            a, b = 1 << bit, 2 << bit
            got = [swapped(piece, flip, 0) for flip in (a, b, a | b)]
            piece = (piece + got[0]) + (got[1] + got[2])
            bit += 2
        else:
            piece = piece + swapped(piece, 1 << bit, 0)
            bit += 1
    mine = [piece] + [swapped(piece, *flip) for flip in FLIPS]
    return mine, [swapped(x, 0, 1) for x in mine]


def against(left, right_rows):
    lh, ll = left
    rh, rl = right_rows
    return lax.dot_general(
        jnp.concatenate([lh, lh, ll], axis=1),
        jnp.concatenate([rh, rl, rh], axis=1),
        (((1,), (1,)), ((), ())),
        preferred_element_type=F32,
    )


def times(left, right):
    lh, ll = left
    rh, rl = right
    return jnp.dot(
        jnp.concatenate([lh, lh, ll], axis=1),
        jnp.concatenate([rh, rl, rh], axis=0),
        preferred_element_type=F32,
    )


def factor_kernel(chunks, scale, rounds, *refs):
    pieces, rows = refs[:8], refs[8 : 8 + chunks]
    basis, triangle, gram_out, flag = refs[8 + chunks : 12 + chunks]
    blocks, gram, w, wh, wl, gh, gl, yh, yl, ph = refs[12 + chunks :]
    size = gram.shape[0]
    order = size // BLOCK
    core_bit, me = place()
    half = blocks.shape[0] // 2
    for n, piece in enumerate(pieces):
        at = (core_bit ^ (n // 4)) * half + (me ^ (n % 4)) * piece.shape[0]
        blocks[pl.ds(pl.multiple_of(at, 8), piece.shape[0])] = piece[...]
    at = [slice(i * BLOCK, (i + 1) * BLOCK) for i in range(order)]
    for n, (i, j) in enumerate(block_list(order)):
        block = blocks[n * BLOCK : (n + 1) * BLOCK]
        gram[at[i], at[j]] = block
        if i != j:
            gram[at[j], at[i]] = block.T
    high, low = halves(gram[...])
    gh[...] = high
    gl[...] = low
    gram_out[...] = gram[...]

    def index(i):
        shape = (BLOCK, size)
        return (
            lax.broadcasted_iota(jnp.int32, shape, 0) + i * BLOCK,
            lax.broadcasted_iota(jnp.int32, shape, 1),
        )

    def phi(error, i):
        r, c = index(i)
        r, c = r[:, : error.shape[1]], c[:, : error.shape[1]]
        return jnp.where(r > c, error, jnp.where(r == c, 0.5 * error, 0.0))

    row_scale, col_scale = [], []
    for i in range(order):
        block = gram[at[i], at[i]]
        r, c = index(0)
        diagonal = jnp.where(r[:, :BLOCK] == c[:, :BLOCK], block, 0.0)
        row_scale.append(lax.rsqrt(jnp.sum(diagonal, axis=1, keepdims=True)))
        col_scale.append(lax.rsqrt(jnp.sum(diagonal, axis=0, keepdims=True)))
    col_scale = jnp.concatenate(col_scale, axis=1)
    for i in range(order):
        r, c = index(i)
        same = jnp.where(r == c, 1.0, 0.0)
        error = gram[at[i], :] * row_scale[i] * col_scale - same
        w[at[i], :] = (same - phi(error, i)) * col_scale

    def split_w():
        for i in range(order):
            high, low = halves(w[at[i], :])
            wh[at[i], :] = high
            wl[at[i], :] = low

    def step(exact):
        split_w()
        for i in range(order):
            if exact:
                y = against((gh[at[i], :], gl[at[i], :]), (wh[...], wl[...]))
            else:
                y = lax.dot_general(
                    gh[at[i], :], wh[...], (((1,), (1,)), ((), ())), preferred_element_type=F32
                )
            high, low = halves(y)
            yh[at[i], :] = high
            yl[at[i], :] = low
        norm = jnp.zeros((1, 1), F32)
        for i in range(order):
            k = (i + 1) * BLOCK
            if exact:
                m = times((wh[at[i], :k], wl[at[i], :k]), (yh[:k, :k], yl[:k, :k]))
            else:
                m = jnp.dot(wh[at[i], :k], yh[:k, :k], preferred_element_type=F32)
            r, c = index(i)
            p = phi(m - jnp.where(r[:, :k] == c[:, :k], 1.0, 0.0), i)
            ph[at[i], :k] = p.astype(BF16)
            norm = norm + jnp.sum(p * p, keepdims=True)
        for i in range(order):
            k = (i + 1) * BLOCK
            w[at[i], :k] -= jnp.dot(ph[at[i], :k], wh[:k, :k], preferred_element_type=F32)
        return jnp.sum(norm)

    step(False)

    def not_done(state):
        count, norm = state
        return jnp.logical_and(count < rounds, jnp.logical_not(norm < 2.5e-5))

    def again(state):
        count, _ = state
        return count + 1, step(True)

    _, norm = lax.while_loop(not_done, again, (jnp.int32(0), jnp.float32(1.0)))
    flag[0] = jnp.where(norm < 2.5e-5, 1, 0).astype(jnp.int32)
    split_w()
    for i in range(order):
        k = (i + 1) * BLOCK
        upper = times((wh[at[i], :k], wl[at[i], :k]), (gh[:k, :], gl[:k, :]))
        r, c = index(i)
        triangle[at[i], :] = jnp.where(r <= c, upper, 0.0) * (1.0 / scale)
    first = 0
    for part in rows:
        size = part.shape[0]
        out = against(halves(part[...]), (wh[...], wl[...]))
        basis[pl.ds(first, size), :] = out * scale
        first += size


def factor(pieces, rows, scale):
    width = rows[0].shape[1]
    square = (width, width)
    local = sum(part.shape[0] for part in rows)
    number = len(block_list(width // BLOCK))
    return pl.pallas_call(
        functools.partial(factor_kernel, len(rows), scale, 12),
        out_shape=[
            jax.ShapeDtypeStruct((local, width), F32),
            jax.ShapeDtypeStruct(square, F32),
            jax.ShapeDtypeStruct(square, F32),
            jax.ShapeDtypeStruct((1,), jnp.int32),
        ],
        in_specs=[VMEM] * (8 + len(rows)),
        out_specs=[VMEM, VMEM, VMEM, SMEM],
        scratch_shapes=[
            pltpu.VMEM((number * BLOCK, BLOCK), F32),
            pltpu.VMEM(square, F32),
            pltpu.VMEM(square, F32),
        ]
        + [pltpu.VMEM(square, BF16)] * 7,
        compiler_params=params(24 << 20),
    )(*pieces, *rows)


def direct(gram, rows, scale):
    lower = jnp.linalg.cholesky(gram)
    own_rows = jnp.concatenate(rows, axis=0)
    basis = jax.scipy.linalg.solve_triangular(lower, own_rows.T, lower=True).T * scale
    return basis, lower.T / scale


def body(tile_values, tile_places, tile_counts, sketch):
    tiles = tile_values[0, 0]
    size = tiles.shape[1]
    width = sketch.shape[1]
    row_devices = lax.axis_size("row")
    col_devices = lax.axis_size("col")
    local_rows = sketch.shape[0] // row_devices
    tile_rows = local_rows * col_devices // size
    panels = sketch.reshape(-1, size, width)
    places = tile_places[0, 0]
    scale = math.sqrt(local_rows * row_devices * col_devices)
    per_owner = tile_rows // col_devices
    chunks = math.gcd(CHUNKS, per_owner)

    def products(first, last, flip, limit):
        span = (first * per_owner // chunks, last * per_owner // chunks)
        out = tile_products(
            tile_counts, places, tiles, panels, tile_rows, span, last - first, flip, limit
        )
        return out[: last - first], out[last - first :]

    across = []
    for first, last in ((0, 1), (1, chunks))[: min(2, chunks)]:
        send, keep = products(first, last, 1, 56 << 20)
        own = [k + swapped(x, 0, 1) for k, x in zip(keep, send)]
        places, *own = lax.optimization_barrier((places, *own))
        across += [swapped(x, 0, 2) for x in own]
    send, keep = products(0, chunks, 0, 0)
    rows, grams = [], []
    for n in range(chunks):
        last = n == chunks - 1
        out = gram_chunk(keep[n], swapped(send[n], 0, 1), across[n], grams, last)
        rows.append(out[0])
        grams.append(out[1])
    mine, theirs = gram_sum(*out[1:])
    basis, triangle, gram, flag = factor(mine + theirs, rows, scale)
    return lax.cond(
        flag[0] == 1,
        lambda: (basis, triangle),
        lambda: direct(gram, rows, scale),
    )


def solution(mesh):
    in_specs = (
        P("row", "col", None, None, None),
        P("row", "col", None, None),
        P("row", "col"),
        P("col", None),
    )
    out_specs = (P(("row", "col"), None), P())
    return jax.shard_map(body, mesh=mesh, in_specs=in_specs, out_specs=out_specs, check_vma=False)
```

profile of v0, /device:TPU:0, one launch (start us, length us, event | category | flops | bytes accessed | tf_op | source)
XLA Modules:
  0.0 301.2 jit_solution(17475994781364582203)
XLA Ops:
  1.3 8.6 %shard_map.63 = (f32[2,128,512]{2,1,0:T(8,128)}, f32[2,128,512]{2,1,0:T(8,128)}) custom-call(s32[1,1]{1,0:T(1,128)S(6)} %copy.38.counts, s32[2,360]{1,0:T(2,128)} %bitcast.78, bf16[360,128,128]{2,1,0:T(8,128)(2,1)} %bitcast.70, bf16[48,128,512]{2,1,0:T(8,128)(2,1)} %bitcast.73), custom_call_target="tpu_custom_call" | custom-call | flops 3019898880 | bytes 12189696 | tf_op jit(solution)/shard_map/pallas_call | solution.py:153
  10.8 1.7 collective-permute-done
  12.6 1.3 add.92
  13.9 9.8 %shard_map.64 = (f32[2,128,512]{2,1,0:T(8,128)}, f32[2,128,512]{2,1,0:T(8,128)}, f32[2,128,512]{2,1,0:T(8,128)}, f32[2,128,512]{2,1,0:T(8,128)}) custom-call(s32[1,1]{1,0:T(1,128)S(6)} %copy.38.counts, s32[2,360]{1,0:T(2,128)} %bitcast.79, bf16[360,128,128]{2,1,0:T(8,128)(2,1)} %bitcast.71, bf16[48,128,512]{2,1,0:T(8,128)(2,1)} %bitcast.74), custom_call_target="tpu_custom_call" | custom-call | flops 3019898880 | bytes 12189696 | tf_op jit(solution)/shard_map/pallas_call | solution.py:153
  23.7 1.4 collective-permute-start.1
  25.2 3.7 %collective-permute-start.6 = (f32[2,128,512]{2,1,0:T(8,128)S(1)}, f32[2,128,512]{2,1,0:T(8,128)S(1)}, u32[]{:S(2)}, u32[]{:S(2)}) collective-permute-start(f32[2,128,512]{2,1,0:T(8,128)S(1)} %add.92), channel_id=1, source_target_pairs={{0,2},{1,3},{2,0},{3,1},{4,6},{5,7},{6,4},{7,5},{8,10},{9,11},{10,... | collective-permute-start | bytes 1572872 | tf_op jit(solution)/shard_map/ppermute | solution.py:251
  30.2 4.3 %copy-done = bf16[1,1,360,128,128]{4,3,2,1,0:T(8,128)(2,1)S(1)} copy-done((bf16[1,1,360,128,128]{4,3,2,1,0:T(8,128)(2,1)S(1)}, bf16[1,1,360,128,128]{4,3,2,1,0:T(8,128)(2,1)}, u32[]{:S(2)}) %copy-start) | copy-done | bytes 11796504
  34.5 5.4 %shard_map.65 = (f32[2,128,512]{2,1,0:T(8,128)S(1)}, f32[2,128,512]{2,1,0:T(8,128)S(1)}, f32[2,128,512]{2,1,0:T(8,128)S(1)}, f32[2,128,512]{2,1,0:T(8,128)S(1)},...) custom-call(s32[1,1]{1,0:T(1,128)S(6)} %copy.38.counts, s32[2,360]{1,0:T(2,128)S(1)} %bitcast.80, ...), custom_call_target="tpu_custom_call" | custom-call | flops 3019898880 | bytes 12189696 | tf_op jit(solution)/shard_map/pallas_call | solution.py:153
  40.0 4.2 %collective-permute-start.5 = (f32[2,128,512]{2,1,0:T(8,128)S(1)}, f32[2,128,512]{2,1,0:T(8,128)S(1)}, u32[]{:S(2)}, u32[]{:S(2)}) collective-permute-start(f32[2,128,512]{2,1,0:T(8,128)S(1)} %get-tuple-element.58), channel_id=1, source_target_pairs={{0,1},{1,0},{2,3},{3,2},{4,5},{5,4},{6,7},{7,6},{8,9},{9,8},{10,11... | collective-permute-start | bytes 1572872 | tf_op jit(solution)/shard_map/ppermute | solution.py:251
  44.2 3.3 %collective-permute-start.8 = (f32[2,128,512]{2,1,0:T(8,128)S(1)}, f32[2,128,512]{2,1,0:T(8,128)S(1)}, u32[]{:S(2)}, u32[]{:S(2)}) collective-permute-start(f32[2,128,512]{2,1,0:T(8,128)S(1)} %add.93), channel_id=1, source_target_pairs={{0,2},{1,3},{2,0},{3,1},{4,6},{5,7},{6,4},{7,5},{8,10},{9,11},{10,... | collective-permute-start | bytes 1572872 | tf_op jit(solution)/shard_map/ppermute | solution.py:251
  48.6 11.6 %collective-permute-done.8.refs_2_ = f32[2,128,512]{2,1,0:T(8,128)S(1)} collective-permute-done((f32[2,128,512]{2,1,0:T(8,128)S(1)}, f32[2,128,512]{2,1,0:T(8,128)S(1)}, u32[]{:S(2)}, u32[]{:S(2)}) %collective-permute-start.8) | collective-permute-done | bytes 524320 | tf_op jit(solution)/shard_map/ppermute | solution.py:251
  61.2 9.6 %collective-permute-done.4.refs_2_ = f32[2,128,512]{2,1,0:T(8,128)S(1)} collective-permute-done((f32[2,128,512]{2,1,0:T(8,128)S(1)}, f32[2,128,512]{2,1,0:T(8,128)S(1)}, u32[]{:S(2)}, u32[]{:S(2)}) %collective-permute-start.4) | collective-permute-done | bytes 524320 | tf_op jit(solution)/shard_map/ppermute | solution.py:251
  71.9 1.6 collective-permute-done.9
  73.7 1.8 collective-permute-start.11
  75.5 1.7 collective-permute-start.10
  77.1 2.3 collective-permute-done.12
  81.1 4.9 %collective-permute-start.15 = (f32[160,128]{1,0:T(8,128)S(1)}, f32[160,128]{1,0:T(8,128)S(1)}, u32[]{:S(2)}, u32[]{:S(2)}) collective-permute-start(f32[160,128]{1,0:T(8,128)S(1)} %fusion.37), channel_id=1, source_target_pairs={{0,24},{4,28},{8,16},{12,20},{16,8},{20,12},{24,0},{28,4},{1,25},{... | collective-permute-start | bytes 245768 | tf_op jit(solution)/shard_map/ppermute | solution.py:253
  86.7 2.4 collective-permute-done.15
  89.0 3.3 %collective-permute-done.14 = f32[160,128]{1,0:T(8,128)S(1)} collective-permute-done((f32[160,128]{1,0:T(8,128)S(1)}, f32[160,128]{1,0:T(8,128)S(1)}, u32[]{:S(2)}, u32[]{:S(2)}) %collective-permute-start.14) | collective-permute-done | bytes 81952 | tf_op jit(solution)/shard_map/ppermute | solution.py:253
  92.4 1.6 collective-permute-start.18
  95.9 2.6 collective-permute-done.18.refs_3_
  100.7 40.0 %shard_map.69 = (f32[768,512]{1,0:T(8,128)}, f32[512,512]{1,0:T(8,128)}, f32[512,512]{1,0:T(8,128)S(1)}, s32[1]{0:T(128)}) custom-call(f32[160,128]{1,0:T(8,128)S(1)} %add_add_fusion.refs_0_, f32[160,128]{1,0:T(8,128)S(1)} %collective-permute-done.16.refs_1_, f32[160,128]{1,0:T(8,128)S(1)} %collective-permute-done.17.refs_2_, ...), custom_call_target="tpu_custom_call" | custom-call | tf_op jit(solution)/shard_map/pallas_call | solution.py:419
  141.3 158.8 %conditional.1 = ((f32[768,512]{1,0:T(8,128)}, f32[512,512]{1,0:T(8,128)})) conditional(s32[]{:T(128)} %bitcast.21, (f32[512,512]{1,0:T(8,128)S(1)}, f32[256,512]{1,0:T(8,128)S(1)}, f32[256,512]{1,0:T(8,128)}, f32[256,512]{1,0:T(8,128)}) %tuple.18, (f32[768,512]{1,0:T(8,128)}, f32[512,512]{1,0:T(8,128)}) %tuple.19), branch_computations={%region_0.9_spmd, %region_9.10_spmd} | conditional | flops 1918272000 | bytes 37753128 | solution.py:482
  141.7 1.3 maximum_bitcast_fusion
  143.0 1.4 copy.11
  144.4 1.4 fusion.6
  146.9 11.7 %cholesky.5 = f32[128,128]{1,0:T(8,128)S(1)} custom-call(f32[128,128]{1,0:T(8,128)S(1)} %cholesky.100), custom_call_target="Cholesky" | custom-call | tf_op jit(solution)/shard_map/cond/branch_0_fun/jit(cholesky)/cholesky | solution.py:440
  158.6 9.8 %custom-call.27 = f32[1,128,128]{1,2,0:T(8,128)S(1)} custom-call(f32[1,128,128]{2,1,0:T(8,128)S(1)} %get-tuple-element.117), custom_call_target="InvertDiagBlocksLowerTriangular" | custom-call | tf_op jit(solution)/shard_map/cond/branch_0_fun/jit(cholesky)/cholesky | solution.py:440
  168.6 1.2 constant_dynamic-update-slice_fusion.3
  169.8 1.3 convolution_subtract_fusion.3
  171.1 11.7 %cholesky.29 = f32[128,128]{1,0:T(8,128)S(1)} custom-call(f32[128,128]{1,0:T(8,128)S(1)} %cholesky.104), custom_call_target="Cholesky" | custom-call | tf_op jit(solution)/shard_map/cond/branch_0_fun/jit(cholesky)/cholesky | solution.py:440
  184.8 9.9 %custom-call.28 = f32[1,128,128]{1,2,0:T(8,128)S(1)} custom-call(f32[1,128,128]{2,1,0:T(8,128)S(1)} %get-tuple-element.114), custom_call_target="InvertDiagBlocksLowerTriangular" | custom-call | tf_op jit(solution)/shard_map/cond/branch_0_fun/jit(cholesky)/cholesky | solution.py:440
  195.0 1.3 convolution_subtract_fusion.4
  196.3 11.7 %cholesky.62 = f32[128,128]{1,0:T(8,128)S(1)} custom-call(f32[128,128]{1,0:T(8,128)S(1)} %cholesky.111), custom_call_target="Cholesky" | custom-call | tf_op jit(solution)/shard_map/cond/branch_0_fun/jit(cholesky)/cholesky | solution.py:440
  209.4 9.8 %custom-call.29 = f32[1,128,128]{1,2,0:T(8,128)S(1)} custom-call(f32[1,128,128]{2,1,0:T(8,128)S(1)} %get-tuple-element.111), custom_call_target="InvertDiagBlocksLowerTriangular" | custom-call | tf_op jit(solution)/shard_map/cond/branch_0_fun/jit(cholesky)/cholesky | solution.py:440
  220.7 11.7 %cholesky.89 = f32[128,128]{1,0:T(8,128)S(1)} custom-call(f32[128,128]{1,0:T(8,128)S(1)} %convolution_subtract_fusion.5), custom_call_target="Cholesky" | custom-call | tf_op jit(solution)/shard_map/cond/branch_0_fun/jit(cholesky)/cholesky | solution.py:440
  233.8 1.6 multiply_bitcast_fusion
  235.4 2.5 copy.18
  238.0 11.6 %while.1 = (s32[]{:T(128)}, f32[512,512]{1,0:T(8,128)}, s32[4,2]{0,1:T(2,128)S(1)}, f32[4,128,128]{2,1,0:T(8,128)S(1)}, s32[]{:T(128)}) while((s32[]{:T(128)}, f32[512,512]{1,0:T(8,128)}, s32[4,2]{0,1:T(2,128)S(1)}, f32[4,128,128]{2,1,0:T(8,128)S(1)}, s32[]{:T(128)}) %tuple.56), condition=%wide.while_cond, body=%wide.while_body.sunk | while | flops 2 | bytes 131189 | solution.py:442
  238.6 2.2 bitcast_dynamic-update-slice_fusion.2
  241.6 2.2 bitcast_dynamic-update-slice_fusion.2
  244.5 2.2 bitcast_dynamic-update-slice_fusion.2
  247.4 2.2 bitcast_dynamic-update-slice_fusion.2
  249.6 39.3 %custom-call.30 = f32[4,128,128]{1,2,0:T(8,128)S(1)} custom-call(f32[4,128,128]{2,1,0:T(8,128)S(1)} %get-tuple-element.85), custom_call_target="InvertDiagBlocksLowerTriangular" | custom-call | tf_op jit(solution)/shard_map/cond/branch_0_fun/jit(_solve_triangular)/triangular_solve | solution.py:442
  289.4 1.6 convolution_subtract_fusion.1
  291.6 2.3 convolution_subtract_fusion.2
  294.5 3.0 %convolution_subtract_fusion = f32[128,768]{0,1:T(8,128)S(1)} fusion(f32[128,768]{1,0:T(8,128)S(1)} %fusion.22, f32[128,768]{1,0:T(8,128)S(1)} %fusion.24, f32[128,768]{1,0:T(8,128)S(1)} %fusion.11, f32[512,768]{0,1:T(8,128)S(1)} %maximum_bitcast_fusion, f32[512,512]{1,0:T(8,128)} %get-tuple-element.198), kind=kOutput, calls=%fused_computation.5 | convolution fusion | flops 453672960 | bytes 2162688 | tf_op jit(solution)/shard_map/cond/branch_0_fun/jit(_solve_triangular)/triangular_solve | solution.py:442
  298.2 1.6 copy.16
  (80 shorter events, 22.4 us)
Async XLA Ops:
  9.9 2.7 collective-permute-start
  12.6 17.6 %slice-start = ((s8[6291456]{0:T(1024)(128)(4,1)}), s8[4194304]{0:T(1024)(128)(4,1)S(1)}, s32[]{:S(2)}) async-start(s8[6291456]{0:T(1024)(128)(4,1)} %bitcast.75), calls=%async_computation | async-start | bytes 8388608
  13.8 16.3 %slice-start.1 = ((s8[6291456]{0:T(1024)(128)(4,1)}), s8[2097152]{0:T(1024)(128)(4,1)S(1)}, s32[]{:S(2)}) async-start(s8[6291456]{0:T(1024)(128)(4,1)} %bitcast.75), calls=%async_computation.1 | async-start | bytes 4194304
  23.7 6.3 %copy-start.3 = (f32[2,128,512]{2,1,0:T(8,128)S(1)}, f32[2,128,512]{2,1,0:T(8,128)}, u32[]{:S(2)}) copy-start(f32[2,128,512]{2,1,0:T(8,128)} %get-tuple-element.51) | copy-start | bytes 1572868
  23.7 5.2 %collective-permute-start.1 = (f32[2,128,512]{2,1,0:T(8,128)}, f32[2,128,512]{2,1,0:T(8,128)S(1)}, u32[]{:S(2)}, u32[]{:S(2)}) collective-permute-start(f32[2,128,512]{2,1,0:T(8,128)} %get-tuple-element.50), channel_id=1, source_target_pairs={{0,1},{1,0},{2,3},{3,2},{4,5},{5,4},{6,7},{7,6},{8,9},{9,8},{10,11... | collective-permute-start | bytes 1572872 | tf_op jit(solution)/shard_map/ppermute | solution.py:251
  25.1 4.9 %collective-permute-start.2 = (f32[2,128,512]{2,1,0:T(8,128)}, f32[2,128,512]{2,1,0:T(8,128)S(1)}, u32[]{:S(2)}, u32[]{:S(2)}) collective-permute-start(f32[2,128,512]{2,1,0:T(8,128)} %get-tuple-element.52), channel_id=1, source_target_pairs={{0,1},{1,0},{2,3},{3,2},{4,5},{5,4},{6,7},{7,6},{8,9},{9,8},{10,11... | collective-permute-start | bytes 1572872 | tf_op jit(solution)/shard_map/ppermute | solution.py:251
  25.2 22.4 %collective-permute-start.6 = (f32[2,128,512]{2,1,0:T(8,128)S(1)}, f32[2,128,512]{2,1,0:T(8,128)S(1)}, u32[]{:S(2)}, u32[]{:S(2)}) collective-permute-start(f32[2,128,512]{2,1,0:T(8,128)S(1)} %add.92), channel_id=1, source_target_pairs={{0,2},{1,3},{2,0},{3,1},{4,6},{5,7},{6,4},{7,5},{8,10},{9,11},{10,... | collective-permute-start | bytes 1572872 | tf_op jit(solution)/shard_map/ppermute | solution.py:251
  28.9 1.3 copy-start.1
  30.2 4.4 %copy-start = (bf16[1,1,360,128,128]{4,3,2,1,0:T(8,128)(2,1)S(1)}, bf16[1,1,360,128,128]{4,3,2,1,0:T(8,128)(2,1)}, u32[]{:S(2)}) copy-start(bf16[1,1,360,128,128]{4,3,2,1,0:T(8,128)(2,1)} %param.6) | copy-start | bytes 35389444
  40.0 8.0 %collective-permute-start.5 = (f32[2,128,512]{2,1,0:T(8,128)S(1)}, f32[2,128,512]{2,1,0:T(8,128)S(1)}, u32[]{:S(2)}, u32[]{:S(2)}) collective-permute-start(f32[2,128,512]{2,1,0:T(8,128)S(1)} %get-tuple-element.58), channel_id=1, source_target_pairs={{0,1},{1,0},{2,3},{3,2},{4,5},{5,4},{6,7},{7,6},{8,9},{9,8},{10,11... | collective-permute-start | bytes 1572872 | tf_op jit(solution)/shard_map/ppermute | solution.py:251
  44.2 16.0 %collective-permute-start.8 = (f32[2,128,512]{2,1,0:T(8,128)S(1)}, f32[2,128,512]{2,1,0:T(8,128)S(1)}, u32[]{:S(2)}, u32[]{:S(2)}) collective-permute-start(f32[2,128,512]{2,1,0:T(8,128)S(1)} %add.93), channel_id=1, source_target_pairs={{0,2},{1,3},{2,0},{3,1},{4,6},{5,7},{6,4},{7,5},{8,10},{9,11},{10,... | collective-permute-start | bytes 1572872 | tf_op jit(solution)/shard_map/ppermute | solution.py:251
  47.4 12.7 %collective-permute-start.7 = (f32[2,128,512]{2,1,0:T(8,128)S(1)}, f32[2,128,512]{2,1,0:T(8,128)S(1)}, u32[]{:S(2)}, u32[]{:S(2)}) collective-permute-start(f32[2,128,512]{2,1,0:T(8,128)S(1)} %get-tuple-element.62), channel_id=1, source_target_pairs={{0,1},{1,0},{2,3},{3,2},{4,5},{5,4},{6,7},{7,6},{8,9},{9,8},{10,11... | collective-permute-start | bytes 1572872 | tf_op jit(solution)/shard_map/ppermute | solution.py:251
  47.4 23.4 %collective-permute-start.4 = (f32[2,128,512]{2,1,0:T(8,128)S(1)}, f32[2,128,512]{2,1,0:T(8,128)S(1)}, u32[]{:S(2)}, u32[]{:S(2)}) collective-permute-start(f32[2,128,512]{2,1,0:T(8,128)S(1)} %add.94), channel_id=1, source_target_pairs={{0,2},{1,3},{2,0},{3,1},{4,6},{5,7},{6,4},{7,5},{8,10},{9,11},{10,... | collective-permute-start | bytes 1572872 | tf_op jit(solution)/shard_map/ppermute | solution.py:251
  47.6 23.2 %collective-permute-start.3 = (f32[2,128,512]{2,1,0:T(8,128)S(1)}, f32[2,128,512]{2,1,0:T(8,128)S(1)}, u32[]{:S(2)}, u32[]{:S(2)}) collective-permute-start(f32[2,128,512]{2,1,0:T(8,128)S(1)} %get-tuple-element.55), channel_id=1, source_target_pairs={{0,1},{1,0},{2,3},{3,2},{4,5},{5,4},{6,7},{7,6},{8,9},{9,8},{10,11... | collective-permute-start | bytes 1572872 | tf_op jit(solution)/shard_map/ppermute | solution.py:251
  71.9 1.6 collective-permute-start.9
  73.6 5.9 %collective-permute-start.12 = (f32[160,128]{1,0:T(8,128)S(1)}, f32[160,128]{1,0:T(8,128)S(1)}, u32[]{:S(2)}, u32[]{:S(2)}) collective-permute-start(f32[160,128]{1,0:T(8,128)S(1)} %get-tuple-element.122), channel_id=1, source_target_pairs={{0,6},{1,7},{2,4},{3,5},{4,2},{5,3},{6,0},{7,1},{8,14},{9,15},{10,... | collective-permute-start | bytes 245768 | tf_op jit(solution)/shard_map/ppermute | solution.py:259
  73.7 6.3 %collective-permute-start.11 = (f32[160,128]{1,0:T(8,128)S(1)}, f32[160,128]{1,0:T(8,128)S(1)}, u32[]{:S(2)}, u32[]{:S(2)}) collective-permute-start(f32[160,128]{1,0:T(8,128)S(1)} %get-tuple-element.123), channel_id=1, source_target_pairs={{0,2},{1,3},{2,0},{3,1},{4,6},{5,7},{6,4},{7,5},{8,10},{9,11},{10,... | collective-permute-start | bytes 245768 | tf_op jit(solution)/shard_map/ppermute | solution.py:251
  75.5 5.6 %collective-permute-start.10 = (f32[160,128]{1,0:T(8,128)S(1)}, f32[160,128]{1,0:T(8,128)S(1)}, u32[]{:S(2)}, u32[]{:S(2)}) collective-permute-start(f32[160,128]{1,0:T(8,128)S(1)} %get-tuple-element.124), channel_id=1, source_target_pairs={{0,4},{4,0},{8,12},{12,8},{16,20},{20,16},{24,28},{28,24},{1,5},{5... | collective-permute-start | bytes 245768 | tf_op jit(solution)/shard_map/ppermute | solution.py:253
  81.1 7.9 %collective-permute-start.15 = (f32[160,128]{1,0:T(8,128)S(1)}, f32[160,128]{1,0:T(8,128)S(1)}, u32[]{:S(2)}, u32[]{:S(2)}) collective-permute-start(f32[160,128]{1,0:T(8,128)S(1)} %fusion.37), channel_id=1, source_target_pairs={{0,24},{4,28},{8,16},{12,20},{16,8},{20,12},{24,0},{28,4},{1,25},{... | collective-permute-start | bytes 245768 | tf_op jit(solution)/shard_map/ppermute | solution.py:253
  86.0 6.3 %collective-permute-start.14 = (f32[160,128]{1,0:T(8,128)S(1)}, f32[160,128]{1,0:T(8,128)S(1)}, u32[]{:S(2)}, u32[]{:S(2)}) collective-permute-start(f32[160,128]{1,0:T(8,128)S(1)} %fusion.37), channel_id=1, source_target_pairs={{0,16},{4,20},{8,24},{12,28},{16,0},{20,4},{24,8},{28,12},{1,17},{... | collective-permute-start | bytes 245768 | tf_op jit(solution)/shard_map/ppermute | solution.py:253
  86.0 6.3 %collective-permute-start.13 = (f32[160,128]{1,0:T(8,128)S(1)}, f32[160,128]{1,0:T(8,128)S(1)}, u32[]{:S(2)}, u32[]{:S(2)}) collective-permute-start(f32[160,128]{1,0:T(8,128)S(1)} %fusion.37), channel_id=1, source_target_pairs={{0,8},{4,12},{8,0},{12,4},{16,24},{20,28},{24,16},{28,20},{1,9},{5... | collective-permute-start | bytes 245768 | tf_op jit(solution)/shard_map/ppermute | solution.py:253
  92.4 6.2 %collective-permute-start.18 = (f32[160,128]{1,0:T(8,128)S(1)}, f32[160,128]{1,0:T(8,128)S(1)}, u32[]{:S(2)}, u32[]{:S(2)}) collective-permute-start(f32[160,128]{1,0:T(8,128)S(1)} %add_add_fusion.refs_0_), channel_id=1, source_target_pairs={{0,6},{1,7},{2,4},{3,5},{4,2},{5,3},{6,0},{7,1},{8,14},{9,15},{10,... | collective-permute-start | bytes 245768 | tf_op jit(solution)/shard_map/ppermute | solution.py:259
  93.9 5.0 %collective-permute-start.17 = (f32[160,128]{1,0:T(8,128)S(1)}, f32[160,128]{1,0:T(8,128)S(1)}, u32[]{:S(2)}, u32[]{:S(2)}) collective-permute-start(f32[160,128]{1,0:T(8,128)S(1)} %add_add_fusion.refs_0_), channel_id=1, source_target_pairs={{0,2},{1,3},{2,0},{3,1},{4,6},{5,7},{6,4},{7,5},{8,10},{9,11},{10,... | collective-permute-start | bytes 245768 | tf_op jit(solution)/shard_map/ppermute | solution.py:251
  95.0 4.4 %collective-permute-start.16 = (f32[160,128]{1,0:T(8,128)S(1)}, f32[160,128]{1,0:T(8,128)S(1)}, u32[]{:S(2)}, u32[]{:S(2)}) collective-permute-start(f32[160,128]{1,0:T(8,128)S(1)} %add_add_fusion.refs_0_), channel_id=1, source_target_pairs={{0,4},{4,0},{8,12},{12,8},{16,20},{20,16},{24,28},{28,24},{1,5},{5... | collective-permute-start | bytes 245768 | tf_op jit(solution)/shard_map/ppermute | solution.py:253
  95.9 3.5 %collective-permute-start.19 = (f32[160,128]{1,0:T(8,128)S(1)}, f32[160,128]{1,0:T(8,128)S(1)}, u32[]{:S(2)}, u32[]{:S(2)}) collective-permute-start(f32[160,128]{1,0:T(8,128)S(1)} %add_add_fusion.refs_0_), channel_id=1, source_target_pairs={{0,1},{1,0},{2,3},{3,2},{4,5},{5,4},{6,7},{7,6},{8,9},{9,8},{10,11... | collective-permute-start | bytes 245768 | tf_op jit(solution)/shard_map/ppermute | solution.py:251
  98.5 1.3 collective-permute-start.22
  98.9 1.3 collective-permute-start.21
  99.5 1.3 collective-permute-start.20
  145.8 1.0 copy-start.2
where the time goes:
time: 305 us; the launch traced here: 301 us
  other arithmetic  125 us (41%)
  Pallas kernels  66.6 us (22%)
  waiting for transfers between devices  38.8 us (13%)
  starting transfers between devices  26.9 us (9%)
  local copies, waits for them, and re-layouts  22.6 us (7%)
  matrix products  14.6 us (5%)
  loops' own time  3.37 us (1%)
  between operations  3.1 us (1%)
    another operation x14, other arithmetic, direct(): lower = jnp.linalg.cholesky(gram)  78.8 us
    pallas_call x1, Pallas kernels, factor(): pl.pallas_call(functools.partial(factor_kernel, len(rows), scale, 12), ou...  40 us
    another operation x2, other arithmetic, direct(): jax.scipy.linalg.solve_triangular(lower, own_rows.T, lower=True).T * scale  39.3 us
    ppermute x16, waiting for transfers between devices, swapped(): return lax.ppermute(x, 'col', [(c, c ^ col_flip) for c in range(cols)])  26.7 us
    pallas_call x3, Pallas kernels, tile_products(): pl.pallas_call(functools.partial(tile_kernel, resident, span, chunks, fli...  23.8 us
    ppermute x16, starting transfers between devices, swapped(): return lax.ppermute(x, 'col', [(c, c ^ col_flip) for c in range(cols)])  17.1 us
    another operation x13, local copies, waits for them, and re-layouts  12.9 us
    another operation x7, matrix products, direct(): jax.scipy.linalg.solve_triangular(lower, own_rows.T, lower=True).T * scale  9.1 us
  transfers between devices with their start and end apart: 23, of which 15 were waited for; matrix products, arithmetic and copies ran while one was open for 0% of the time, Pallas kernels for 2%

commit v1 on v0

--- a/solution.py
+++ b/solution.py
@@ -11,14 +11,13 @@
 BF16 = jnp.bfloat16
 F32 = jnp.float32
 PAIR = 2
-TURN = 8
-CHUNKS = 3
+TURN = 12
+PARTS = 2
 BLOCK = 128
 SMEM = pl.BlockSpec(memory_space=pltpu.SMEM)
 VMEM = pl.BlockSpec(memory_space=pltpu.VMEM)
 ANY = pl.BlockSpec(memory_space=pl.ANY)
 
-
 def params(size):
     return pltpu.CompilerParams(vmem_limit_bytes=size)
 
@@ -28,52 +27,63 @@
     return high, (x - high.astype(F32)).astype(BF16)
 
 
-def tile_kernel(resident, span, chunks, flip, stride, counts, places, tiles, panels, *refs):
-    outs = refs[: 2 * chunks]
-    refs = refs[2 * chunks :]
-    acc, tile_buf, panel_buf, key, fill, slot, column, first_of, key_of = refs[:9]
-    tile_sem, panel_sem, out_sem = refs[9:]
+def tile_kernel(resident, flip, stride, counts, places, tiles, panels, *refs):
+    outs, refs = refs[:-13], refs[-13:]
+    tile_buf, panel_buf, live_of, place_of, key, fill, slot, column, first_of, key_of = refs[:10]
+    acc, load_sem, panel_sem = refs[10:]
     slots = tiles.shape[0]
     blocks = acc.shape[0]
-    per_owner = key.shape[0] // lax.axis_size("col")
-    here = blocks // 2
-    bulk_copy = pltpu.make_async_copy(tiles, tile_buf.at[pl.ds(0, slots)], tile_sem.at[0])
-    bulk_copy.start()
-    if resident:
-        panel_copy = pltpu.make_async_copy(panels, panel_buf, panel_sem.at[0])
-        panel_copy.start()
-    live = counts[0, 0]
+    per_owner = blocks // 2
+    index_loads = [
+        pltpu.make_async_copy(counts, live_of, load_sem.at[0]),
+        pltpu.make_async_copy(places, place_of, load_sem.at[1]),
+    ]
+    panel_loads = [pltpu.make_async_copy(panels, panel_buf, panel_sem.at[0])] if resident else []
+    cuts = [slots * n // PARTS for n in range(PARTS + 1)]
+    tile_loads = [
+        pltpu.make_async_copy(
+            tiles.at[pl.ds(a, b - a)], tile_buf.at[pl.ds(a, b - a)], load_sem.at[2 + n]
+        )
+        for n, (a, b) in enumerate(zip(cuts, cuts[1:]))
+    ]
+    for load in index_loads + panel_loads + tile_loads:
+        load.start()
     own = lax.axis_index("col")
 
     for owner in range(key.shape[0] // per_owner):
-        base = jnp.where((owner & 1) == (own & 1), here, 0)
+        base = jnp.where((owner & 1) == (own & 1), per_owner, 0)
         wanted = (owner >> 1) == ((own >> 1) ^ flip)
         for inside in range(per_owner):
-            name = jnp.where(wanted, base + inside - span[0], blocks)
-            key[owner * per_owner + inside] = name if span[0] <= inside < span[1] else blocks
-    for k in range(blocks + 1):
+            key[owner * per_owner + inside] = jnp.where(wanted, base + inside, blocks)
+    lists = PARTS * blocks
+    for k in range(lists + 1):
         fill[k] = k * stride
+    for load in index_loads:
+        load.wait()
+    live = live_of[0, 0]
 
     unroll = math.gcd(slots, 8)
 
     def put(g, carry):
         for i in range(unroll):
             t = g * unroll + i
-            k = jnp.where(t < live, key[places[0, t]], blocks)
+            part = sum(jnp.where(t >= cut, blocks, 0) for cut in cuts[1:-1])
+            row = key[place_of[0, t]]
+            k = jnp.where(jnp.logical_and(t < live, row < blocks), part + row, lists)
             p = fill[k]
             fill[k] = p + 1
             slot[p] = t
-            column[p] = places[1, t]
+            column[p] = place_of[1, t]
         return carry
 
     lax.fori_loop(0, (live + unroll - 1) // unroll, put, 0)
 
-    empty = blocks * stride + slots
+    empty = lists * stride + slots
     for i in range(PAIR):
         slot[empty + i] = slots
         column[empty + i] = 0
     number, bounds = 0, [0]
-    for k in range(blocks):
+    for k in range(lists):
         size = fill[k] - k * stride
         for i in range(PAIR - 1):
             slot[fill[k] + i] = slots
@@ -81,23 +91,22 @@
 
         def add_pair(j, at, k=k):
             first_of[at + j] = k * stride + j * PAIR
-            key_of[at + j] = k
+            key_of[at + j] = k % blocks
             return at
 
         pairs = (size + PAIR - 1) // PAIR
         lax.fori_loop(0, pairs, add_pair, number)
         number += pairs
-        if (k + 1) % here == 0:
+        if (k + 1) % blocks == 0:
             for i in range(TURN - 1):
                 first_of[number + i] = empty
-                key_of[number + i] = k
+                key_of[number + i] = 0
             number = (number + TURN - 1) // TURN * TURN
             bounds.append(number // TURN)
     acc[...] = jnp.zeros_like(acc)
     tile_buf[slots] = jnp.zeros_like(tile_buf[slots])
-    bulk_copy.wait()
-    if resident:
-        panel_copy.wait()
+    for load in panel_loads:
+        load.wait()
 
     def turn(g, carry):
         firsts = [first_of[g * TURN + i] for i in range(TURN)]
@@ -127,54 +136,46 @@
             acc[key_of[g * TURN + i]] += jnp.dot(left, right, preferred_element_type=F32)
         return carry
 
-    size = here // chunks
-    copies = []
-    for half in range(2):
-        lax.fori_loop(bounds[half], bounds[half + 1], turn, 0)
-        for n in range(half * chunks, (half + 1) * chunks):
-            copy = pltpu.make_async_copy(acc.at[pl.ds(n * size, size)], outs[n], out_sem.at[n])
-            copy.start()
-            copies.append(copy)
-    for copy in copies:
-        copy.wait()
-
-
-def tile_products(counts, places, tiles, panels, tile_rows, span, chunks, flip, limit):
+    for n, load in enumerate(tile_loads):
+        load.wait()
+        lax.fori_loop(bounds[n], bounds[n + 1], turn, 0)
+    first = 0
+    for out in outs:
+        out[...] = acc[first : first + out.shape[0]]
+        first += out.shape[0]
+
+
+def tile_products(counts, places, tiles, panels, tile_rows, sizes, flip):
     slots, size, _ = tiles.shape
     width = panels.shape[2]
-    blocks = (span[1] - span[0]) * 2
+    blocks = 2 * sum(sizes)
     stride = (min(slots, panels.shape[0]) // PAIR + 1) * PAIR
-    entries = blocks * stride + slots + PAIR
-    pairs = blocks * stride // PAIR + 2 * TURN
+    lists = PARTS * blocks
+    entries = lists * stride + slots + PAIR
+    pairs = lists * stride // PAIR + TURN * (PARTS + 1)
     resident = panels.size * 2 <= 16 << 20
     panel_shape = (panels.shape[0] if resident else PAIR * TURN, size, width)
-    used = blocks * size * width * 4 + (slots + 1) * size * size * 2 + math.prod(panel_shape) * 2
-    piece = jax.ShapeDtypeStruct((blocks // 2 // chunks, size, width), F32)
     return pl.pallas_call(
-        functools.partial(tile_kernel, resident, span, chunks, flip, stride),
-        out_shape=[piece] * (2 * chunks),
-        in_specs=[SMEM, SMEM, ANY, ANY],
-        out_specs=[ANY] * (2 * chunks),
+        functools.partial(tile_kernel, resident, flip, stride),
+        out_shape=[jax.ShapeDtypeStruct((n, size, width), F32) for n in (*sizes, *sizes)],
+        in_specs=[ANY] * 4,
+        out_specs=[VMEM] * (2 * len(sizes)),
         scratch_shapes=[
-            pltpu.VMEM((blocks, size, width), F32),
             pltpu.VMEM((slots + 1, size, size), BF16),
             pltpu.VMEM(panel_shape, BF16),
+            pltpu.SMEM((1, 1), jnp.int32),
+            pltpu.SMEM((2, slots), jnp.int32),
             pltpu.SMEM((tile_rows,), jnp.int32),
-            pltpu.SMEM((blocks + 1,), jnp.int32),
+            pltpu.SMEM((lists + 1,), jnp.int32),
             pltpu.SMEM((entries,), jnp.int32),
             pltpu.SMEM((entries,), jnp.int32),
             pltpu.SMEM((pairs,), jnp.int32),
             pltpu.SMEM((pairs,), jnp.int32),
-            pltpu.SemaphoreType.DMA((1,)),
+            pltpu.VMEM((blocks, size, width), F32),
+            pltpu.SemaphoreType.DMA((2 + PARTS,)),
             pltpu.SemaphoreType.DMA((1 if resident else PAIR * TURN,)),
-            pltpu.SemaphoreType.DMA((2 * chunks,)),
         ],
-        compiler_params=params(max(limit, used + (6 << 20))),
-        cost_estimate=pl.CostEstimate(
-            flops=slots * size * size * width,
-            bytes_accessed=tiles.size + panels.size * 2,
-            transcendentals=0,
-        ),
+        compiler_params=params(50 << 20),
     )(counts, places, tiles, panels)
 
 
@@ -239,9 +240,6 @@
         out_specs=[VMEM] * len(outs),
         scratch_shapes=[pltpu.VMEM(whole.shape, F32)] if last else [],
         compiler_params=params(16 << 20),
-        cost_estimate=pl.CostEstimate(
-            flops=4 * rows * width * width, bytes_accessed=rows * width * 16, transcendentals=0
-        ),
     )(*args)
 
 
@@ -455,26 +453,21 @@
     places = tile_places[0, 0]
     scale = math.sqrt(local_rows * row_devices * col_devices)
     per_owner = tile_rows // col_devices
-    chunks = math.gcd(CHUNKS, per_owner)
-
-    def products(first, last, flip, limit):
-        span = (first * per_owner // chunks, last * per_owner // chunks)
-        out = tile_products(
-            tile_counts, places, tiles, panels, tile_rows, span, last - first, flip, limit
-        )
-        return out[: last - first], out[last - first :]
-
-    across = []
-    for first, last in ((0, 1), (1, chunks))[: min(2, chunks)]:
-        send, keep = products(first, last, 1, 56 << 20)
-        own = [k + swapped(x, 0, 1) for k, x in zip(keep, send)]
-        places, *own = lax.optimization_barrier((places, *own))
-        across += [swapped(x, 0, 2) for x in own]
-    send, keep = products(0, chunks, 0, 0)
+    first = max(1, per_owner // 3)
+    sizes = (first, per_owner - first) if per_owner > first else (first,)
+    chunks = len(sizes)
+
+    def products(flip):
+        out = tile_products(tile_counts, places, tiles, panels, tile_rows, sizes, flip)
+        return out[:chunks], out[chunks:]
+
+    send, keep = products(1)
+    across = [swapped(k + swapped(x, 0, 1), 0, 2) for k, x in zip(keep, send)]
+    send, keep = products(0)
+    send, keep, across[0] = lax.optimization_barrier((send, keep, across[0]))
     rows, grams = [], []
     for n in range(chunks):
-        last = n == chunks - 1
-        out = gram_chunk(keep[n], swapped(send[n], 0, 1), across[n], grams, last)
+        out = gram_chunk(keep[n], swapped(send[n], 0, 1), across[n], grams, n == chunks - 1)
         rows.append(out[0])
         grams.append(out[1])
     mine, theirs = gram_sum(*out[1:])

time: 305 us -> 287 us (0.941)
  starting transfers between devices: 26.9 us -> 13.8 us
  Pallas kernels: 66.6 us -> 58.9 us
  waiting for transfers between devices: 38.8 us -> 45.7 us
    ppermute x16 -> x13, starting transfers between devices: 17.1 us -> 4.86 us  [swapped(): return lax.ppermute(x, 'col', [(c, c ^ col_flip) for c in range(cols)])]
    ppermute x16 -> x13, waiting for transfers between devices: 26.7 us -> 33.5 us  [swapped(): return lax.ppermute(x, 'col', [(c, c ^ col_flip) for c in range(cols)])]
    pallas_call x3 -> x2, Pallas kernels: 23.8 us -> 18.1 us  [tile_products(): pl.pallas_call(functools.partial(tile_kernel, resident, flip, stride), ou...]
    unnamed x10 -> x2, local copies, waits for them, and re-layouts: 4.37 us -> 0.68 us
  transfers between devices with their start and end apart: 23 -> 20, of which waited for: 15 -> 16; matrix products, arithmetic and copies ran while one was open for 0% -> 0% of each run, Pallas kernels for 2% -> 3%
where the time goes in v1:
time: 287 us; the launch traced here: 282 us
  other arithmetic  122 us (43%)
  Pallas kernels  58.9 us (21%)
  waiting for transfers between devices  45.7 us (16%)
  local copies, waits for them, and re-layouts  20.4 us (7%)
  matrix products  14.5 us (5%)
  starting transfers between devices  13.8 us (5%)
  loops' own time  3.52 us (1%)
  between operations  3.12 us (1%)
    another operation x14, other arithmetic, direct(): lower = jnp.linalg.cholesky(gram)  78.8 us
    another operation x2, other arithmetic, direct(): jax.scipy.linalg.solve_triangular(lower, own_rows.T, lower=True).T * scale  39.3 us
    pallas_call x1, Pallas kernels, factor(): pl.pallas_call(functools.partial(factor_kernel, len(rows), scale, 12), ou...  39.1 us
    ppermute x13, waiting for transfers between devices, swapped(): return lax.ppermute(x, 'col', [(c, c ^ col_flip) for c in range(cols)])  33.5 us
    pallas_call x2, Pallas kernels, tile_products(): pl.pallas_call(functools.partial(tile_kernel, resident, flip, stride), ou...  18.1 us
    another operation x13, local copies, waits for them, and re-layouts  14.5 us
    another operation x7, matrix products, direct(): jax.scipy.linalg.solve_triangular(lower, own_rows.T, lower=True).T * scale  9.05 us
    ppermute x5, waiting for transfers between devices, swapped(): return lax.ppermute(x, 'row', [(r, r ^ row_flip) for r in range(rows)])  7.65 us
  transfers between devices with their start and end apart: 20, of which 16 were waited for; matrix products, arithmetic and copies ran while one was open for 0% of the time, Pallas kernels for 3%

profile of v1, /device:TPU:0, one launch (start us, length us, event | category | flops | bytes accessed | tf_op | source)
XLA Modules:
  0.0 281.8 jit_solution(10147224505268977600)
XLA Ops:
  2.0 9.5 %shard_map.64 = (f32[2,128,512]{2,1,0:T(8,128)S(1)}, f32[4,128,512]{2,1,0:T(8,128)S(1)}, f32[2,128,512]{2,1,0:T(8,128)S(1)}, f32[4,128,512]{2,1,0:T(8,128)S(1)}) custom-call(s32[1,1]{1,0:T(1,128)S(6)} %copy.38.counts, s32[2,360]{1,0:T(2,128)S(1)} %bitcast.70, bf16[360,128,128]{2,1,0:T(8,128)(2,1)} %bitcast.72, bf16[48,128,512]{2,1,0:T(8,128)(2,1)} %bitcast.74), custom_call_target="tpu_custom_call" | custom-call | tf_op jit(solution)/shard_map/pallas_call | solution.py:158
  12.1 2.9 %collective-permute-done = f32[2,128,512]{2,1,0:T(8,128)S(1)} collective-permute-done((f32[2,128,512]{2,1,0:T(8,128)S(1)}, f32[2,128,512]{2,1,0:T(8,128)S(1)}, u32[]{:S(2)}, u32[]{:S(2)}) %collective-permute-start) | collective-permute-done | bytes 524320 | tf_op jit(solution)/shard_map/ppermute | solution.py:249
  15.8 8.5 %shard_map.63 = (f32[2,128,512]{2,1,0:T(8,128)S(1)}, f32[4,128,512]{2,1,0:T(8,128)S(1)}, f32[2,128,512]{2,1,0:T(8,128)S(1)}, f32[4,128,512]{2,1,0:T(8,128)S(1)}) custom-call(s32[1,1]{1,0:T(1,128)S(6)} %copy.38.counts, s32[2,360]{1,0:T(2,128)S(1)} %bitcast.71, bf16[360,128,128]{2,1,0:T(8,128)(2,1)} %bitcast.73, bf16[48,128,512]{2,1,0:T(8,128)(2,1)} %bitcast.75), custom_call_target="tpu_custom_call" | custom-call | tf_op jit(solution)/shard_map/pallas_call | solution.py:158
  24.6 5.3 %collective-permute-done.1.refs_2_ = f32[2,128,512]{2,1,0:T(8,128)S(1)} collective-permute-done((f32[2,128,512]{2,1,0:T(8,128)S(1)}, f32[2,128,512]{2,1,0:T(8,128)S(1)}, u32[]{:S(2)}, u32[]{:S(2)}) %collective-permute-start.1) | collective-permute-done | bytes 524320 | tf_op jit(solution)/shard_map/ppermute | solution.py:249
  30.4 2.9 %collective-permute-done.5.refs_1_ = f32[2,128,512]{2,1,0:T(8,128)S(1)} collective-permute-done((f32[2,128,512]{2,1,0:T(8,128)S(1)}, f32[2,128,512]{2,1,0:T(8,128)S(1)}, u32[]{:S(2)}, u32[]{:S(2)}) %collective-permute-start.5) | collective-permute-done | bytes 524320 | tf_op jit(solution)/shard_map/ppermute | solution.py:249
  33.9 17.6 %collective-permute-done.4.refs_2_ = f32[4,128,512]{2,1,0:T(8,128)S(1)} collective-permute-done((f32[4,128,512]{2,1,0:T(8,128)S(1)}, f32[4,128,512]{2,1,0:T(8,128)S(1)}, u32[]{:S(2)}, u32[]{:S(2)}) %collective-permute-start.4) | collective-permute-done | bytes 1048608 | tf_op jit(solution)/shard_map/ppermute | solution.py:249
  51.6 1.0 shard_map.66
  52.7 1.6 collective-permute-done.6
  54.3 1.6 collective-permute-start.9
  55.9 1.7 collective-permute-start.8
  57.9 2.2 collective-permute-done.9
  60.1 1.5 collective-permute-done.8
  62.1 4.0 %collective-permute-start.12 = (f32[160,128]{1,0:T(8,128)S(1)}, f32[160,128]{1,0:T(8,128)S(1)}, u32[]{:S(2)}, u32[]{:S(2)}) collective-permute-start(f32[160,128]{1,0:T(8,128)S(1)} %fusion.37), channel_id=1, source_target_pairs={{0,24},{4,28},{8,16},{12,20},{16,8},{20,12},{24,0},{28,4},{1,25},{... | collective-permute-start | bytes 245768 | tf_op jit(solution)/shard_map/ppermute | solution.py:251
  66.8 2.2 collective-permute-done.12
  69.0 4.5 %collective-permute-done.11 = f32[160,128]{1,0:T(8,128)S(1)} collective-permute-done((f32[160,128]{1,0:T(8,128)S(1)}, f32[160,128]{1,0:T(8,128)S(1)}, u32[]{:S(2)}, u32[]{:S(2)}) %collective-permute-start.11) | collective-permute-done | bytes 81952 | tf_op jit(solution)/shard_map/ppermute | solution.py:251
  73.5 1.3 collective-permute-start.15
  74.8 1.2 collective-permute-start.14
  76.0 1.1 collective-permute-start.13
  77.0 2.4 collective-permute-done.15.refs_3_
  81.7 39.1 %shard_map.67 = (f32[768,512]{1,0:T(8,128)}, f32[512,512]{1,0:T(8,128)}, f32[512,512]{1,0:T(8,128)}, s32[1]{0:T(128)}) custom-call(f32[160,128]{1,0:T(8,128)S(1)} %add_add_fusion.refs_0_, f32[160,128]{1,0:T(8,128)S(1)} %collective-permute-done.13.refs_1_, f32[160,128]{1,0:T(8,128)S(1)} %collective-permute-done.14.refs_2_, ...), custom_call_target="tpu_custom_call" | custom-call | tf_op jit(solution)/shard_map/pallas_call | solution.py:417
  121.5 159.2 %conditional.1 = ((f32[768,512]{1,0:T(8,128)}, f32[512,512]{1,0:T(8,128)})) conditional(s32[]{:T(128)} %bitcast.21, (f32[512,512]{1,0:T(8,128)}, f32[256,512]{1,0:T(8,128)S(1)}, f32[512,512]{1,0:T(8,128)S(1)}) %tuple.16, (f32[768,512]{1,0:T(8,128)}, f32[512,512]{1,0:T(8,128)}) %tuple.17), branch_computations={%region_0.9_spmd, %region_9.10_spmd} | conditional | flops 1917878784 | bytes 41947460 | solution.py:475
  122.0 2.6 copy.11
  124.7 1.4 fusion.6
  126.1 1.0 copy-done.2
  127.1 11.7 %cholesky.5 = f32[128,128]{1,0:T(8,128)S(1)} custom-call(f32[128,128]{1,0:T(8,128)S(1)} %cholesky.100), custom_call_target="Cholesky" | custom-call | tf_op jit(solution)/shard_map/cond/branch_0_fun/jit(cholesky)/cholesky | solution.py:438
  138.9 9.8 %custom-call.27 = f32[1,128,128]{1,2,0:T(8,128)S(1)} custom-call(f32[1,128,128]{2,1,0:T(8,128)S(1)} %get-tuple-element.101), custom_call_target="InvertDiagBlocksLowerTriangular" | custom-call | tf_op jit(solution)/shard_map/cond/branch_0_fun/jit(cholesky)/cholesky | solution.py:438
  148.8 1.2 constant_dynamic-update-slice_fusion.3
  150.1 1.3 convolution_subtract_fusion.3
  151.3 11.7 %cholesky.29 = f32[128,128]{1,0:T(8,128)S(1)} custom-call(f32[128,128]{1,0:T(8,128)S(1)} %cholesky.104), custom_call_target="Cholesky" | custom-call | tf_op jit(solution)/shard_map/cond/branch_0_fun/jit(cholesky)/cholesky | solution.py:438
  163.1 0.7 compare_reduce_fusion.2
  165.1 10.0 %custom-call.28 = f32[1,128,128]{1,2,0:T(8,128)S(1)} custom-call(f32[1,128,128]{2,1,0:T(8,128)S(1)} %get-tuple-element.98), custom_call_target="InvertDiagBlocksLowerTriangular" | custom-call | tf_op jit(solution)/shard_map/cond/branch_0_fun/jit(cholesky)/cholesky | solution.py:438
  175.4 1.3 convolution_subtract_fusion.4
  176.7 11.7 %cholesky.62 = f32[128,128]{1,0:T(8,128)S(1)} custom-call(f32[128,128]{1,0:T(8,128)S(1)} %cholesky.111), custom_call_target="Cholesky" | custom-call | tf_op jit(solution)/shard_map/cond/branch_0_fun/jit(cholesky)/cholesky | solution.py:438
  189.7 9.8 %custom-call.29 = f32[1,128,128]{1,2,0:T(8,128)S(1)} custom-call(f32[1,128,128]{2,1,0:T(8,128)S(1)} %get-tuple-element.95), custom_call_target="InvertDiagBlocksLowerTriangular" | custom-call | tf_op jit(solution)/shard_map/cond/branch_0_fun/jit(cholesky)/cholesky | solution.py:438
  199.7 1.2 convolution_subtract_fusion.5
  200.9 11.7 %cholesky.89 = f32[128,128]{1,0:T(8,128)S(1)} custom-call(f32[128,128]{1,0:T(8,128)S(1)} %convolution_subtract_fusion.5), custom_call_target="Cholesky" | custom-call | tf_op jit(solution)/shard_map/cond/branch_0_fun/jit(cholesky)/cholesky | solution.py:438
  214.2 1.6 multiply_bitcast_fusion
  215.8 2.5 copy.18
  218.3 11.9 %while.1 = (s32[]{:T(128)}, f32[512,512]{1,0:T(8,128)}, s32[4,2]{0,1:T(2,128)S(1)}, f32[4,128,128]{2,1,0:T(8,128)S(1)}, s32[]{:T(128)}) while((s32[]{:T(128)}, f32[512,512]{1,0:T(8,128)}, s32[4,2]{0,1:T(2,128)S(1)}, f32[4,128,128]{2,1,0:T(8,128)S(1)}, s32[]{:T(128)}) %tuple.54), condition=%wide.while_cond, body=%wide.while_body.sunk | while | flops 2 | bytes 131189 | solution.py:440
  219.0 2.3 bitcast_dynamic-update-slice_fusion.2
  222.0 2.3 bitcast_dynamic-update-slice_fusion.2
  225.0 2.3 bitcast_dynamic-update-slice_fusion.2
  228.0 2.2 bitcast_dynamic-update-slice_fusion.2
  230.2 39.3 %custom-call.30 = f32[4,128,128]{1,2,0:T(8,128)S(1)} custom-call(f32[4,128,128]{2,1,0:T(8,128)S(1)} %get-tuple-element.70), custom_call_target="InvertDiagBlocksLowerTriangular" | custom-call | tf_op jit(solution)/shard_map/cond/branch_0_fun/jit(_solve_triangular)/triangular_solve | solution.py:440
  270.1 1.6 convolution_subtract_fusion.1
  272.3 2.3 convolution_subtract_fusion.2
  275.1 3.0 %convolution_subtract_fusion = f32[128,768]{0,1:T(8,128)S(1)} fusion(f32[128,768]{1,0:T(8,128)S(1)} %fusion.22, f32[128,768]{1,0:T(8,128)S(1)} %fusion.24, f32[128,768]{1,0:T(8,128)S(1)} %fusion.11, f32[512,768]{0,1:T(8,128)S(1)} %maximum_bitcast_fusion, f32[512,512]{1,0:T(8,128)} %get-tuple-element.181), kind=kOutput, calls=%fused_computation.5 | convolution fusion | flops 453672960 | bytes 2162688 | tf_op jit(solution)/shard_map/cond/branch_0_fun/jit(_solve_triangular)/triangular_solve | solution.py:440
  278.8 1.6 copy.16
  (64 shorter events, 14.6 us)
Async XLA Ops:
  1.3 0.7 copy-start
  11.5 12.8 %collective-permute-start.3 = (f32[4,128,512]{2,1,0:T(8,128)S(1)}, f32[4,128,512]{2,1,0:T(8,128)S(1)}, u32[]{:S(2)}, u32[]{:S(2)}) collective-permute-start(f32[4,128,512]{2,1,0:T(8,128)S(1)} %get-tuple-element.46), channel_id=1, source_target_pairs={{0,1},{1,0},{2,3},{3,2},{4,5},{5,4},{6,7},{7,6},{8,9},{9,8},{10,11... | collective-permute-start | bytes 3145736 | tf_op jit(solution)/shard_map/ppermute | solution.py:249
  11.6 3.4 %collective-permute-start = (f32[2,128,512]{2,1,0:T(8,128)S(1)}, f32[2,128,512]{2,1,0:T(8,128)S(1)}, u32[]{:S(2)}, u32[]{:S(2)}) collective-permute-start(f32[2,128,512]{2,1,0:T(8,128)S(1)} %get-tuple-element.42), channel_id=1, source_target_pairs={{0,1},{1,0},{2,3},{3,2},{4,5},{5,4},{6,7},{7,6},{8,9},{9,8},{10,11... | collective-permute-start | bytes 1572872 | tf_op jit(solution)/shard_map/ppermute | solution.py:249
  15.1 14.8 %collective-permute-start.1 = (f32[2,128,512]{2,1,0:T(8,128)S(1)}, f32[2,128,512]{2,1,0:T(8,128)S(1)}, u32[]{:S(2)}, u32[]{:S(2)}) collective-permute-start(f32[2,128,512]{2,1,0:T(8,128)S(1)} %add.89), channel_id=1, source_target_pairs={{0,2},{1,3},{2,0},{3,1},{4,6},{5,7},{6,4},{7,5},{8,10},{9,11},{10,... | collective-permute-start | bytes 1572872 | tf_op jit(solution)/shard_map/ppermute | solution.py:249
  24.5 27.0 %collective-permute-start.4 = (f32[4,128,512]{2,1,0:T(8,128)S(1)}, f32[4,128,512]{2,1,0:T(8,128)S(1)}, u32[]{:S(2)}, u32[]{:S(2)}) collective-permute-start(f32[4,128,512]{2,1,0:T(8,128)S(1)} %add.90), channel_id=1, source_target_pairs={{0,2},{1,3},{2,0},{3,1},{4,6},{5,7},{6,4},{7,5},{8,10},{9,11},{10,... | collective-permute-start | bytes 3145736 | tf_op jit(solution)/shard_map/ppermute | solution.py:249
  29.9 21.7 %collective-permute-start.2 = (f32[4,128,512]{2,1,0:T(8,128)S(1)}, f32[4,128,512]{2,1,0:T(8,128)S(1)}, u32[]{:S(2)}, u32[]{:S(2)}) collective-permute-start(f32[4,128,512]{2,1,0:T(8,128)S(1)} %get-tuple-element.44), channel_id=1, source_target_pairs={{0,1},{1,0},{2,3},{3,2},{4,5},{5,4},{6,7},{7,6},{8,9},{9,8},{10,11... | collective-permute-start | bytes 3145736 | tf_op jit(solution)/shard_map/ppermute | solution.py:249
  29.9 3.4 %collective-permute-start.5 = (f32[2,128,512]{2,1,0:T(8,128)S(1)}, f32[2,128,512]{2,1,0:T(8,128)S(1)}, u32[]{:S(2)}, u32[]{:S(2)}) collective-permute-start(f32[2,128,512]{2,1,0:T(8,128)S(1)} %get-tuple-element.48), channel_id=1, source_target_pairs={{0,1},{1,0},{2,3},{3,2},{4,5},{5,4},{6,7},{7,6},{8,9},{9,8},{10,11... | collective-permute-start | bytes 1572872 | tf_op jit(solution)/shard_map/ppermute | solution.py:249
  52.6 1.7 collective-permute-start.6
  54.3 5.7 %collective-permute-start.9 = (f32[160,128]{1,0:T(8,128)S(1)}, f32[160,128]{1,0:T(8,128)S(1)}, u32[]{:S(2)}, u32[]{:S(2)}) collective-permute-start(f32[160,128]{1,0:T(8,128)S(1)} %get-tuple-element.106), channel_id=1, source_target_pairs={{0,6},{1,7},{2,4},{3,5},{4,2},{5,3},{6,0},{7,1},{8,14},{9,15},{10,... | collective-permute-start | bytes 245768 | tf_op jit(solution)/shard_map/ppermute | solution.py:257
  55.9 5.6 %collective-permute-start.8 = (f32[160,128]{1,0:T(8,128)S(1)}, f32[160,128]{1,0:T(8,128)S(1)}, u32[]{:S(2)}, u32[]{:S(2)}) collective-permute-start(f32[160,128]{1,0:T(8,128)S(1)} %get-tuple-element.107), channel_id=1, source_target_pairs={{0,2},{1,3},{2,0},{3,1},{4,6},{5,7},{6,4},{7,5},{8,10},{9,11},{10,... | collective-permute-start | bytes 245768 | tf_op jit(solution)/shard_map/ppermute | solution.py:249
  57.6 4.4 %collective-permute-start.7 = (f32[160,128]{1,0:T(8,128)S(1)}, f32[160,128]{1,0:T(8,128)S(1)}, u32[]{:S(2)}, u32[]{:S(2)}) collective-permute-start(f32[160,128]{1,0:T(8,128)S(1)} %get-tuple-element.108), channel_id=1, source_target_pairs={{0,4},{4,0},{8,12},{12,8},{16,20},{20,16},{24,28},{28,24},{1,5},{5... | collective-permute-start | bytes 245768 | tf_op jit(solution)/shard_map/ppermute | solution.py:251
  62.1 6.9 %collective-permute-start.12 = (f32[160,128]{1,0:T(8,128)S(1)}, f32[160,128]{1,0:T(8,128)S(1)}, u32[]{:S(2)}, u32[]{:S(2)}) collective-permute-start(f32[160,128]{1,0:T(8,128)S(1)} %fusion.37), channel_id=1, source_target_pairs={{0,24},{4,28},{8,16},{12,20},{16,8},{20,12},{24,0},{28,4},{1,25},{... | collective-permute-start | bytes 245768 | tf_op jit(solution)/shard_map/ppermute | solution.py:251
  66.1 7.3 %collective-permute-start.11 = (f32[160,128]{1,0:T(8,128)S(1)}, f32[160,128]{1,0:T(8,128)S(1)}, u32[]{:S(2)}, u32[]{:S(2)}) collective-permute-start(f32[160,128]{1,0:T(8,128)S(1)} %fusion.37), channel_id=1, source_target_pairs={{0,16},{4,20},{8,24},{12,28},{16,0},{20,4},{24,8},{28,12},{1,17},{... | collective-permute-start | bytes 245768 | tf_op jit(solution)/shard_map/ppermute | solution.py:251
  66.7 6.7 %collective-permute-start.10 = (f32[160,128]{1,0:T(8,128)S(1)}, f32[160,128]{1,0:T(8,128)S(1)}, u32[]{:S(2)}, u32[]{:S(2)}) collective-permute-start(f32[160,128]{1,0:T(8,128)S(1)} %fusion.37), channel_id=1, source_target_pairs={{0,8},{4,12},{8,0},{12,4},{16,24},{20,28},{24,16},{28,20},{1,9},{5... | collective-permute-start | bytes 245768 | tf_op jit(solution)/shard_map/ppermute | solution.py:251
  73.5 5.9 %collective-permute-start.15 = (f32[160,128]{1,0:T(8,128)S(1)}, f32[160,128]{1,0:T(8,128)S(1)}, u32[]{:S(2)}, u32[]{:S(2)}) collective-permute-start(f32[160,128]{1,0:T(8,128)S(1)} %add_add_fusion.refs_0_), channel_id=1, source_target_pairs={{0,6},{1,7},{2,4},{3,5},{4,2},{5,3},{6,0},{7,1},{8,14},{9,15},{10,... | collective-permute-start | bytes 245768 | tf_op jit(solution)/shard_map/ppermute | solution.py:257
  74.8 5.2 %collective-permute-start.14 = (f32[160,128]{1,0:T(8,128)S(1)}, f32[160,128]{1,0:T(8,128)S(1)}, u32[]{:S(2)}, u32[]{:S(2)}) collective-permute-start(f32[160,128]{1,0:T(8,128)S(1)} %add_add_fusion.refs_0_), channel_id=1, source_target_pairs={{0,2},{1,3},{2,0},{3,1},{4,6},{5,7},{6,4},{7,5},{8,10},{9,11},{10,... | collective-permute-start | bytes 245768 | tf_op jit(solution)/shard_map/ppermute | solution.py:249
  76.0 4.4 %collective-permute-start.13 = (f32[160,128]{1,0:T(8,128)S(1)}, f32[160,128]{1,0:T(8,128)S(1)}, u32[]{:S(2)}, u32[]{:S(2)}) collective-permute-start(f32[160,128]{1,0:T(8,128)S(1)} %add_add_fusion.refs_0_), channel_id=1, source_target_pairs={{0,4},{4,0},{8,12},{12,8},{16,20},{20,16},{24,28},{28,24},{1,5},{5... | collective-permute-start | bytes 245768 | tf_op jit(solution)/shard_map/ppermute | solution.py:251
  77.0 3.4 %collective-permute-start.16 = (f32[160,128]{1,0:T(8,128)S(1)}, f32[160,128]{1,0:T(8,128)S(1)}, u32[]{:S(2)}, u32[]{:S(2)}) collective-permute-start(f32[160,128]{1,0:T(8,128)S(1)} %add_add_fusion.refs_0_), channel_id=1, source_target_pairs={{0,1},{1,0},{2,3},{3,2},{4,5},{5,4},{6,7},{7,6},{8,9},{9,8},{10,11... | collective-permute-start | bytes 245768 | tf_op jit(solution)/shard_map/ppermute | solution.py:249
  79.4 1.3 collective-permute-start.19
  80.0 1.3 collective-permute-start.18
  80.4 1.3 collective-permute-start.17
  122.0 2.7 copy-start.1
  126.1 1.0 copy-start.2

commit v2 on v1

--- a/solution.py
+++ b/solution.py
@@ -14,9 +14,14 @@
 TURN = 12
 PARTS = 2
 BLOCK = 128
+SMALL = 0.01
 SMEM = pl.BlockSpec(memory_space=pltpu.SMEM)
 VMEM = pl.BlockSpec(memory_space=pltpu.VMEM)
-ANY = pl.BlockSpec(memory_space=pl.ANY)
+HBM = pl.BlockSpec(memory_space=pltpu.HBM)
+
+def in_hbm(x):
+    return pltpu.with_memory_space_constraint(x, pltpu.HBM)
+
 
 def params(size):
     return pltpu.CompilerParams(vmem_limit_bytes=size)
@@ -28,25 +33,22 @@
 
 
 def tile_kernel(resident, flip, stride, counts, places, tiles, panels, *refs):
-    outs, refs = refs[:-13], refs[-13:]
-    tile_buf, panel_buf, live_of, place_of, key, fill, slot, column, first_of, key_of = refs[:10]
-    acc, load_sem, panel_sem = refs[10:]
+    outs, refs = refs[:-12], refs[-12:]
+    tile_buf, panel_buf, place_of, key, fill, slot, column, first_of, key_of = refs[:9]
+    acc, load_sem, panel_sem = refs[9:]
     slots = tiles.shape[0]
     blocks = acc.shape[0]
     per_owner = blocks // 2
-    index_loads = [
-        pltpu.make_async_copy(counts, live_of, load_sem.at[0]),
-        pltpu.make_async_copy(places, place_of, load_sem.at[1]),
-    ]
+    place_load = pltpu.make_async_copy(places, place_of, load_sem.at[0])
     panel_loads = [pltpu.make_async_copy(panels, panel_buf, panel_sem.at[0])] if resident else []
     cuts = [slots * n // PARTS for n in range(PARTS + 1)]
     tile_loads = [
         pltpu.make_async_copy(
-            tiles.at[pl.ds(a, b - a)], tile_buf.at[pl.ds(a, b - a)], load_sem.at[2 + n]
+            tiles.at[pl.ds(a, b - a)], tile_buf.at[pl.ds(a, b - a)], load_sem.at[1 + n]
         )
         for n, (a, b) in enumerate(zip(cuts, cuts[1:]))
     ]
-    for load in index_loads + panel_loads + tile_loads:
+    for load in [place_load] + panel_loads + tile_loads:
         load.start()
     own = lax.axis_index("col")
 
@@ -58,9 +60,8 @@
     lists = PARTS * blocks
     for k in range(lists + 1):
         fill[k] = k * stride
-    for load in index_loads:
-        load.wait()
-    live = live_of[0, 0]
+    place_load.wait()
+    live = counts[0, 0]
 
     unroll = math.gcd(slots, 8)
 
@@ -158,12 +159,11 @@
     return pl.pallas_call(
         functools.partial(tile_kernel, resident, flip, stride),
         out_shape=[jax.ShapeDtypeStruct((n, size, width), F32) for n in (*sizes, *sizes)],
-        in_specs=[ANY] * 4,
+        in_specs=[SMEM, HBM, HBM, HBM],
         out_specs=[VMEM] * (2 * len(sizes)),
         scratch_shapes=[
             pltpu.VMEM((slots + 1, size, size), BF16),
             pltpu.VMEM(panel_shape, BF16),
-            pltpu.SMEM((1, 1), jnp.int32),
             pltpu.SMEM((2, slots), jnp.int32),
             pltpu.SMEM((tile_rows,), jnp.int32),
             pltpu.SMEM((lists + 1,), jnp.int32),
@@ -172,11 +172,11 @@
             pltpu.SMEM((pairs,), jnp.int32),
             pltpu.SMEM((pairs,), jnp.int32),
             pltpu.VMEM((blocks, size, width), F32),
-            pltpu.SemaphoreType.DMA((2 + PARTS,)),
+            pltpu.SemaphoreType.DMA((1 + PARTS,)),
             pltpu.SemaphoreType.DMA((1 if resident else PAIR * TURN,)),
         ],
         compiler_params=params(50 << 20),
-    )(counts, places, tiles, panels)
+    )(counts, in_hbm(places), tiles, panels)
 
 
 def block_list(order):
@@ -303,8 +303,9 @@
 
 def factor_kernel(chunks, scale, rounds, *refs):
     pieces, rows = refs[:8], refs[8 : 8 + chunks]
-    basis, triangle, gram_out, flag = refs[8 + chunks : 12 + chunks]
-    blocks, gram, w, wh, wl, gh, gl, yh, yl, ph = refs[12 + chunks :]
+    basis_out, triangle_out, gram, flag = refs[8 + chunks : 12 + chunks]
+    blocks, half_mask, half_eye, w, basis, triangle, out_sem = refs[12 + chunks : 19 + chunks]
+    wb, gh, gl, yh, yl, ph, dh, dl = refs[19 + chunks :]
     size = gram.shape[0]
     order = size // BLOCK
     core_bit, me = place()
@@ -313,100 +314,127 @@
         at = (core_bit ^ (n // 4)) * half + (me ^ (n % 4)) * piece.shape[0]
         blocks[pl.ds(pl.multiple_of(at, 8), piece.shape[0])] = piece[...]
     at = [slice(i * BLOCK, (i + 1) * BLOCK) for i in range(order)]
+
+    r = lax.broadcasted_iota(jnp.int32, (BLOCK, BLOCK), 0)
+    c = lax.broadcasted_iota(jnp.int32, (BLOCK, BLOCK), 1)
+    row_scale, col_scale = [], []
+    for i in range(order):
+        n = i * (i + 1) // 2 + i
+        diagonal = jnp.where(r == c, blocks[n * BLOCK : (n + 1) * BLOCK], 0.0)
+        row_scale.append(lax.rsqrt(jnp.sum(diagonal, axis=1, keepdims=True)))
+        col_scale.append(lax.rsqrt(jnp.sum(diagonal, axis=0, keepdims=True)))
     for n, (i, j) in enumerate(block_list(order)):
         block = blocks[n * BLOCK : (n + 1) * BLOCK]
-        gram[at[i], at[j]] = block
+        first = -(block * row_scale[i] * col_scale[j])
+        if i == j:
+            first = jnp.where(r > c, first, jnp.where(r == c, 1.0, 0.0))
+        wb[at[i], at[j]] = (first * col_scale[j]).astype(BF16)
+        for p, q, x in [(i, j, block)] + ([(j, i, block.T)] if i != j else []):
+            gram[at[p], at[q]] = x
+            gh[at[p], at[q]], gl[at[p], at[q]] = halves(x)
         if i != j:
-            gram[at[j], at[i]] = block.T
-    high, low = halves(gram[...])
-    gh[...] = high
-    gl[...] = low
-    gram_out[...] = gram[...]
-
-    def index(i):
-        shape = (BLOCK, size)
-        return (
-            lax.broadcasted_iota(jnp.int32, shape, 0) + i * BLOCK,
-            lax.broadcasted_iota(jnp.int32, shape, 1),
-        )
-
-    def phi(error, i):
-        r, c = index(i)
-        r, c = r[:, : error.shape[1]], c[:, : error.shape[1]]
-        return jnp.where(r > c, error, jnp.where(r == c, 0.5 * error, 0.0))
-
-    row_scale, col_scale = [], []
-    for i in range(order):
-        block = gram[at[i], at[i]]
-        r, c = index(0)
-        diagonal = jnp.where(r[:, :BLOCK] == c[:, :BLOCK], block, 0.0)
-        row_scale.append(lax.rsqrt(jnp.sum(diagonal, axis=1, keepdims=True)))
-        col_scale.append(lax.rsqrt(jnp.sum(diagonal, axis=0, keepdims=True)))
-    col_scale = jnp.concatenate(col_scale, axis=1)
-    for i in range(order):
-        r, c = index(i)
-        same = jnp.where(r == c, 1.0, 0.0)
-        error = gram[at[i], :] * row_scale[i] * col_scale - same
-        w[at[i], :] = (same - phi(error, i)) * col_scale
-
-    def split_w():
-        for i in range(order):
-            high, low = halves(w[at[i], :])
-            wh[at[i], :] = high
-            wl[at[i], :] = low
+            wb[at[j], at[i]] = jnp.zeros((BLOCK, BLOCK), BF16)
+
+    wide = size // 2
+    top, low = slice(0, wide), slice(wide, size)
+    r = lax.broadcasted_iota(jnp.int32, (wide, wide), 0)
+    c = lax.broadcasted_iota(jnp.int32, (wide, wide), 1)
+    half_mask[...] = jnp.where(r > c, 1.0, jnp.where(r == c, 0.5, 0.0))
+    half_eye[...] = jnp.where(r == c, 0.5, 0.0)
+    for ref in (ph, dh, dl):
+        ref[top, low] = jnp.zeros((wide, wide), BF16)
+
+    def dot(left, right):
+        return jnp.dot(left, right, preferred_element_type=F32)
+
+    def dot_rows(left, right):
+        return lax.dot_general(left, right, (((1,), (1,)), ((), ())), preferred_element_type=F32)
+
+    def twice(x, axis=1):
+        return jnp.concatenate([x, x], axis=axis)
+
+    def both(x, y, axis=1):
+        return jnp.concatenate([x, y], axis=axis)
 
     def step(exact):
-        split_w()
-        for i in range(order):
+        for cols, k in ((top, wide), (low, size)):
+            y = dot_rows(both(gh[:, :k], gl[:, :k]), twice(wb[cols, :k]))
             if exact:
-                y = against((gh[at[i], :], gl[at[i], :]), (wh[...], wl[...]))
+                yh[:, cols], yl[:, cols] = halves(y)
             else:
-                y = lax.dot_general(
-                    gh[at[i], :], wh[...], (((1,), (1,)), ((), ())), preferred_element_type=F32
-                )
-            high, low = halves(y)
-            yh[at[i], :] = high
-            yl[at[i], :] = low
+                yh[:, cols] = y.astype(BF16)
         norm = jnp.zeros((1, 1), F32)
-        for i in range(order):
-            k = (i + 1) * BLOCK
+        strips = []
+        for part, k in ((top, wide), (low, size)):
             if exact:
-                m = times((wh[at[i], :k], wl[at[i], :k]), (yh[:k, :k], yl[:k, :k]))
+                m = dot(twice(wb[part, :k]), both(yh[:k, :k], yl[:k, :k], 0))
             else:
-                m = jnp.dot(wh[at[i], :k], yh[:k, :k], preferred_element_type=F32)
-            r, c = index(i)
-            p = phi(m - jnp.where(r[:, :k] == c[:, :k], 1.0, 0.0), i)
-            ph[at[i], :k] = p.astype(BF16)
-            norm = norm + jnp.sum(p * p, keepdims=True)
-        for i in range(order):
-            k = (i + 1) * BLOCK
-            w[at[i], :k] -= jnp.dot(ph[at[i], :k], wh[:k, :k], preferred_element_type=F32)
+                m = dot(wb[part, :k], yh[:k, :k])
+            corner = m[:, k - wide :] * half_mask[...] - half_eye[...]
+            p = corner if k == wide else both(m[:, :wide], corner)
+            ph[part, :k] = p.astype(BF16)
+            strips.append(p)
+            if exact:
+                norm = norm + jnp.sum(p * p, keepdims=True)
+        for p, part, k in zip(strips, (top, low), (wide, size)):
+            square = dot(ph[part, :k], ph[:k, :k])
+            cross = dot_rows(ph[part, :k], ph[:k, :k])
+            corner = cross[:, k - wide :] * half_mask[...]
+            cross = corner if k == wide else both(cross[:, :wide], corner)
+            d = p - square - cross
+            if exact:
+                dh[part, :k], dl[part, :k] = halves(d)
+            else:
+                dh[part, :k] = d.astype(BF16)
+        for part, k in ((top, wide), (low, size)):
+            if exact:
+                change = dot(both(dh[part, :k], dl[part, :k]), twice(wb[:k, :k], 0))
+            else:
+                change = dot(dh[part, :k], wb[:k, :k])
+            w[part, :k] = wb[part, :k].astype(F32) - change
         return jnp.sum(norm)
+
+    def rounded():
+        for part, k in ((top, wide), (low, size)):
+            wb[part, :k] = w[part, :k].astype(BF16)
 
     step(False)
 
     def not_done(state):
         count, norm = state
-        return jnp.logical_and(count < rounds, jnp.logical_not(norm < 2.5e-5))
+        return jnp.logical_and(count < rounds, jnp.logical_not(norm < SMALL))
 
     def again(state):
-        count, _ = state
-        return count + 1, step(True)
+        rounded()
+        return state[0] + 1, step(True)
 
     _, norm = lax.while_loop(not_done, again, (jnp.int32(0), jnp.float32(1.0)))
-    flag[0] = jnp.where(norm < 2.5e-5, 1, 0).astype(jnp.int32)
-    split_w()
-    for i in range(order):
-        k = (i + 1) * BLOCK
-        upper = times((wh[at[i], :k], wl[at[i], :k]), (gh[:k, :], gl[:k, :]))
-        r, c = index(i)
-        triangle[at[i], :] = jnp.where(r <= c, upper, 0.0) * (1.0 / scale)
+    flag[0] = jnp.where(norm < SMALL, 1, 0).astype(jnp.int32)
+    for part, k in ((top, wide), (low, size)):
+        wb[part, :k], dl[part, :k] = halves(w[part, :k])
+    for part, k in ((top, wide), (low, size)):
+        upper = times((wb[part, :k], dl[part, :k]), (gh[:k, k - wide :], gl[:k, k - wide :]))
+        corner = jnp.where(r <= c, upper[:, :wide], 0.0)
+        upper = both(corner, upper[:, wide:]) if k == wide else corner
+        triangle[part, k - wide :] = upper * (1.0 / scale)
+    triangle[low, top] = jnp.zeros((wide, wide), F32)
+    copies = [pltpu.make_async_copy(triangle, triangle_out, out_sem.at[0])]
+    copies[0].start()
     first = 0
     for part in rows:
-        size = part.shape[0]
-        out = against(halves(part[...]), (wh[...], wl[...]))
-        basis[pl.ds(first, size), :] = out * scale
-        first += size
+        for head in range(0, part.shape[0], wide):
+            count = min(wide, part.shape[0] - head)
+            sh, sl = halves(part[head : head + count])
+            here = pl.ds(first, count)
+            for cols, k in ((top, wide), (low, size)):
+                out = against((sh[:, :k], sl[:, :k]), (wb[cols, :k], dl[cols, :k]))
+                basis[here, cols] = out * scale
+            sem = out_sem.at[len(copies)]
+            copies.append(pltpu.make_async_copy(basis.at[here], basis_out.at[here], sem))
+            copies[-1].start()
+            first += count
+    for copy in copies:
+        copy.wait()
 
 
 def factor(pieces, rows, scale):
@@ -417,19 +445,23 @@
     return pl.pallas_call(
         functools.partial(factor_kernel, len(rows), scale, 12),
         out_shape=[
-            jax.ShapeDtypeStruct((local, width), F32),
-            jax.ShapeDtypeStruct(square, F32),
+            pltpu.HBM((local, width), F32),
+            pltpu.HBM(square, F32),
             jax.ShapeDtypeStruct(square, F32),
             jax.ShapeDtypeStruct((1,), jnp.int32),
         ],
         in_specs=[VMEM] * (8 + len(rows)),
-        out_specs=[VMEM, VMEM, VMEM, SMEM],
+        out_specs=[HBM, HBM, VMEM, SMEM],
         scratch_shapes=[
             pltpu.VMEM((number * BLOCK, BLOCK), F32),
+            pltpu.VMEM((width // 2, width // 2), F32),
+            pltpu.VMEM((width // 2, width // 2), F32),
             pltpu.VMEM(square, F32),
+            pltpu.VMEM((local, width), F32),
             pltpu.VMEM(square, F32),
+            pltpu.SemaphoreType.DMA((1 + sum(-(-part.shape[0] * 2 // width) for part in rows),)),
         ]
-        + [pltpu.VMEM(square, BF16)] * 7,
+        + [pltpu.VMEM(square, BF16)] * 8,
         compiler_params=params(24 << 20),
     )(*pieces, *rows)
 
@@ -453,16 +485,23 @@
     places = tile_places[0, 0]
     scale = math.sqrt(local_rows * row_devices * col_devices)
     per_owner = tile_rows // col_devices
-    first = max(1, per_owner // 3)
+    first = max(1, per_owner // 6)
     sizes = (first, per_owner - first) if per_owner > first else (first,)
     chunks = len(sizes)
 
     def products(flip):
         out = tile_products(tile_counts, places, tiles, panels, tile_rows, sizes, flip)
-        return out[:chunks], out[chunks:]
+        return list(out[:chunks]), list(out[chunks:])
 
     send, keep = products(1)
-    across = [swapped(k + swapped(x, 0, 1), 0, 2) for k, x in zip(keep, send)]
+    own, core = [], None
+    for n in range(chunks):
+        if n:
+            send[n], core = lax.optimization_barrier((send[n], core))
+        core = swapped(send[n], 0, 1)
+        own.append(keep[n] + core)
+    across = [swapped(x, 0, 2) for x in own]
+    places, own = lax.optimization_barrier((places, own))
     send, keep = products(0)
     send, keep, across[0] = lax.optimization_barrier((send, keep, across[0]))
     rows, grams = [], []

time: 287 us -> 274 us (0.955)
  Pallas kernels: 58.9 us -> 44.1 us
  starting transfers between devices: 13.8 us -> 22.2 us
  waiting for transfers between devices: 45.7 us -> 41.2 us
    pallas_call x1, Pallas kernels: 39.1 us -> 28.4 us  [factor(): pl.pallas_call(functools.partial(factor_kernel, len(rows), scale, 12), ou...]
    ppermute x13, starting transfers between devices: 4.86 us -> 13.4 us  [swapped(): return lax.ppermute(x, 'col', [(c, c ^ col_flip) for c in range(cols)])]
    pallas_call x2, Pallas kernels: 18.1 us -> 13.3 us  [tile_products(): pl.pallas_call(functools.partial(tile_kernel, resident, flip, stride), ou...]
    ppermute x13, waiting for transfers between devices: 33.5 us -> 29 us  [swapped(): return lax.ppermute(x, 'col', [(c, c ^ col_flip) for c in range(cols)])]
  transfers between devices with their start and end apart: 20 -> 20, of which waited for: 16 -> 14; matrix products, arithmetic and copies ran while one was open for 0% -> 0% of each run, Pallas kernels for 3% -> 3%
where the time goes in v2:
time: 274 us; the launch traced here: 270 us
  other arithmetic  123 us (45%)
  Pallas kernels  44.1 us (16%)
  waiting for transfers between devices  41.2 us (15%)
  starting transfers between devices  22.2 us (8%)
  local copies, waits for them, and re-layouts  18.4 us (7%)
  matrix products  14.6 us (5%)
  loops' own time  3.71 us (1%)
  between operations  3.02 us (1%)
    another operation x14, other arithmetic, direct(): lower = jnp.linalg.cholesky(gram)  78.6 us
    another operation x2, other arithmetic, direct(): jax.scipy.linalg.solve_triangular(lower, own_rows.T, lower=True).T * scale  39.3 us
    ppermute x13, waiting for transfers between devices, swapped(): return lax.ppermute(x, 'col', [(c, c ^ col_flip) for c in range(cols)])  29 us
    pallas_call x1, Pallas kernels, factor(): pl.pallas_call(functools.partial(factor_kernel, len(rows), scale, 12), ou...  28.4 us
    ppermute x13, starting transfers between devices, swapped(): return lax.ppermute(x, 'col', [(c, c ^ col_flip) for c in range(cols)])  13.4 us
    pallas_call x2, Pallas kernels, tile_products(): pl.pallas_call(functools.partial(tile_kernel, resident, flip, stride), ou...  13.3 us
    another operation x13, local copies, waits for them, and re-layouts  13.1 us
    another operation x7, matrix products, direct(): jax.scipy.linalg.solve_triangular(lower, own_rows.T, lower=True).T * scale  9.11 us
  transfers between devices with their start and end apart: 20, of which 14 were waited for; matrix products, arithmetic and copies ran while one was open for 0% of the time, Pallas kernels for 3%

profile of v2, /device:TPU:0, one launch (start us, length us, event | category | flops | bytes accessed | tf_op | source)
XLA Modules:
  0.0 270.1 jit_solution(6939862636858279827)
XLA Ops:
  1.3 6.5 %shard_map.63 = (f32[1,128,512]{2,1,0:T(8,128)S(1)}, f32[5,128,512]{2,1,0:T(8,128)S(1)}, f32[1,128,512]{2,1,0:T(8,128)S(1)}, f32[5,128,512]{2,1,0:T(8,128)S(1)}) custom-call(s32[1,1]{1,0:T(1,128)S(6)} %copy.38.counts, s32[2,360]{1,0:T(2,128)} %bitcast.74, bf16[360,128,128]{2,1,0:T(8,128)(2,1)} %bitcast.70, bf16[48,128,512]{2,1,0:T(8,128)(2,1)} %bitcast.72), custom_call_target="tpu_custom_call" | custom-call | tf_op jit(solution)/shard_map/pallas_call | solution.py:159
  7.8 1.7 collective-permute-start
  11.1 2.7 %collective-permute-start.2 = (f32[1,128,512]{2,1,0:T(8,128)S(1)}, f32[1,128,512]{2,1,0:T(8,128)S(1)}, u32[]{:S(2)}, u32[]{:S(2)}) collective-permute-start(f32[1,128,512]{2,1,0:T(8,128)S(1)} %add.89), channel_id=1, source_target_pairs={{0,2},{1,3},{2,0},{3,1},{4,6},{5,7},{6,4},{7,5},{8,10},{9,11},{10,... | collective-permute-start | bytes 786440 | tf_op jit(solution)/shard_map/ppermute | solution.py:249
  14.2 2.8 %collective-permute-start.4 = (f32[5,128,512]{2,1,0:T(8,128)S(1)}, f32[5,128,512]{2,1,0:T(8,128)S(1)}, u32[]{:S(2)}, u32[]{:S(2)}) collective-permute-start(f32[5,128,512]{2,1,0:T(8,128)S(1)} %add.90), channel_id=1, source_target_pairs={{0,2},{1,3},{2,0},{3,1},{4,6},{5,7},{6,4},{7,5},{8,10},{9,11},{10,... | collective-permute-start | bytes 3932168 | tf_op jit(solution)/shard_map/ppermute | solution.py:249
  17.0 6.7 %shard_map.64 = (f32[1,128,512]{2,1,0:T(8,128)S(1)}, f32[5,128,512]{2,1,0:T(8,128)S(1)}, f32[1,128,512]{2,1,0:T(8,128)S(1)}, f32[5,128,512]{2,1,0:T(8,128)S(1)}) custom-call(s32[1,1]{1,0:T(1,128)S(6)} %copy.38.counts, s32[2,360]{1,0:T(2,128)} %bitcast.75, bf16[360,128,128]{2,1,0:T(8,128)(2,1)} %bitcast.71, bf16[48,128,512]{2,1,0:T(8,128)(2,1)} %bitcast.73), custom_call_target="tpu_custom_call" | custom-call | tf_op jit(solution)/shard_map/pallas_call | solution.py:159
  23.8 1.7 collective-permute-start.3
  25.6 3.0 %collective-permute-done.5.refs_1_ = f32[1,128,512]{2,1,0:T(8,128)S(1)} collective-permute-done((f32[1,128,512]{2,1,0:T(8,128)S(1)}, f32[1,128,512]{2,1,0:T(8,128)S(1)}, u32[]{:S(2)}, u32[]{:S(2)}) %collective-permute-start.5) | collective-permute-done | bytes 262176 | tf_op jit(solution)/shard_map/ppermute | solution.py:249
  28.9 19.8 %collective-permute-done.4.refs_2_ = f32[5,128,512]{2,1,0:T(8,128)S(1)} collective-permute-done((f32[5,128,512]{2,1,0:T(8,128)S(1)}, f32[5,128,512]{2,1,0:T(8,128)S(1)}, u32[]{:S(2)}, u32[]{:S(2)}) %collective-permute-start.4) | collective-permute-done | bytes 1310752 | tf_op jit(solution)/shard_map/ppermute | solution.py:249
  48.8 2.0 shard_map.66
  50.7 1.6 collective-permute-done.6
  52.4 2.7 collective-permute-start.9
  55.1 1.7 collective-permute-start.8
  57.9 1.7 collective-permute-done.8
  59.6 1.7 collective-permute-done.7
  61.3 4.0 %collective-permute-start.12 = (f32[160,128]{1,0:T(8,128)S(1)}, f32[160,128]{1,0:T(8,128)S(1)}, u32[]{:S(2)}, u32[]{:S(2)}) collective-permute-start(f32[160,128]{1,0:T(8,128)S(1)} %fusion.37), channel_id=1, source_target_pairs={{0,24},{4,28},{8,16},{12,20},{16,8},{20,12},{24,0},{28,4},{1,25},{... | collective-permute-start | bytes 245768 | tf_op jit(solution)/shard_map/ppermute | solution.py:251
  66.0 2.1 collective-permute-done.12
  68.1 3.7 %collective-permute-done.11 = f32[160,128]{1,0:T(8,128)S(1)} collective-permute-done((f32[160,128]{1,0:T(8,128)S(1)}, f32[160,128]{1,0:T(8,128)S(1)}, u32[]{:S(2)}, u32[]{:S(2)}) %collective-permute-start.11) | collective-permute-done | bytes 81952 | tf_op jit(solution)/shard_map/ppermute | solution.py:251
  71.8 1.3 collective-permute-start.15
  73.1 2.1 collective-permute-start.14
  75.4 2.6 collective-permute-done.15.refs_3_
  80.9 28.4 %shard_map.67 = (f32[768,512]{1,0:T(8,128)}, f32[512,512]{1,0:T(8,128)}, f32[512,512]{1,0:T(8,128)S(1)}, s32[1]{0:T(128)}) custom-call(f32[160,128]{1,0:T(8,128)S(1)} %add_add_fusion.refs_0_, f32[160,128]{1,0:T(8,128)S(1)} %collective-permute-done.13.refs_1_, f32[160,128]{1,0:T(8,128)S(1)} %collective-permute-done.14.refs_2_, ...), custom_call_target="tpu_custom_call" | custom-call | tf_op jit(solution)/shard_map/pallas_call | solution.py:445
  109.8 159.2 %conditional.1 = ((f32[768,512]{1,0:T(8,128)}, f32[512,512]{1,0:T(8,128)})) conditional(s32[]{:T(128)} %bitcast.21, (f32[512,512]{1,0:T(8,128)S(1)}, f32[128,512]{1,0:T(8,128)S(1)}, f32[640,512]{1,0:T(8,128)}) %tuple.20, (f32[768,512]{1,0:T(8,128)}, f32[512,512]{1,0:T(8,128)}) %tuple.21), branch_computations={%region_0.9_spmd, %region_9.10_spmd} | conditional | flops 1917878784 | bytes 37753128 | solution.py:514
  110.3 1.4 maximum_bitcast_fusion
  111.7 1.3 copy.11
  113.0 1.4 fusion.6
  115.5 11.7 %cholesky.5 = f32[128,128]{1,0:T(8,128)S(1)} custom-call(f32[128,128]{1,0:T(8,128)S(1)} %cholesky.100), custom_call_target="Cholesky" | custom-call | tf_op jit(solution)/shard_map/cond/branch_0_fun/jit(cholesky)/cholesky | solution.py:470
  127.2 9.8 %custom-call.27 = f32[1,128,128]{1,2,0:T(8,128)S(1)} custom-call(f32[1,128,128]{2,1,0:T(8,128)S(1)} %get-tuple-element.105), custom_call_target="InvertDiagBlocksLowerTriangular" | custom-call | tf_op jit(solution)/shard_map/cond/branch_0_fun/jit(cholesky)/cholesky | solution.py:470
  137.2 1.2 constant_dynamic-update-slice_fusion.3
  138.4 1.3 convolution_subtract_fusion.3
  139.7 11.7 %cholesky.29 = f32[128,128]{1,0:T(8,128)S(1)} custom-call(f32[128,128]{1,0:T(8,128)S(1)} %cholesky.104), custom_call_target="Cholesky" | custom-call | tf_op jit(solution)/shard_map/cond/branch_0_fun/jit(cholesky)/cholesky | solution.py:470
  153.5 9.9 %custom-call.28 = f32[1,128,128]{1,2,0:T(8,128)S(1)} custom-call(f32[1,128,128]{2,1,0:T(8,128)S(1)} %get-tuple-element.102), custom_call_target="InvertDiagBlocksLowerTriangular" | custom-call | tf_op jit(solution)/shard_map/cond/branch_0_fun/jit(cholesky)/cholesky | solution.py:470
  163.7 1.3 convolution_subtract_fusion.4
  165.0 11.7 %cholesky.62 = f32[128,128]{1,0:T(8,128)S(1)} custom-call(f32[128,128]{1,0:T(8,128)S(1)} %cholesky.111), custom_call_target="Cholesky" | custom-call | tf_op jit(solution)/shard_map/cond/branch_0_fun/jit(cholesky)/cholesky | solution.py:470
  178.1 9.8 %custom-call.29 = f32[1,128,128]{1,2,0:T(8,128)S(1)} custom-call(f32[1,128,128]{2,1,0:T(8,128)S(1)} %get-tuple-element.99), custom_call_target="InvertDiagBlocksLowerTriangular" | custom-call | tf_op jit(solution)/shard_map/cond/branch_0_fun/jit(cholesky)/cholesky | solution.py:470
  188.2 1.2 convolution_subtract_fusion.5
  189.4 11.7 %cholesky.89 = f32[128,128]{1,0:T(8,128)S(1)} custom-call(f32[128,128]{1,0:T(8,128)S(1)} %convolution_subtract_fusion.5), custom_call_target="Cholesky" | custom-call | tf_op jit(solution)/shard_map/cond/branch_0_fun/jit(cholesky)/cholesky | solution.py:470
  202.5 1.6 multiply_bitcast_fusion
  204.1 2.5 copy.18
  206.7 11.9 %while.1 = (s32[]{:T(128)}, f32[512,512]{1,0:T(8,128)}, s32[4,2]{0,1:T(2,128)S(1)}, f32[4,128,128]{2,1,0:T(8,128)S(1)}, s32[]{:T(128)}) while((s32[]{:T(128)}, f32[512,512]{1,0:T(8,128)}, s32[4,2]{0,1:T(2,128)S(1)}, f32[4,128,128]{2,1,0:T(8,128)S(1)}, s32[]{:T(128)}) %tuple.58), condition=%wide.while_cond, body=%wide.while_body.sunk | while | flops 2 | bytes 131189 | solution.py:472
  207.3 2.3 bitcast_dynamic-update-slice_fusion.2
  210.3 2.3 bitcast_dynamic-update-slice_fusion.2
  213.3 2.3 bitcast_dynamic-update-slice_fusion.2
  216.3 2.2 bitcast_dynamic-update-slice_fusion.2
  218.6 39.3 %custom-call.30 = f32[4,128,128]{1,2,0:T(8,128)S(1)} custom-call(f32[4,128,128]{2,1,0:T(8,128)S(1)} %get-tuple-element.74), custom_call_target="InvertDiagBlocksLowerTriangular" | custom-call | tf_op jit(solution)/shard_map/cond/branch_0_fun/jit(_solve_triangular)/triangular_solve | solution.py:472
  258.4 1.6 convolution_subtract_fusion.1
  260.6 2.3 convolution_subtract_fusion.2
  263.5 3.0 %convolution_subtract_fusion = f32[128,768]{0,1:T(8,128)S(1)} fusion(f32[128,768]{1,0:T(8,128)S(1)} %fusion.22, f32[128,768]{1,0:T(8,128)S(1)} %fusion.24, f32[128,768]{1,0:T(8,128)S(1)} %fusion.11, f32[512,768]{0,1:T(8,128)S(1)} %maximum_bitcast_fusion, f32[512,512]{1,0:T(8,128)} %get-tuple-element.185), kind=kOutput, calls=%fused_computation.5 | convolution fusion | flops 453672960 | bytes 2162688 | tf_op jit(solution)/shard_map/cond/branch_0_fun/jit(_solve_triangular)/triangular_solve | solution.py:472
  267.2 1.6 copy.16
  (60 shorter events, 15.9 us)
Async XLA Ops:
  7.8 2.9 %collective-permute-start = (f32[1,128,512]{2,1,0:T(8,128)S(1)}, f32[1,128,512]{2,1,0:T(8,128)S(1)}, u32[]{:S(2)}, u32[]{:S(2)}) collective-permute-start(f32[1,128,512]{2,1,0:T(8,128)S(1)} %get-tuple-element.40), channel_id=1, source_target_pairs={{0,1},{1,0},{2,3},{3,2},{4,5},{5,4},{6,7},{7,6},{8,9},{9,8},{10,11... | collective-permute-start | bytes 786440 | tf_op jit(solution)/shard_map/ppermute | solution.py:249
  10.7 3.1 %collective-permute-start.1 = (f32[5,128,512]{2,1,0:T(8,128)S(1)}, f32[5,128,512]{2,1,0:T(8,128)S(1)}, u32[]{:S(2)}, u32[]{:S(2)}) collective-permute-start(f32[5,128,512]{2,1,0:T(8,128)S(1)} %get-tuple-element.43), channel_id=1, source_target_pairs={{0,1},{1,0},{2,3},{3,2},{4,5},{5,4},{6,7},{7,6},{8,9},{9,8},{10,11... | collective-permute-start | bytes 3932168 | tf_op jit(solution)/shard_map/ppermute | solution.py:249
  11.1 12.6 %collective-permute-start.2 = (f32[1,128,512]{2,1,0:T(8,128)S(1)}, f32[1,128,512]{2,1,0:T(8,128)S(1)}, u32[]{:S(2)}, u32[]{:S(2)}) collective-permute-start(f32[1,128,512]{2,1,0:T(8,128)S(1)} %add.89), channel_id=1, source_target_pairs={{0,2},{1,3},{2,0},{3,1},{4,6},{5,7},{6,4},{7,5},{8,10},{9,11},{10,... | collective-permute-start | bytes 786440 | tf_op jit(solution)/shard_map/ppermute | solution.py:249
  14.2 34.6 %collective-permute-start.4 = (f32[5,128,512]{2,1,0:T(8,128)S(1)}, f32[5,128,512]{2,1,0:T(8,128)S(1)}, u32[]{:S(2)}, u32[]{:S(2)}) collective-permute-start(f32[5,128,512]{2,1,0:T(8,128)S(1)} %add.90), channel_id=1, source_target_pairs={{0,2},{1,3},{2,0},{3,1},{4,6},{5,7},{6,4},{7,5},{8,10},{9,11},{10,... | collective-permute-start | bytes 3932168 | tf_op jit(solution)/shard_map/ppermute | solution.py:249
  23.8 25.0 %collective-permute-start.3 = (f32[5,128,512]{2,1,0:T(8,128)S(1)}, f32[5,128,512]{2,1,0:T(8,128)S(1)}, u32[]{:S(2)}, u32[]{:S(2)}) collective-permute-start(f32[5,128,512]{2,1,0:T(8,128)S(1)} %get-tuple-element.50), channel_id=1, source_target_pairs={{0,1},{1,0},{2,3},{3,2},{4,5},{5,4},{6,7},{7,6},{8,9},{9,8},{10,11... | collective-permute-start | bytes 3932168 | tf_op jit(solution)/shard_map/ppermute | solution.py:249
  25.5 3.0 %collective-permute-start.5 = (f32[1,128,512]{2,1,0:T(8,128)S(1)}, f32[1,128,512]{2,1,0:T(8,128)S(1)}, u32[]{:S(2)}, u32[]{:S(2)}) collective-permute-start(f32[1,128,512]{2,1,0:T(8,128)S(1)} %get-tuple-element.52), channel_id=1, source_target_pairs={{0,1},{1,0},{2,3},{3,2},{4,5},{5,4},{6,7},{7,6},{8,9},{9,8},{10,11... | collective-permute-start | bytes 786440 | tf_op jit(solution)/shard_map/ppermute | solution.py:249
  50.7 1.6 collective-permute-start.6
  52.4 5.5 %collective-permute-start.9 = (f32[160,128]{1,0:T(8,128)S(1)}, f32[160,128]{1,0:T(8,128)S(1)}, u32[]{:S(2)}, u32[]{:S(2)}) collective-permute-start(f32[160,128]{1,0:T(8,128)S(1)} %get-tuple-element.110), channel_id=1, source_target_pairs={{0,6},{1,7},{2,4},{3,5},{4,2},{5,3},{6,0},{7,1},{8,14},{9,15},{10,... | collective-permute-start | bytes 245768 | tf_op jit(solution)/shard_map/ppermute | solution.py:257
  55.1 4.5 %collective-permute-start.8 = (f32[160,128]{1,0:T(8,128)S(1)}, f32[160,128]{1,0:T(8,128)S(1)}, u32[]{:S(2)}, u32[]{:S(2)}) collective-permute-start(f32[160,128]{1,0:T(8,128)S(1)} %get-tuple-element.111), channel_id=1, source_target_pairs={{0,2},{1,3},{2,0},{3,1},{4,6},{5,7},{6,4},{7,5},{8,10},{9,11},{10,... | collective-permute-start | bytes 245768 | tf_op jit(solution)/shard_map/ppermute | solution.py:249
  56.8 4.4 %collective-permute-start.7 = (f32[160,128]{1,0:T(8,128)S(1)}, f32[160,128]{1,0:T(8,128)S(1)}, u32[]{:S(2)}, u32[]{:S(2)}) collective-permute-start(f32[160,128]{1,0:T(8,128)S(1)} %get-tuple-element.112), channel_id=1, source_target_pairs={{0,4},{4,0},{8,12},{12,8},{16,20},{20,16},{24,28},{28,24},{1,5},{5... | collective-permute-start | bytes 245768 | tf_op jit(solution)/shard_map/ppermute | solution.py:251
  61.3 6.8 %collective-permute-start.12 = (f32[160,128]{1,0:T(8,128)S(1)}, f32[160,128]{1,0:T(8,128)S(1)}, u32[]{:S(2)}, u32[]{:S(2)}) collective-permute-start(f32[160,128]{1,0:T(8,128)S(1)} %fusion.37), channel_id=1, source_target_pairs={{0,24},{4,28},{8,16},{12,20},{16,8},{20,12},{24,0},{28,4},{1,25},{... | collective-permute-start | bytes 245768 | tf_op jit(solution)/shard_map/ppermute | solution.py:251
  65.3 6.5 %collective-permute-start.11 = (f32[160,128]{1,0:T(8,128)S(1)}, f32[160,128]{1,0:T(8,128)S(1)}, u32[]{:S(2)}, u32[]{:S(2)}) collective-permute-start(f32[160,128]{1,0:T(8,128)S(1)} %fusion.37), channel_id=1, source_target_pairs={{0,16},{4,20},{8,24},{12,28},{16,0},{20,4},{24,8},{28,12},{1,17},{... | collective-permute-start | bytes 245768 | tf_op jit(solution)/shard_map/ppermute | solution.py:251
  65.3 6.5 %collective-permute-start.10 = (f32[160,128]{1,0:T(8,128)S(1)}, f32[160,128]{1,0:T(8,128)S(1)}, u32[]{:S(2)}, u32[]{:S(2)}) collective-permute-start(f32[160,128]{1,0:T(8,128)S(1)} %fusion.37), channel_id=1, source_target_pairs={{0,8},{4,12},{8,0},{12,4},{16,24},{20,28},{24,16},{28,20},{1,9},{5... | collective-permute-start | bytes 245768 | tf_op jit(solution)/shard_map/ppermute | solution.py:251
  71.8 6.2 %collective-permute-start.15 = (f32[160,128]{1,0:T(8,128)S(1)}, f32[160,128]{1,0:T(8,128)S(1)}, u32[]{:S(2)}, u32[]{:S(2)}) collective-permute-start(f32[160,128]{1,0:T(8,128)S(1)} %add_add_fusion.refs_0_), channel_id=1, source_target_pairs={{0,6},{1,7},{2,4},{3,5},{4,2},{5,3},{6,0},{7,1},{8,14},{9,15},{10,... | collective-permute-start | bytes 245768 | tf_op jit(solution)/shard_map/ppermute | solution.py:257
  73.1 5.3 %collective-permute-start.14 = (f32[160,128]{1,0:T(8,128)S(1)}, f32[160,128]{1,0:T(8,128)S(1)}, u32[]{:S(2)}, u32[]{:S(2)}) collective-permute-start(f32[160,128]{1,0:T(8,128)S(1)} %add_add_fusion.refs_0_), channel_id=1, source_target_pairs={{0,2},{1,3},{2,0},{3,1},{4,6},{5,7},{6,4},{7,5},{8,10},{9,11},{10,... | collective-permute-start | bytes 245768 | tf_op jit(solution)/shard_map/ppermute | solution.py:249
  75.2 4.4 %collective-permute-start.13 = (f32[160,128]{1,0:T(8,128)S(1)}, f32[160,128]{1,0:T(8,128)S(1)}, u32[]{:S(2)}, u32[]{:S(2)}) collective-permute-start(f32[160,128]{1,0:T(8,128)S(1)} %add_add_fusion.refs_0_), channel_id=1, source_target_pairs={{0,4},{4,0},{8,12},{12,8},{16,20},{20,16},{24,28},{28,24},{1,5},{5... | collective-permute-start | bytes 245768 | tf_op jit(solution)/shard_map/ppermute | solution.py:251
  75.4 4.2 %collective-permute-start.16 = (f32[160,128]{1,0:T(8,128)S(1)}, f32[160,128]{1,0:T(8,128)S(1)}, u32[]{:S(2)}, u32[]{:S(2)}) collective-permute-start(f32[160,128]{1,0:T(8,128)S(1)} %add_add_fusion.refs_0_), channel_id=1, source_target_pairs={{0,1},{1,0},{2,3},{3,2},{4,5},{5,4},{6,7},{7,6},{8,9},{9,8},{10,11... | collective-permute-start | bytes 245768 | tf_op jit(solution)/shard_map/ppermute | solution.py:249
  78.0 1.6 collective-permute-start.19
  78.4 1.3 collective-permute-start.18
  79.6 1.3 collective-permute-start.17
  114.5 1.0 copy-start

commit v3 on v2

--- a/solution.py
+++ b/solution.py
@@ -179,8 +179,23 @@
     )(counts, in_hbm(places), tiles, panels)
 
 
-def block_list(order):
-    return [(i, j) for i in range(order) for j in range(i + 1)]
+def gram_rows(order):
+    under = [(i, j) for i in range(order) for j in range(i)]
+    heads = {block: n * BLOCK for n, block in enumerate(under)}
+    first = len(under) * BLOCK
+    pairs = []
+    for i in range(0, order, 2):
+        pairs.append((i, i + 1, first, 0))
+        first += BLOCK
+    pairs = [(i, j, head, first + n) for n, (i, j, head, _) in enumerate(pairs)]
+    return heads, pairs, first, -(-(first + len(pairs)) // 64) * 64
+
+
+def square_index():
+    return (
+        lax.broadcasted_iota(jnp.int32, (BLOCK, BLOCK), 0),
+        lax.broadcasted_iota(jnp.int32, (BLOCK, BLOCK), 1),
+    )
 
 
 def gram_kernel(last, *refs):
@@ -195,6 +210,8 @@
     left = jnp.concatenate([high, high, low], axis=0)
     right = jnp.concatenate([high, low, high], axis=0)
     order = rows.shape[1] // BLOCK
+    heads, pairs, slab, number = gram_rows(order)
+    diagonal = {}
     for i in range(order):
         strip = lax.dot_general(
             left[:, i * BLOCK : (i + 1) * BLOCK],
@@ -202,13 +219,17 @@
             (((0,), (0,)), ((), ())),
             preferred_element_type=F32,
         )
-        for j in range(i + 1):
-            at = pl.ds((i * (i + 1) // 2 + j) * BLOCK, BLOCK)
-            part = strip[:, j * BLOCK : (j + 1) * BLOCK]
-            if last:
-                for gram in earlier:
-                    part = part + gram[at]
-            acc[at] = part
+        for j in range(i):
+            acc[pl.ds(heads[i, j], BLOCK)] = strip[:, j * BLOCK : (j + 1) * BLOCK]
+        diagonal[i] = strip[:, i * BLOCK :]
+    acc[pl.ds(slab, number - slab)] = jnp.zeros((number - slab, BLOCK), F32)
+    r, c = square_index()
+    for i, j, head, line in pairs:
+        acc[pl.ds(head, BLOCK)] = jnp.where(r >= c, diagonal[i], diagonal[j])
+        acc[pl.ds(line, 1)] = jnp.sum(jnp.where(r == c, diagonal[j], 0.0), axis=0, keepdims=True)
+    if last:
+        for gram in earlier:
+            acc[...] += gram[...]
     if last:
         core_bit, me = place()
         size = own.shape[1]
@@ -227,7 +248,7 @@
 def gram_chunk(keep, core, across, earlier, last):
     width = keep.shape[2]
     rows = keep.shape[0] * keep.shape[1]
-    number = len(block_list(width // BLOCK)) * BLOCK
+    number = gram_rows(width // BLOCK)[3]
     whole = jax.ShapeDtypeStruct((number, BLOCK), F32)
     pieces = jax.ShapeDtypeStruct((4, number // 8, BLOCK), F32)
     row_shape = jax.ShapeDtypeStruct((rows, width), F32)
@@ -315,16 +336,23 @@
         blocks[pl.ds(pl.multiple_of(at, 8), piece.shape[0])] = piece[...]
     at = [slice(i * BLOCK, (i + 1) * BLOCK) for i in range(order)]
 
-    r = lax.broadcasted_iota(jnp.int32, (BLOCK, BLOCK), 0)
-    c = lax.broadcasted_iota(jnp.int32, (BLOCK, BLOCK), 1)
+    r, c = square_index()
     row_scale, col_scale = [], []
+    heads, pairs, _, _ = gram_rows(order)
+    lower = {}
+    for i, j, head, line in pairs:
+        packed = blocks[pl.ds(head, BLOCK)]
+        turned = packed.T
+        lower[i, i] = jnp.where(r >= c, packed, turned)
+        lower[j, j] = jnp.where(
+            r < c, packed, jnp.where(r == c, blocks[pl.ds(line, 1)], turned)
+        )
     for i in range(order):
-        n = i * (i + 1) // 2 + i
-        diagonal = jnp.where(r == c, blocks[n * BLOCK : (n + 1) * BLOCK], 0.0)
+        diagonal = jnp.where(r == c, lower[i, i], 0.0)
         row_scale.append(lax.rsqrt(jnp.sum(diagonal, axis=1, keepdims=True)))
         col_scale.append(lax.rsqrt(jnp.sum(diagonal, axis=0, keepdims=True)))
-    for n, (i, j) in enumerate(block_list(order)):
-        block = blocks[n * BLOCK : (n + 1) * BLOCK]
+    for i, j in [(i, j) for i in range(order) for j in range(i + 1)]:
+        block = lower[i, i] if i == j else blocks[pl.ds(heads[i, j], BLOCK)]
         first = -(block * row_scale[i] * col_scale[j])
         if i == j:
             first = jnp.where(r > c, first, jnp.where(r == c, 1.0, 0.0))
@@ -441,7 +469,7 @@
     width = rows[0].shape[1]
     square = (width, width)
     local = sum(part.shape[0] for part in rows)
-    number = len(block_list(width // BLOCK))
+    number = gram_rows(width // BLOCK)[3]
     return pl.pallas_call(
         functools.partial(factor_kernel, len(rows), scale, 12),
         out_shape=[
@@ -453,7 +481,7 @@
         in_specs=[VMEM] * (8 + len(rows)),
         out_specs=[HBM, HBM, VMEM, SMEM],
         scratch_shapes=[
-            pltpu.VMEM((number * BLOCK, BLOCK), F32),
+            pltpu.VMEM((number, BLOCK), F32),
             pltpu.VMEM((width // 2, width // 2), F32),
             pltpu.VMEM((width // 2, width // 2), F32),
             pltpu.VMEM(square, F32),
@@ -485,8 +513,7 @@
     places = tile_places[0, 0]
     scale = math.sqrt(local_rows * row_devices * col_devices)
     per_owner = tile_rows // col_devices
-    first = max(1, per_owner // 6)
-    sizes = (first, per_owner - first) if per_owner > first else (first,)
+    sizes = tuple(n for n in (per_owner // 6, per_owner - 3 * (per_owner // 6), 2 * (per_owner // 6)) if n)
     chunks = len(sizes)
 
     def products(flip):

time: 274 us -> 277 us (1.011)
  waiting for transfers between devices: 41.2 us -> 38.2 us
  starting transfers between devices: 22.2 us -> 25 us
    ppermute x13 -> x16, starting transfers between devices: 13.4 us -> 16.1 us  [swapped(): return lax.ppermute(x, 'col', [(c, c ^ col_flip) for c in range(cols)])]
    ppermute x13 -> x16, waiting for transfers between devices: 29 us -> 27.8 us  [swapped(): return lax.ppermute(x, 'col', [(c, c ^ col_flip) for c in range(cols)])]
  transfers between devices with their start and end apart: 20 -> 23, of which waited for: 14 -> 18; matrix products, arithmetic and copies ran while one was open for 0% -> 0% of each run, Pallas kernels for 3% -> 3%
where the time goes in v3:
time: 277 us; the launch traced here: 272 us
  other arithmetic  124 us (45%)
  Pallas kernels  44.3 us (16%)
  waiting for transfers between devices  38.2 us (14%)
  starting transfers between devices  25 us (9%)
  local copies, waits for them, and re-layouts  20.3 us (7%)
  matrix products  14.5 us (5%)
  loops' own time  3.35 us (1%)
  between operations  3.15 us (1%)
    another operation x14, other arithmetic, direct(): lower = jnp.linalg.cholesky(gram)  78.8 us
    another operation x2, other arithmetic, direct(): jax.scipy.linalg.solve_triangular(lower, own_rows.T, lower=True).T * scale  40.1 us
    pallas_call x1, Pallas kernels, factor(): pl.pallas_call(functools.partial(factor_kernel, len(rows), scale, 12), ou...  28.3 us
    ppermute x16, waiting for transfers between devices, swapped(): return lax.ppermute(x, 'col', [(c, c ^ col_flip) for c in range(cols)])  27.8 us
    ppermute x16, starting transfers between devices, swapped(): return lax.ppermute(x, 'col', [(c, c ^ col_flip) for c in range(cols)])  16.1 us
    another operation x13, local copies, waits for them, and re-layouts  15 us
    pallas_call x2, Pallas kernels, tile_products(): pl.pallas_call(functools.partial(tile_kernel, resident, flip, stride), ou...  13.2 us
    another operation x7, matrix products, direct(): jax.scipy.linalg.solve_triangular(lower, own_rows.T, lower=True).T * scale  9.08 us
  transfers between devices with their start and end apart: 23, of which 18 were waited for; matrix products, arithmetic and copies ran while one was open for 0% of the time, Pallas kernels for 3%

profile of v3, /device:TPU:0, one launch (start us, length us, event | category | flops | bytes accessed | tf_op | source)
XLA Modules:
  0.0 272.4 jit_solution(2339048113201943541)
XLA Ops:
  1.3 6.5 %shard_map.63 = (f32[1,128,512]{2,1,0:T(8,128)S(1)}, f32[3,128,512]{2,1,0:T(8,128)S(1)}, f32[2,128,512]{2,1,0:T(8,128)S(1)}, f32[1,128,512]{2,1,0:T(8,128)S(1)},...) custom-call(s32[1,1]{1,0:T(1,128)S(6)} %copy.38.counts, s32[2,360]{1,0:T(2,128)} %bitcast.74, ...), custom_call_target="tpu_custom_call" | custom-call | tf_op jit(solution)/shard_map/pallas_call | solution.py:159
  7.8 3.5 %collective-permute-start = (f32[1,128,512]{2,1,0:T(8,128)S(1)}, f32[1,128,512]{2,1,0:T(8,128)S(1)}, u32[]{:S(2)}, u32[]{:S(2)}) collective-permute-start(f32[1,128,512]{2,1,0:T(8,128)S(1)} %get-tuple-element.52), channel_id=1, source_target_pairs={{0,1},{1,0},{2,3},{3,2},{4,5},{5,4},{6,7},{7,6},{8,9},{9,8},{10,11... | collective-permute-start | bytes 786440 | tf_op jit(solution)/shard_map/ppermute | solution.py:270
  11.3 1.2 collective-permute-done
  12.9 1.9 collective-permute-done.1
  15.2 3.4 %collective-permute-start.3 = (f32[1,128,512]{2,1,0:T(8,128)S(1)}, f32[1,128,512]{2,1,0:T(8,128)S(1)}, u32[]{:S(2)}, u32[]{:S(2)}) collective-permute-start(f32[1,128,512]{2,1,0:T(8,128)S(1)} %add.92), channel_id=1, source_target_pairs={{0,2},{1,3},{2,0},{3,1},{4,6},{5,7},{6,4},{7,5},{8,10},{9,11},{10,... | collective-permute-start | bytes 786440 | tf_op jit(solution)/shard_map/ppermute | solution.py:270
  18.9 6.6 %shard_map.64 = (f32[1,128,512]{2,1,0:T(8,128)S(1)}, f32[3,128,512]{2,1,0:T(8,128)S(1)}, f32[2,128,512]{2,1,0:T(8,128)S(1)}, f32[1,128,512]{2,1,0:T(8,128)S(1)},...) custom-call(s32[1,1]{1,0:T(1,128)S(6)} %copy.38.counts, s32[2,360]{1,0:T(2,128)} %bitcast.75, ...), custom_call_target="tpu_custom_call" | custom-call | tf_op jit(solution)/shard_map/pallas_call | solution.py:159
  25.7 2.5 collective-permute-start.7
  28.1 2.6 collective-permute-start.5
  31.3 1.8 collective-permute-done.6.refs_1_
  33.9 8.7 %collective-permute-done.8.refs_2_ = f32[3,128,512]{2,1,0:T(8,128)S(1)} collective-permute-done((f32[3,128,512]{2,1,0:T(8,128)S(1)}, f32[3,128,512]{2,1,0:T(8,128)S(1)}, u32[]{:S(2)}, u32[]{:S(2)}) %collective-permute-start.8) | collective-permute-done | bytes 786464 | tf_op jit(solution)/shard_map/ppermute | solution.py:270
  43.4 10.0 %collective-permute-done.5.refs_2_ = f32[2,128,512]{2,1,0:T(8,128)S(1)} collective-permute-done((f32[2,128,512]{2,1,0:T(8,128)S(1)}, f32[2,128,512]{2,1,0:T(8,128)S(1)}, u32[]{:S(2)}, u32[]{:S(2)}) %collective-permute-start.5) | collective-permute-done | bytes 524320 | tf_op jit(solution)/shard_map/ppermute | solution.py:270
  54.6 1.6 collective-permute-done.9
  56.2 1.8 collective-permute-start.11
  58.0 1.7 collective-permute-start.10
  59.7 1.9 collective-permute-done.12
  63.1 4.0 %collective-permute-start.15 = (f32[136,128]{1,0:T(8,128)S(1)}, f32[136,128]{1,0:T(8,128)S(1)}, u32[]{:S(2)}, u32[]{:S(2)}) collective-permute-start(f32[136,128]{1,0:T(8,128)S(1)} %fusion.37), channel_id=1, source_target_pairs={{0,24},{4,28},{8,16},{12,20},{16,8},{20,12},{24,0},{28,4},{1,25},{... | collective-permute-start | bytes 208904 | tf_op jit(solution)/shard_map/ppermute | solution.py:272
  67.8 1.7 collective-permute-done.15
  69.5 2.9 %collective-permute-done.14 = f32[136,128]{1,0:T(8,128)S(1)} collective-permute-done((f32[136,128]{1,0:T(8,128)S(1)}, f32[136,128]{1,0:T(8,128)S(1)}, u32[]{:S(2)}, u32[]{:S(2)}) %collective-permute-start.14) | collective-permute-done | bytes 69664 | tf_op jit(solution)/shard_map/ppermute | solution.py:272
  72.6 1.6 collective-permute-start.18
  76.2 1.7 collective-permute-done.18.refs_3_
  80.8 28.3 %shard_map.68 = (f32[768,512]{1,0:T(8,128)}, f32[512,512]{1,0:T(8,128)}, f32[512,512]{1,0:T(8,128)S(1)}, s32[1]{0:T(128)}) custom-call(f32[136,128]{1,0:T(8,128)S(1)} %add_add_fusion.refs_0_, f32[136,128]{1,0:T(8,128)S(1)} %collective-permute-done.16.refs_1_, f32[136,128]{1,0:T(8,128)S(1)} %collective-permute-done.17.refs_2_, ...), custom_call_target="tpu_custom_call" | custom-call | tf_op jit(solution)/shard_map/pallas_call | solution.py:473
  109.8 161.5 %conditional.1 = ((f32[768,512]{1,0:T(8,128)}, f32[512,512]{1,0:T(8,128)})) conditional(s32[]{:T(128)} %bitcast.21, (f32[512,512]{1,0:T(8,128)S(1)}, f32[128,512]{1,0:T(8,128)}, f32[384,512]{1,0:T(8,128)S(1)}, f32[256,512]{1,0:T(8,128)}) %tuple.22, (f32[768,512]{1,0:T(8,128)}, f32[512,512]{1,0:T(8,128)}) %tuple.23), branch_computations={%region_0.9_spmd, %region_9.10_spmd} | conditional | flops 1918272000 | bytes 37754144 | solution.py:541
  110.2 1.2 maximum_bitcast_fusion
  111.5 1.3 copy.11
  112.8 1.4 fusion.6
  115.2 11.7 %cholesky.5 = f32[128,128]{1,0:T(8,128)S(1)} custom-call(f32[128,128]{1,0:T(8,128)S(1)} %cholesky.100), custom_call_target="Cholesky" | custom-call | tf_op jit(solution)/shard_map/cond/branch_0_fun/jit(cholesky)/cholesky | solution.py:498
  127.0 9.8 %custom-call.27 = f32[1,128,128]{1,2,0:T(8,128)S(1)} custom-call(f32[1,128,128]{2,1,0:T(8,128)S(1)} %get-tuple-element.127), custom_call_target="InvertDiagBlocksLowerTriangular" | custom-call | tf_op jit(solution)/shard_map/cond/branch_0_fun/jit(cholesky)/cholesky | solution.py:498
  136.9 1.2 constant_dynamic-update-slice_fusion.3
  138.2 1.3 convolution_subtract_fusion.3
  139.4 11.7 %cholesky.29 = f32[128,128]{1,0:T(8,128)S(1)} custom-call(f32[128,128]{1,0:T(8,128)S(1)} %cholesky.104), custom_call_target="Cholesky" | custom-call | tf_op jit(solution)/shard_map/cond/branch_0_fun/jit(cholesky)/cholesky | solution.py:498
  153.1 9.9 %custom-call.28 = f32[1,128,128]{1,2,0:T(8,128)S(1)} custom-call(f32[1,128,128]{2,1,0:T(8,128)S(1)} %get-tuple-element.124), custom_call_target="InvertDiagBlocksLowerTriangular" | custom-call | tf_op jit(solution)/shard_map/cond/branch_0_fun/jit(cholesky)/cholesky | solution.py:498
  163.3 1.3 convolution_subtract_fusion.4
  164.6 11.7 %cholesky.62 = f32[128,128]{1,0:T(8,128)S(1)} custom-call(f32[128,128]{1,0:T(8,128)S(1)} %cholesky.111), custom_call_target="Cholesky" | custom-call | tf_op jit(solution)/shard_map/cond/branch_0_fun/jit(cholesky)/cholesky | solution.py:498
  177.6 9.8 %custom-call.29 = f32[1,128,128]{1,2,0:T(8,128)S(1)} custom-call(f32[1,128,128]{2,1,0:T(8,128)S(1)} %get-tuple-element.121), custom_call_target="InvertDiagBlocksLowerTriangular" | custom-call | tf_op jit(solution)/shard_map/cond/branch_0_fun/jit(cholesky)/cholesky | solution.py:498
  187.6 1.2 convolution_subtract_fusion.5
  188.8 11.7 %cholesky.89 = f32[128,128]{1,0:T(8,128)S(1)} custom-call(f32[128,128]{1,0:T(8,128)S(1)} %convolution_subtract_fusion.5), custom_call_target="Cholesky" | custom-call | tf_op jit(solution)/shard_map/cond/branch_0_fun/jit(cholesky)/cholesky | solution.py:498
  202.2 1.6 multiply_bitcast_fusion
  203.8 2.5 copy.18
  206.3 13.7 %while.1 = (s32[]{:T(128)}, f32[512,512]{1,0:T(8,128)}, s32[4,2]{0,1:T(2,128)S(1)}, f32[4,128,128]{2,1,0:T(8,128)}, s32[]{:T(128)}) while((s32[]{:T(128)}, f32[512,512]{1,0:T(8,128)}, s32[4,2]{0,1:T(2,128)S(1)}, f32[4,128,128]{2,1,0:T(8,128)}, s32[]{:T(128)}) %tuple.60), condition=%wide.while_cond, body=%wide.while_body.sunk | while | flops 2 | bytes 132205 | solution.py:500
  206.9 2.8 %bitcast_dynamic-update-slice_fusion.2 = f32[4,128,128]{2,1,0:T(8,128)} fusion(f32[4,128,128]{2,1,0:T(8,128)} %get-tuple-element.172, s32[]{:T(128)S(6)} %copy.29, f32[512,512]{1,0:T(8,128)} %get-tuple-element.175, s32[]{:T(128)} %bitcast.68, s32[]{:T(128)} %bitcast.69), kind=kLoop, calls=%fused_computation.clone.1 | loop fusion | bytes 132100 | tf_op jit(solution)/shard_map/cond/branch_0_fun/jit(_solve_triangular)/triangular_solve
  210.4 2.8 %bitcast_dynamic-update-slice_fusion.2 = f32[4,128,128]{2,1,0:T(8,128)} fusion(f32[4,128,128]{2,1,0:T(8,128)} %get-tuple-element.172, s32[]{:T(128)S(6)} %copy.29, f32[512,512]{1,0:T(8,128)} %get-tuple-element.175, s32[]{:T(128)} %bitcast.68, s32[]{:T(128)} %bitcast.69), kind=kLoop, calls=%fused_computation.clone.1 | loop fusion | bytes 132100 | tf_op jit(solution)/shard_map/cond/branch_0_fun/jit(_solve_triangular)/triangular_solve
  213.8 2.8 %bitcast_dynamic-update-slice_fusion.2 = f32[4,128,128]{2,1,0:T(8,128)} fusion(f32[4,128,128]{2,1,0:T(8,128)} %get-tuple-element.172, s32[]{:T(128)S(6)} %copy.29, f32[512,512]{1,0:T(8,128)} %get-tuple-element.175, s32[]{:T(128)} %bitcast.68, s32[]{:T(128)} %bitcast.69), kind=kLoop, calls=%fused_computation.clone.1 | loop fusion | bytes 132100 | tf_op jit(solution)/shard_map/cond/branch_0_fun/jit(_solve_triangular)/triangular_solve
  217.3 2.8 %bitcast_dynamic-update-slice_fusion.2 = f32[4,128,128]{2,1,0:T(8,128)} fusion(f32[4,128,128]{2,1,0:T(8,128)} %get-tuple-element.172, s32[]{:T(128)S(6)} %copy.29, f32[512,512]{1,0:T(8,128)} %get-tuple-element.175, s32[]{:T(128)} %bitcast.68, s32[]{:T(128)} %bitcast.69), kind=kLoop, calls=%fused_computation.clone.1 | loop fusion | bytes 132100 | tf_op jit(solution)/shard_map/cond/branch_0_fun/jit(_solve_triangular)/triangular_solve
  220.0 40.1 %custom-call.30 = f32[4,128,128]{1,2,0:T(8,128)S(1)} custom-call(f32[4,128,128]{2,1,0:T(8,128)} %get-tuple-element.95), custom_call_target="InvertDiagBlocksLowerTriangular" | custom-call | tf_op jit(solution)/shard_map/cond/branch_0_fun/jit(_solve_triangular)/triangular_solve | solution.py:500
  260.7 1.6 convolution_subtract_fusion.1
  262.9 2.3 convolution_subtract_fusion.2
  265.7 3.0 %convolution_subtract_fusion = f32[128,768]{0,1:T(8,128)S(1)} fusion(f32[128,768]{1,0:T(8,128)S(1)} %fusion.22, f32[128,768]{1,0:T(8,128)S(1)} %fusion.24, f32[128,768]{1,0:T(8,128)S(1)} %fusion.11, f32[512,768]{0,1:T(8,128)S(1)} %maximum_bitcast_fusion, f32[512,512]{1,0:T(8,128)} %get-tuple-element.211), kind=kOutput, calls=%fused_computation.5 | convolution fusion | flops 453672960 | bytes 2162688 | tf_op jit(solution)/shard_map/cond/branch_0_fun/jit(_solve_triangular)/triangular_solve | solution.py:500
  269.5 1.6 copy.16
  (68 shorter events, 20.7 us)
Async XLA Ops:
  7.8 4.7 %collective-permute-start = (f32[1,128,512]{2,1,0:T(8,128)S(1)}, f32[1,128,512]{2,1,0:T(8,128)S(1)}, u32[]{:S(2)}, u32[]{:S(2)}) collective-permute-start(f32[1,128,512]{2,1,0:T(8,128)S(1)} %get-tuple-element.52), channel_id=1, source_target_pairs={{0,1},{1,0},{2,3},{3,2},{4,5},{5,4},{6,7},{7,6},{8,9},{9,8},{10,11... | collective-permute-start | bytes 786440 | tf_op jit(solution)/shard_map/ppermute | solution.py:270
  12.5 2.3 collective-permute-start.1
  14.8 4.0 %collective-permute-start.2 = (f32[2,128,512]{2,1,0:T(8,128)S(1)}, f32[2,128,512]{2,1,0:T(8,128)S(1)}, u32[]{:S(2)}, u32[]{:S(2)}) collective-permute-start(f32[2,128,512]{2,1,0:T(8,128)S(1)} %get-tuple-element.58), channel_id=1, source_target_pairs={{0,1},{1,0},{2,3},{3,2},{4,5},{5,4},{6,7},{7,6},{8,9},{9,8},{10,11... | collective-permute-start | bytes 1572872 | tf_op jit(solution)/shard_map/ppermute | solution.py:270
  15.2 10.5 %collective-permute-start.3 = (f32[1,128,512]{2,1,0:T(8,128)S(1)}, f32[1,128,512]{2,1,0:T(8,128)S(1)}, u32[]{:S(2)}, u32[]{:S(2)}) collective-permute-start(f32[1,128,512]{2,1,0:T(8,128)S(1)} %add.92), channel_id=1, source_target_pairs={{0,2},{1,3},{2,0},{3,1},{4,6},{5,7},{6,4},{7,5},{8,10},{9,11},{10,... | collective-permute-start | bytes 786440 | tf_op jit(solution)/shard_map/ppermute | solution.py:270
  18.7 23.9 %collective-permute-start.8 = (f32[3,128,512]{2,1,0:T(8,128)S(1)}, f32[3,128,512]{2,1,0:T(8,128)S(1)}, u32[]{:S(2)}, u32[]{:S(2)}) collective-permute-start(f32[3,128,512]{2,1,0:T(8,128)S(1)} %add.93), channel_id=1, source_target_pairs={{0,2},{1,3},{2,0},{3,1},{4,6},{5,7},{6,4},{7,5},{8,10},{9,11},{10,... | collective-permute-start | bytes 2359304 | tf_op jit(solution)/shard_map/ppermute | solution.py:270
  25.7 16.9 %collective-permute-start.7 = (f32[3,128,512]{2,1,0:T(8,128)S(1)}, f32[3,128,512]{2,1,0:T(8,128)S(1)}, u32[]{:S(2)}, u32[]{:S(2)}) collective-permute-start(f32[3,128,512]{2,1,0:T(8,128)S(1)} %get-tuple-element.73), channel_id=1, source_target_pairs={{0,1},{1,0},{2,3},{3,2},{4,5},{5,4},{6,7},{7,6},{8,9},{9,8},{10,11... | collective-permute-start | bytes 2359304 | tf_op jit(solution)/shard_map/ppermute | solution.py:270
  28.1 25.3 %collective-permute-start.5 = (f32[2,128,512]{2,1,0:T(8,128)S(1)}, f32[2,128,512]{2,1,0:T(8,128)S(1)}, u32[]{:S(2)}, u32[]{:S(2)}) collective-permute-start(f32[2,128,512]{2,1,0:T(8,128)S(1)} %add.94), channel_id=1, source_target_pairs={{0,2},{1,3},{2,0},{3,1},{4,6},{5,7},{6,4},{7,5},{8,10},{9,11},{10,... | collective-permute-start | bytes 1572872 | tf_op jit(solution)/shard_map/ppermute | solution.py:270
  30.7 22.7 %collective-permute-start.4 = (f32[2,128,512]{2,1,0:T(8,128)S(1)}, f32[2,128,512]{2,1,0:T(8,128)S(1)}, u32[]{:S(2)}, u32[]{:S(2)}) collective-permute-start(f32[2,128,512]{2,1,0:T(8,128)S(1)} %get-tuple-element.67), channel_id=1, source_target_pairs={{0,1},{1,0},{2,3},{3,2},{4,5},{5,4},{6,7},{7,6},{8,9},{9,8},{10,11... | collective-permute-start | bytes 1572872 | tf_op jit(solution)/shard_map/ppermute | solution.py:270
  30.9 2.1 collective-permute-start.6
  54.6 1.6 collective-permute-start.9
  56.2 5.4 %collective-permute-start.12 = (f32[136,128]{1,0:T(8,128)S(1)}, f32[136,128]{1,0:T(8,128)S(1)}, u32[]{:S(2)}, u32[]{:S(2)}) collective-permute-start(f32[136,128]{1,0:T(8,128)S(1)} %get-tuple-element.132), channel_id=1, source_target_pairs={{0,6},{1,7},{2,4},{3,5},{4,2},{5,3},{6,0},{7,1},{8,14},{9,15},{10,... | collective-permute-start | bytes 208904 | tf_op jit(solution)/shard_map/ppermute | solution.py:278
  56.2 5.9 %collective-permute-start.11 = (f32[136,128]{1,0:T(8,128)S(1)}, f32[136,128]{1,0:T(8,128)S(1)}, u32[]{:S(2)}, u32[]{:S(2)}) collective-permute-start(f32[136,128]{1,0:T(8,128)S(1)} %get-tuple-element.133), channel_id=1, source_target_pairs={{0,2},{1,3},{2,0},{3,1},{4,6},{5,7},{6,4},{7,5},{8,10},{9,11},{10,... | collective-permute-start | bytes 208904 | tf_op jit(solution)/shard_map/ppermute | solution.py:270
  58.0 5.1 %collective-permute-start.10 = (f32[136,128]{1,0:T(8,128)S(1)}, f32[136,128]{1,0:T(8,128)S(1)}, u32[]{:S(2)}, u32[]{:S(2)}) collective-permute-start(f32[136,128]{1,0:T(8,128)S(1)} %get-tuple-element.134), channel_id=1, source_target_pairs={{0,4},{4,0},{8,12},{12,8},{16,20},{20,16},{24,28},{28,24},{1,5},{5... | collective-permute-start | bytes 208904 | tf_op jit(solution)/shard_map/ppermute | solution.py:272
  63.1 6.4 %collective-permute-start.15 = (f32[136,128]{1,0:T(8,128)S(1)}, f32[136,128]{1,0:T(8,128)S(1)}, u32[]{:S(2)}, u32[]{:S(2)}) collective-permute-start(f32[136,128]{1,0:T(8,128)S(1)} %fusion.37), channel_id=1, source_target_pairs={{0,24},{4,28},{8,16},{12,20},{16,8},{20,12},{24,0},{28,4},{1,25},{... | collective-permute-start | bytes 208904 | tf_op jit(solution)/shard_map/ppermute | solution.py:272
  67.1 5.3 %collective-permute-start.14 = (f32[136,128]{1,0:T(8,128)S(1)}, f32[136,128]{1,0:T(8,128)S(1)}, u32[]{:S(2)}, u32[]{:S(2)}) collective-permute-start(f32[136,128]{1,0:T(8,128)S(1)} %fusion.37), channel_id=1, source_target_pairs={{0,16},{4,20},{8,24},{12,28},{16,0},{20,4},{24,8},{28,12},{1,17},{... | collective-permute-start | bytes 208904 | tf_op jit(solution)/shard_map/ppermute | solution.py:272
  67.1 5.5 %collective-permute-start.13 = (f32[136,128]{1,0:T(8,128)S(1)}, f32[136,128]{1,0:T(8,128)S(1)}, u32[]{:S(2)}, u32[]{:S(2)}) collective-permute-start(f32[136,128]{1,0:T(8,128)S(1)} %fusion.37), channel_id=1, source_target_pairs={{0,8},{4,12},{8,0},{12,4},{16,24},{20,28},{24,16},{28,20},{1,9},{5... | collective-permute-start | bytes 208904 | tf_op jit(solution)/shard_map/ppermute | solution.py:272
  72.6 5.3 %collective-permute-start.18 = (f32[136,128]{1,0:T(8,128)S(1)}, f32[136,128]{1,0:T(8,128)S(1)}, u32[]{:S(2)}, u32[]{:S(2)}) collective-permute-start(f32[136,128]{1,0:T(8,128)S(1)} %add_add_fusion.refs_0_), channel_id=1, source_target_pairs={{0,6},{1,7},{2,4},{3,5},{4,2},{5,3},{6,0},{7,1},{8,14},{9,15},{10,... | collective-permute-start | bytes 208904 | tf_op jit(solution)/shard_map/ppermute | solution.py:278
  74.2 4.5 %collective-permute-start.17 = (f32[136,128]{1,0:T(8,128)S(1)}, f32[136,128]{1,0:T(8,128)S(1)}, u32[]{:S(2)}, u32[]{:S(2)}) collective-permute-start(f32[136,128]{1,0:T(8,128)S(1)} %add_add_fusion.refs_0_), channel_id=1, source_target_pairs={{0,2},{1,3},{2,0},{3,1},{4,6},{5,7},{6,4},{7,5},{8,10},{9,11},{10,... | collective-permute-start | bytes 208904 | tf_op jit(solution)/shard_map/ppermute | solution.py:270
  75.2 4.3 %collective-permute-start.16 = (f32[136,128]{1,0:T(8,128)S(1)}, f32[136,128]{1,0:T(8,128)S(1)}, u32[]{:S(2)}, u32[]{:S(2)}) collective-permute-start(f32[136,128]{1,0:T(8,128)S(1)} %add_add_fusion.refs_0_), channel_id=1, source_target_pairs={{0,4},{4,0},{8,12},{12,8},{16,20},{20,16},{24,28},{28,24},{1,5},{5... | collective-permute-start | bytes 208904 | tf_op jit(solution)/shard_map/ppermute | solution.py:272
  76.2 3.4 %collective-permute-start.19 = (f32[136,128]{1,0:T(8,128)S(1)}, f32[136,128]{1,0:T(8,128)S(1)}, u32[]{:S(2)}, u32[]{:S(2)}) collective-permute-start(f32[136,128]{1,0:T(8,128)S(1)} %add_add_fusion.refs_0_), channel_id=1, source_target_pairs={{0,1},{1,0},{2,3},{3,2},{4,5},{5,4},{6,7},{7,6},{8,9},{9,8},{10,11... | collective-permute-start | bytes 208904 | tf_op jit(solution)/shard_map/ppermute | solution.py:270
  77.9 1.7 collective-permute-start.22
  78.6 1.3 collective-permute-start.21
  79.5 1.3 collective-permute-start.20
  114.2 1.0 copy-start

commit v4 on v3

--- a/solution.py
+++ b/solution.py
@@ -11,7 +11,7 @@
 BF16 = jnp.bfloat16
 F32 = jnp.float32
 PAIR = 2
-TURN = 12
+TURN = 16
 PARTS = 2
 BLOCK = 128
 SMALL = 0.01
@@ -32,89 +32,98 @@
     return high, (x - high.astype(F32)).astype(BF16)
 
 
-def tile_kernel(resident, flip, stride, counts, places, tiles, panels, *refs):
-    outs, refs = refs[:-12], refs[-12:]
-    tile_buf, panel_buf, place_of, key, fill, slot, column, first_of, key_of = refs[:9]
-    acc, load_sem, panel_sem = refs[9:]
+def tile_kernel(resident, spans, stride, counts, places, tiles, panels, *refs):
+    outs, refs = refs[: 2 * len(spans)], refs[2 * len(spans) :]
+    tile_buf, panel_buf, place_of, key, first_of, key_of, acc, load_sem, panel_sem = refs[:9]
+    fill, entry = refs[9 : 9 + PARTS], refs[9 + PARTS :]
     slots = tiles.shape[0]
     blocks = acc.shape[0]
-    per_owner = blocks // 2
-    place_load = pltpu.make_async_copy(places, place_of, load_sem.at[0])
+    per_owner = key.shape[0] // lax.axis_size("col")
     panel_loads = [pltpu.make_async_copy(panels, panel_buf, panel_sem.at[0])] if resident else []
-    cuts = [slots * n // PARTS for n in range(PARTS + 1)]
+    cuts = [-(-slots * n // PARTS) for n in range(PARTS + 1)]
     tile_loads = [
         pltpu.make_async_copy(
             tiles.at[pl.ds(a, b - a)], tile_buf.at[pl.ds(a, b - a)], load_sem.at[1 + n]
         )
         for n, (a, b) in enumerate(zip(cuts, cuts[1:]))
     ]
+    place_load = pltpu.make_async_copy(places, place_of, load_sem.at[0])
     for load in [place_load] + panel_loads + tile_loads:
         load.start()
     own = lax.axis_index("col")
 
+    heads = {}
+    for n, (flip, head, end) in enumerate(spans):
+        for inside in range(head, end):
+            heads[flip, inside] = sum(e - h for _, h, e in spans[:n]) + inside - head
     for owner in range(key.shape[0] // per_owner):
-        base = jnp.where((owner & 1) == (own & 1), per_owner, 0)
-        wanted = (owner >> 1) == ((own >> 1) ^ flip)
+        base = jnp.where((owner & 1) == (own & 1), blocks // 2, 0)
+        flipped = (owner >> 1) != (own >> 1)
         for inside in range(per_owner):
-            key[owner * per_owner + inside] = jnp.where(wanted, base + inside, blocks)
-    lists = PARTS * blocks
-    for k in range(lists + 1):
-        fill[k] = k * stride
+            name = [base + heads[f, inside] if (f, inside) in heads else blocks for f in (0, 1)]
+            key[owner * per_owner + inside] = jnp.where(flipped, name[1], name[0])
+    for n in range(PARTS):
+        for k in range(blocks + 1):
+            fill[n][k] = k * stride
     place_load.wait()
     live = counts[0, 0]
-
-    unroll = math.gcd(slots, 8)
+    shift = panels.shape[0].bit_length()
+    unroll = math.gcd(cuts[1], 6)
 
     def put(g, carry):
         for i in range(unroll):
-            t = g * unroll + i
-            part = sum(jnp.where(t >= cut, blocks, 0) for cut in cuts[1:-1])
-            row = key[place_of[0, t]]
-            k = jnp.where(jnp.logical_and(t < live, row < blocks), part + row, lists)
-            p = fill[k]
-            fill[k] = p + 1
-            slot[p] = t
-            column[p] = place_of[1, t]
+            mine = [jnp.minimum(cut + g * unroll + i, slots - 1) for cut in cuts[:-1]]
+            names = [key[place_of[0, t]] for t in mine]
+            made = [(t << shift) | place_of[1, t] for t in mine]
+            lists = [
+                jnp.where(cut + g * unroll + i < live, name, blocks)
+                for cut, name in zip(cuts, names)
+            ]
+            spots = [fill[n][k] for n, k in enumerate(lists)]
+            for n in range(PARTS):
+                fill[n][lists[n]] = spots[n] + 1
+                entry[n][spots[n]] = made[n]
         return carry
 
-    lax.fori_loop(0, (live + unroll - 1) // unroll, put, 0)
-
-    empty = lists * stride + slots
-    for i in range(PAIR):
-        slot[empty + i] = slots
-        column[empty + i] = 0
+    lax.fori_loop(0, (jnp.minimum(live, cuts[1]) + unroll - 1) // unroll, put, 0)
+
+    empty = blocks * stride + cuts[1]
     number, bounds = 0, [0]
-    for k in range(lists):
-        size = fill[k] - k * stride
-        for i in range(PAIR - 1):
-            slot[fill[k] + i] = slots
-            column[fill[k] + i] = 0
-
-        def add_pair(j, at, k=k):
-            first_of[at + j] = k * stride + j * PAIR
-            key_of[at + j] = k % blocks
-            return at
-
-        pairs = (size + PAIR - 1) // PAIR
-        lax.fori_loop(0, pairs, add_pair, number)
-        number += pairs
-        if (k + 1) % blocks == 0:
-            for i in range(TURN - 1):
-                first_of[number + i] = empty
-                key_of[number + i] = 0
-            number = (number + TURN - 1) // TURN * TURN
-            bounds.append(number // TURN)
+    for n in range(PARTS):
+        for i in range(PAIR):
+            entry[n][empty + i] = slots << shift
+        for k in range(blocks):
+            size = fill[n][k] - k * stride
+            for i in range(PAIR - 1):
+                entry[n][fill[n][k] + i] = slots << shift
+
+            def add_pair(j, at, k=k):
+                first_of[at + j] = k * stride + j * PAIR
+                key_of[at + j] = k
+                return at
+
+            pairs = (size + PAIR - 1) // PAIR
+            lax.fori_loop(0, pairs, add_pair, number)
+            number += pairs
+        for i in range(TURN - 1):
+            first_of[number + i] = empty
+            key_of[number + i] = 0
+        number = (number + TURN - 1) // TURN * TURN
+        bounds.append(number // TURN)
     acc[...] = jnp.zeros_like(acc)
     tile_buf[slots] = jnp.zeros_like(tile_buf[slots])
     for load in panel_loads:
         load.wait()
 
-    def turn(g, carry):
+    def turn(n, g, carry):
         firsts = [first_of[g * TURN + i] for i in range(TURN)]
+        entries = [[entry[n][at + j] for j in range(PAIR)] for at in firsts]
+        slot = [[e >> shift for e in pair] for pair in entries]
+        column = [[e & ((1 << shift) - 1) for e in pair] for pair in entries]
         if not resident:
             copies = [
                 pltpu.make_async_copy(
-                    panels.at[column[firsts[i] + j]],
+                    panels.at[column[i][j]],
                     panel_buf.at[i * PAIR + j],
                     panel_sem.at[i * PAIR + j],
                 )
@@ -125,13 +134,10 @@
                 copy.start()
             for copy in copies:
                 copy.wait()
-        for i, at in enumerate(firsts):
-            left = jnp.concatenate([tile_buf[slot[at + j]] for j in range(PAIR)], axis=1)
+        for i in range(TURN):
+            left = jnp.concatenate([tile_buf[slot[i][j]] for j in range(PAIR)], axis=1)
             right = jnp.concatenate(
-                [
-                    panel_buf[column[at + j] if resident else i * PAIR + j]
-                    for j in range(PAIR)
-                ],
+                [panel_buf[column[i][j] if resident else i * PAIR + j] for j in range(PAIR)],
                 axis=0,
             )
             acc[key_of[g * TURN + i]] += jnp.dot(left, right, preferred_element_type=F32)
@@ -139,42 +145,41 @@
 
     for n, load in enumerate(tile_loads):
         load.wait()
-        lax.fori_loop(bounds[n], bounds[n + 1], turn, 0)
+        lax.fori_loop(bounds[n], bounds[n + 1], functools.partial(turn, n), 0)
     first = 0
     for out in outs:
         out[...] = acc[first : first + out.shape[0]]
         first += out.shape[0]
 
 
-def tile_products(counts, places, tiles, panels, tile_rows, sizes, flip):
+def tile_products(counts, places, tiles, panels, tile_rows, spans):
     slots, size, _ = tiles.shape
     width = panels.shape[2]
-    blocks = 2 * sum(sizes)
-    stride = (min(slots, panels.shape[0]) // PAIR + 1) * PAIR
-    lists = PARTS * blocks
-    entries = lists * stride + slots + PAIR
-    pairs = lists * stride // PAIR + TURN * (PARTS + 1)
+    sizes = [end - head for _, head, end in spans] * 2
+    blocks = sum(sizes)
+    part = -(-slots // PARTS)
+    stride = (min(part, panels.shape[0]) // PAIR + 1) * PAIR
+    pairs = PARTS * blocks * stride // PAIR + TURN * (PARTS + 1)
     resident = panels.size * 2 <= 16 << 20
     panel_shape = (panels.shape[0] if resident else PAIR * TURN, size, width)
     return pl.pallas_call(
-        functools.partial(tile_kernel, resident, flip, stride),
-        out_shape=[jax.ShapeDtypeStruct((n, size, width), F32) for n in (*sizes, *sizes)],
+        functools.partial(tile_kernel, resident, spans, stride),
+        out_shape=[jax.ShapeDtypeStruct((n, size, width), F32) for n in sizes],
         in_specs=[SMEM, HBM, HBM, HBM],
-        out_specs=[VMEM] * (2 * len(sizes)),
+        out_specs=[VMEM] * len(sizes),
         scratch_shapes=[
             pltpu.VMEM((slots + 1, size, size), BF16),
             pltpu.VMEM(panel_shape, BF16),
             pltpu.SMEM((2, slots), jnp.int32),
             pltpu.SMEM((tile_rows,), jnp.int32),
-            pltpu.SMEM((lists + 1,), jnp.int32),
-            pltpu.SMEM((entries,), jnp.int32),
-            pltpu.SMEM((entries,), jnp.int32),
             pltpu.SMEM((pairs,), jnp.int32),
             pltpu.SMEM((pairs,), jnp.int32),
             pltpu.VMEM((blocks, size, width), F32),
             pltpu.SemaphoreType.DMA((1 + PARTS,)),
             pltpu.SemaphoreType.DMA((1 if resident else PAIR * TURN,)),
-        ],
+        ]
+        + [pltpu.SMEM((blocks + 1,), jnp.int32)] * PARTS
+        + [pltpu.SMEM((blocks * stride + part + PAIR,), jnp.int32)] * PARTS,
         compiler_params=params(50 << 20),
     )(counts, in_hbm(places), tiles, panels)
 
@@ -513,24 +518,33 @@
     places = tile_places[0, 0]
     scale = math.sqrt(local_rows * row_devices * col_devices)
     per_owner = tile_rows // col_devices
-    sizes = tuple(n for n in (per_owner // 6, per_owner - 3 * (per_owner // 6), 2 * (per_owner // 6)) if n)
-    chunks = len(sizes)
-
-    def products(flip):
-        out = tile_products(tile_counts, places, tiles, panels, tile_rows, sizes, flip)
-        return list(out[:chunks]), list(out[chunks:])
-
-    send, keep = products(1)
-    own, core = [], None
-    for n in range(chunks):
-        if n:
-            send[n], core = lax.optimization_barrier((send[n], core))
-        core = swapped(send[n], 0, 1)
-        own.append(keep[n] + core)
+    cuts = sorted({0, per_owner // 6, per_owner * 5 // 6, per_owner})
+    chunks = list(zip(cuts, cuts[1:]))
+    early = chunks[:-1] or chunks
+    late = chunks[len(early) :]
+
+    def products(spans):
+        out = tile_products(tile_counts, places, tiles, panels, tile_rows, tuple(spans))
+        return out[: len(spans)], out[len(spans) :]
+
+    def across_cores(send, keep):
+        own = []
+        for n in range(len(send)):
+            if n == 1:
+                *send[1:], core = lax.optimization_barrier((*send[1:], core))
+            core = swapped(send[n], 0, 1)
+            own.append(keep[n] + core)
+        return own
+
+    send, keep = products([(1, head, end) for head, end in early])
+    own = across_cores(list(send), keep)
     across = [swapped(x, 0, 2) for x in own]
     places, own = lax.optimization_barrier((places, own))
-    send, keep = products(0)
+    send, keep = products([(1, *chunk) for chunk in late] + [(0, *chunk) for chunk in chunks])
     send, keep, across[0] = lax.optimization_barrier((send, keep, across[0]))
+    across += [swapped(x, 0, 2) for x in across_cores(send[: len(late)], keep[: len(late)])]
+    send, keep = send[len(late) :], keep[len(late) :]
+    chunks = len(chunks)
     rows, grams = [], []
     for n in range(chunks):
         out = gram_chunk(keep[n], swapped(send[n], 0, 1), across[n], grams, n == chunks - 1)
@@ -538,10 +552,9 @@
         grams.append(out[1])
     mine, theirs = gram_sum(*out[1:])
     basis, triangle, gram, flag = factor(mine + theirs, rows, scale)
-    return lax.cond(
-        flag[0] == 1,
-        lambda: (basis, triangle),
-        lambda: direct(gram, rows, scale),
+    return lax.switch(
+        flag[0],
+        (lambda: direct(gram, rows, scale), lambda: (basis, triangle)),
     )
 
 

time: 277 us -> 270 us (0.975)
  starting transfers between devices: 25 us -> 21.1 us
    ppermute x16, starting transfers between devices: 16.1 us -> 11.3 us  [swapped(): return lax.ppermute(x, 'col', [(c, c ^ col_flip) for c in range(cols)])]
    ppermute x2, starting transfers between devices: 1.63 us -> 4.74 us  [swapped(): return lax.ppermute(x, ('row', 'col'), route)]
  transfers between devices with their start and end apart: 23 -> 23, of which waited for: 18 -> 16; matrix products, arithmetic and copies ran while one was open for 0% -> 0% of each run, Pallas kernels for 3% -> 3%
where the time goes in v4:
time: 270 us; the launch traced here: 265 us
  other arithmetic  122 us (45%)
  Pallas kernels  42.6 us (16%)
  waiting for transfers between devices  38.8 us (14%)
  starting transfers between devices  21.1 us (8%)
  local copies, waits for them, and re-layouts  19.5 us (7%)
  matrix products  14.6 us (5%)
  loops' own time  3.5 us (1%)
  between operations  3.14 us (1%)
    another operation x14, other arithmetic, direct(): lower = jnp.linalg.cholesky(gram)  78.9 us
    another operation x2, other arithmetic, direct(): jax.scipy.linalg.solve_triangular(lower, own_rows.T, lower=True).T * scale  39.3 us
    ppermute x16, waiting for transfers between devices, swapped(): return lax.ppermute(x, 'col', [(c, c ^ col_flip) for c in range(cols)])  28.8 us
    pallas_call x1, Pallas kernels, factor(): pl.pallas_call(functools.partial(factor_kernel, len(rows), scale, 12), ou...  27.6 us
    another operation x13, local copies, waits for them, and re-layouts  14.2 us
    pallas_call x2, Pallas kernels, tile_products(): pl.pallas_call(functools.partial(tile_kernel, resident, spans, stride), o...  13.1 us
    ppermute x16, starting transfers between devices, swapped(): return lax.ppermute(x, 'col', [(c, c ^ col_flip) for c in range(cols)])  11.3 us
    another operation x7, matrix products, direct(): jax.scipy.linalg.solve_triangular(lower, own_rows.T, lower=True).T * scale  9.11 us
  transfers between devices with their start and end apart: 23, of which 16 were waited for; matrix products, arithmetic and copies ran while one was open for 0% of the time, Pallas kernels for 3%

profile of v4, /device:TPU:0, one launch (start us, length us, event | category | flops | bytes accessed | tf_op | source)
XLA Modules:
  0.0 265.0 jit_solution(16966328607356700872)
XLA Ops:
  1.3 6.4 %shard_map.63 = (f32[1,128,512]{2,1,0:T(8,128)S(1)}, f32[4,128,512]{2,1,0:T(8,128)S(1)}, f32[1,128,512]{2,1,0:T(8,128)S(1)}, f32[4,128,512]{2,1,0:T(8,128)S(1)}) custom-call(s32[1,1]{1,0:T(1,128)S(6)} %copy.38.counts, s32[2,360]{1,0:T(2,128)} %bitcast.74, bf16[360,128,128]{2,1,0:T(8,128)(2,1)} %bitcast.70, bf16[48,128,512]{2,1,0:T(8,128)(2,1)} %bitcast.72), custom_call_target="tpu_custom_call" | custom-call | tf_op jit(solution)/shard_map/pallas_call | solution.py:165
  7.7 3.3 %collective-permute-start = (f32[1,128,512]{2,1,0:T(8,128)S(1)}, f32[1,128,512]{2,1,0:T(8,128)S(1)}, u32[]{:S(2)}, u32[]{:S(2)}) collective-permute-start(f32[1,128,512]{2,1,0:T(8,128)S(1)} %get-tuple-element.53), channel_id=1, source_target_pairs={{0,1},{1,0},{2,3},{3,2},{4,5},{5,4},{6,7},{7,6},{8,9},{9,8},{10,11... | collective-permute-start | bytes 786440 | tf_op jit(solution)/shard_map/ppermute | solution.py:275
  10.9 1.2 collective-permute-done
  12.6 2.2 collective-permute-done.1
  15.2 6.7 %shard_map.64 = (f32[1,128,512]{2,1,0:T(8,128)S(1)}, f32[1,128,512]{2,1,0:T(8,128)S(1)}, f32[4,128,512]{2,1,0:T(8,128)S(1)}, f32[1,128,512]{2,1,0:T(8,128)S(1)},...) custom-call(s32[1,1]{1,0:T(1,128)S(6)} %copy.38.counts, ...), custom_call_target="tpu_custom_call" | custom-call | tf_op jit(solution)/shard_map/pallas_call | solution.py:165
  21.9 4.5 %collective-permute-start.7 = (f32[4,128,512]{2,1,0:T(8,128)S(1)}, f32[4,128,512]{2,1,0:T(8,128)S(1)}, u32[]{:S(2)}, u32[]{:S(2)}) collective-permute-start(f32[4,128,512]{2,1,0:T(8,128)S(1)} %get-tuple-element.75), channel_id=1, source_target_pairs={{0,1},{1,0},{2,3},{3,2},{4,5},{5,4},{6,7},{7,6},{8,9},{9,8},{10,11... | collective-permute-start | bytes 3145736 | tf_op jit(solution)/shard_map/ppermute | solution.py:275
  27.0 2.1 collective-permute-done.4
  29.8 14.4 %collective-permute-done.8.refs_2_ = f32[4,128,512]{2,1,0:T(8,128)S(1)} collective-permute-done((f32[4,128,512]{2,1,0:T(8,128)S(1)}, f32[4,128,512]{2,1,0:T(8,128)S(1)}, u32[]{:S(2)}, u32[]{:S(2)}) %collective-permute-start.8) | collective-permute-done | bytes 1048608 | tf_op jit(solution)/shard_map/ppermute | solution.py:275
  45.3 3.7 %collective-permute-done.5.refs_2_ = f32[1,128,512]{2,1,0:T(8,128)S(1)} collective-permute-done((f32[1,128,512]{2,1,0:T(8,128)S(1)}, f32[1,128,512]{2,1,0:T(8,128)S(1)}, u32[]{:S(2)}, u32[]{:S(2)}) %collective-permute-start.5) | collective-permute-done | bytes 262176 | tf_op jit(solution)/shard_map/ppermute | solution.py:275
  49.6 1.5 collective-permute-done.9
  51.1 3.2 %collective-permute-start.12 = (f32[136,128]{1,0:T(8,128)S(1)}, f32[136,128]{1,0:T(8,128)S(1)}, u32[]{:S(2)}, u32[]{:S(2)}) collective-permute-start(f32[136,128]{1,0:T(8,128)S(1)} %get-tuple-element.134), channel_id=1, source_target_pairs={{0,6},{1,7},{2,4},{3,5},{4,2},{5,3},{6,0},{7,1},{8,14},{9,15},{10,... | collective-permute-start | bytes 208904 | tf_op jit(solution)/shard_map/ppermute | solution.py:283
  54.9 1.9 collective-permute-done.12
  56.8 1.8 collective-permute-done.11
  58.9 3.1 %collective-permute-start.15 = (f32[136,128]{1,0:T(8,128)S(1)}, f32[136,128]{1,0:T(8,128)S(1)}, u32[]{:S(2)}, u32[]{:S(2)}) collective-permute-start(f32[136,128]{1,0:T(8,128)S(1)} %fusion.37), channel_id=1, source_target_pairs={{0,24},{4,28},{8,16},{12,20},{16,8},{20,12},{24,0},{28,4},{1,25},{... | collective-permute-start | bytes 208904 | tf_op jit(solution)/shard_map/ppermute | solution.py:277
  63.4 2.0 collective-permute-done.15
  65.4 2.3 collective-permute-done.14
  67.7 1.6 collective-permute-start.18
  69.3 1.7 collective-permute-start.17
  71.3 2.3 collective-permute-done.18.refs_3_
  74.0 1.3 collective-permute-done.16.refs_1_
  75.4 1.2 collective-permute-done.20.refs_5_
  76.6 27.6 %shard_map.68 = (f32[768,512]{1,0:T(8,128)}, f32[512,512]{1,0:T(8,128)}, f32[512,512]{1,0:T(8,128)}, s32[1]{0:T(128)}) custom-call(f32[136,128]{1,0:T(8,128)S(1)} %add_add_fusion.refs_0_, f32[136,128]{1,0:T(8,128)S(1)} %collective-permute-done.16.refs_1_, f32[136,128]{1,0:T(8,128)S(1)} %collective-permute-done.17.refs_2_, ...), custom_call_target="tpu_custom_call" | custom-call | tf_op jit(solution)/shard_map/pallas_call | solution.py:478
  104.9 159.0 %conditional.1 = ((f32[768,512]{1,0:T(8,128)}, f32[512,512]{1,0:T(8,128)})) conditional(s32[]{:T(128)} %bitcast.21, (f32[512,512]{1,0:T(8,128)}, f32[128,512]{1,0:T(8,128)S(1)}, f32[512,512]{1,0:T(8,128)S(1)}, f32[128,512]{1,0:T(8,128)S(1)}) %tuple.20, (f32[768,512]{1,0:T(8,128)}, f32[512,512]{1,0:T(8,128)}) %tuple.21), branch_computations={%region_0.9_spmd, %region_9.10_spmd} | conditional | flops 1918272000 | bytes 41947460 | solution.py:555
  105.4 2.6 copy.11
  108.1 1.4 fusion.6
  110.5 11.7 %cholesky.5 = f32[128,128]{1,0:T(8,128)S(1)} custom-call(f32[128,128]{1,0:T(8,128)S(1)} %cholesky.100), custom_call_target="Cholesky" | custom-call | tf_op jit(solution)/shard_map/cond/branch_0_fun/jit(cholesky)/cholesky | solution.py:503
  122.3 9.8 %custom-call.27 = f32[1,128,128]{1,2,0:T(8,128)S(1)} custom-call(f32[1,128,128]{2,1,0:T(8,128)S(1)} %get-tuple-element.129), custom_call_target="InvertDiagBlocksLowerTriangular" | custom-call | tf_op jit(solution)/shard_map/cond/branch_0_fun/jit(cholesky)/cholesky | solution.py:503
  132.2 1.2 constant_dynamic-update-slice_fusion.3
  133.5 1.3 convolution_subtract_fusion.3
  134.7 11.7 %cholesky.29 = f32[128,128]{1,0:T(8,128)S(1)} custom-call(f32[128,128]{1,0:T(8,128)S(1)} %cholesky.104), custom_call_target="Cholesky" | custom-call | tf_op jit(solution)/shard_map/cond/branch_0_fun/jit(cholesky)/cholesky | solution.py:503
  148.4 10.0 %custom-call.28 = f32[1,128,128]{1,2,0:T(8,128)S(1)} custom-call(f32[1,128,128]{2,1,0:T(8,128)S(1)} %get-tuple-element.126), custom_call_target="InvertDiagBlocksLowerTriangular" | custom-call | tf_op jit(solution)/shard_map/cond/branch_0_fun/jit(cholesky)/cholesky | solution.py:503
  158.7 1.3 convolution_subtract_fusion.4
  160.0 11.7 %cholesky.62 = f32[128,128]{1,0:T(8,128)S(1)} custom-call(f32[128,128]{1,0:T(8,128)S(1)} %cholesky.111), custom_call_target="Cholesky" | custom-call | tf_op jit(solution)/shard_map/cond/branch_0_fun/jit(cholesky)/cholesky | solution.py:503
  173.1 9.8 %custom-call.29 = f32[1,128,128]{1,2,0:T(8,128)S(1)} custom-call(f32[1,128,128]{2,1,0:T(8,128)S(1)} %get-tuple-element.123), custom_call_target="InvertDiagBlocksLowerTriangular" | custom-call | tf_op jit(solution)/shard_map/cond/branch_0_fun/jit(cholesky)/cholesky | solution.py:503
  183.1 1.2 convolution_subtract_fusion.5
  184.4 11.7 %cholesky.89 = f32[128,128]{1,0:T(8,128)S(1)} custom-call(f32[128,128]{1,0:T(8,128)S(1)} %convolution_subtract_fusion.5), custom_call_target="Cholesky" | custom-call | tf_op jit(solution)/shard_map/cond/branch_0_fun/jit(cholesky)/cholesky | solution.py:503
  197.6 1.6 multiply_bitcast_fusion
  199.2 2.5 copy.18
  201.7 11.6 %while.1 = (s32[]{:T(128)}, f32[512,512]{1,0:T(8,128)}, s32[4,2]{0,1:T(2,128)S(1)}, f32[4,128,128]{2,1,0:T(8,128)S(1)}, s32[]{:T(128)}) while((s32[]{:T(128)}, f32[512,512]{1,0:T(8,128)}, s32[4,2]{0,1:T(2,128)S(1)}, f32[4,128,128]{2,1,0:T(8,128)S(1)}, s32[]{:T(128)}) %tuple.58), condition=%wide.while_cond, body=%wide.while_body.sunk | while | flops 2 | bytes 131189 | solution.py:505
  202.4 2.2 bitcast_dynamic-update-slice_fusion.2
  205.3 2.2 bitcast_dynamic-update-slice_fusion.2
  208.3 2.2 bitcast_dynamic-update-slice_fusion.2
  211.2 2.2 bitcast_dynamic-update-slice_fusion.2
  213.4 39.3 %custom-call.30 = f32[4,128,128]{1,2,0:T(8,128)S(1)} custom-call(f32[4,128,128]{2,1,0:T(8,128)S(1)} %get-tuple-element.97), custom_call_target="InvertDiagBlocksLowerTriangular" | custom-call | tf_op jit(solution)/shard_map/cond/branch_0_fun/jit(_solve_triangular)/triangular_solve | solution.py:505
  253.2 1.6 convolution_subtract_fusion.1
  255.4 2.3 convolution_subtract_fusion.2
  258.3 3.0 %convolution_subtract_fusion = f32[128,768]{0,1:T(8,128)S(1)} fusion(f32[128,768]{1,0:T(8,128)S(1)} %fusion.22, f32[128,768]{1,0:T(8,128)S(1)} %fusion.24, f32[128,768]{1,0:T(8,128)S(1)} %fusion.11, f32[512,768]{0,1:T(8,128)S(1)} %maximum_bitcast_fusion, f32[512,512]{1,0:T(8,128)} %get-tuple-element.213), kind=kOutput, calls=%fused_computation.5 | convolution fusion | flops 453672960 | bytes 2162688 | tf_op jit(solution)/shard_map/cond/branch_0_fun/jit(_solve_triangular)/triangular_solve | solution.py:505
  262.0 1.6 copy.16
  (70 shorter events, 16.0 us)
Async XLA Ops:
  7.7 4.4 %collective-permute-start = (f32[1,128,512]{2,1,0:T(8,128)S(1)}, f32[1,128,512]{2,1,0:T(8,128)S(1)}, u32[]{:S(2)}, u32[]{:S(2)}) collective-permute-start(f32[1,128,512]{2,1,0:T(8,128)S(1)} %get-tuple-element.53), channel_id=1, source_target_pairs={{0,1},{1,0},{2,3},{3,2},{4,5},{5,4},{6,7},{7,6},{8,9},{9,8},{10,11... | collective-permute-start | bytes 786440 | tf_op jit(solution)/shard_map/ppermute | solution.py:275
  12.1 2.7 %collective-permute-start.1 = (f32[4,128,512]{2,1,0:T(8,128)S(1)}, f32[4,128,512]{2,1,0:T(8,128)S(1)}, u32[]{:S(2)}, u32[]{:S(2)}) collective-permute-start(f32[4,128,512]{2,1,0:T(8,128)S(1)} %get-tuple-element.56), channel_id=1, source_target_pairs={{0,1},{1,0},{2,3},{3,2},{4,5},{5,4},{6,7},{7,6},{8,9},{9,8},{10,11... | collective-permute-start | bytes 3145736 | tf_op jit(solution)/shard_map/ppermute | solution.py:275
  12.5 9.3 %collective-permute-start.2 = (f32[1,128,512]{2,1,0:T(8,128)S(1)}, f32[1,128,512]{2,1,0:T(8,128)S(1)}, u32[]{:S(2)}, u32[]{:S(2)}) collective-permute-start(f32[1,128,512]{2,1,0:T(8,128)S(1)} %add.92), channel_id=1, source_target_pairs={{0,2},{1,3},{2,0},{3,1},{4,6},{5,7},{6,4},{7,5},{8,10},{9,11},{10,... | collective-permute-start | bytes 786440 | tf_op jit(solution)/shard_map/ppermute | solution.py:275
  15.0 29.2 %collective-permute-start.8 = (f32[4,128,512]{2,1,0:T(8,128)S(1)}, f32[4,128,512]{2,1,0:T(8,128)S(1)}, u32[]{:S(2)}, u32[]{:S(2)}) collective-permute-start(f32[4,128,512]{2,1,0:T(8,128)S(1)} %add.93), channel_id=1, source_target_pairs={{0,2},{1,3},{2,0},{3,1},{4,6},{5,7},{6,4},{7,5},{8,10},{9,11},{10,... | collective-permute-start | bytes 3145736 | tf_op jit(solution)/shard_map/ppermute | solution.py:275
  21.9 22.3 %collective-permute-start.7 = (f32[4,128,512]{2,1,0:T(8,128)S(1)}, f32[4,128,512]{2,1,0:T(8,128)S(1)}, u32[]{:S(2)}, u32[]{:S(2)}) collective-permute-start(f32[4,128,512]{2,1,0:T(8,128)S(1)} %get-tuple-element.75), channel_id=1, source_target_pairs={{0,1},{1,0},{2,3},{3,2},{4,5},{5,4},{6,7},{7,6},{8,9},{9,8},{10,11... | collective-permute-start | bytes 3145736 | tf_op jit(solution)/shard_map/ppermute | solution.py:275
  26.4 2.7 %collective-permute-start.4 = (f32[1,128,512]{2,1,0:T(8,128)S(1)}, f32[1,128,512]{2,1,0:T(8,128)S(1)}, u32[]{:S(2)}, u32[]{:S(2)}) collective-permute-start(f32[1,128,512]{2,1,0:T(8,128)S(1)} %get-tuple-element.69), channel_id=1, source_target_pairs={{0,1},{1,0},{2,3},{3,2},{4,5},{5,4},{6,7},{7,6},{8,9},{9,8},{10,11... | collective-permute-start | bytes 786440 | tf_op jit(solution)/shard_map/ppermute | solution.py:275
  26.5 3.0 %collective-permute-start.6 = (f32[1,128,512]{2,1,0:T(8,128)S(1)}, f32[1,128,512]{2,1,0:T(8,128)S(1)}, u32[]{:S(2)}, u32[]{:S(2)}) collective-permute-start(f32[1,128,512]{2,1,0:T(8,128)S(1)} %get-tuple-element.71), channel_id=1, source_target_pairs={{0,1},{1,0},{2,3},{3,2},{4,5},{5,4},{6,7},{7,6},{8,9},{9,8},{10,11... | collective-permute-start | bytes 786440 | tf_op jit(solution)/shard_map/ppermute | solution.py:275
  26.9 18.4 %collective-permute-start.3 = (f32[1,128,512]{2,1,0:T(8,128)S(1)}, f32[1,128,512]{2,1,0:T(8,128)S(1)}, u32[]{:S(2)}, u32[]{:S(2)}) collective-permute-start(f32[1,128,512]{2,1,0:T(8,128)S(1)} %get-tuple-element.67), channel_id=1, source_target_pairs={{0,1},{1,0},{2,3},{3,2},{4,5},{5,4},{6,7},{7,6},{8,9},{9,8},{10,11... | collective-permute-start | bytes 786440 | tf_op jit(solution)/shard_map/ppermute | solution.py:275
  29.1 19.9 %collective-permute-start.5 = (f32[1,128,512]{2,1,0:T(8,128)S(1)}, f32[1,128,512]{2,1,0:T(8,128)S(1)}, u32[]{:S(2)}, u32[]{:S(2)}) collective-permute-start(f32[1,128,512]{2,1,0:T(8,128)S(1)} %add.94), channel_id=1, source_target_pairs={{0,2},{1,3},{2,0},{3,1},{4,6},{5,7},{6,4},{7,5},{8,10},{9,11},{10,... | collective-permute-start | bytes 786440 | tf_op jit(solution)/shard_map/ppermute | solution.py:275
  49.5 1.6 collective-permute-start.9
  51.1 5.7 %collective-permute-start.12 = (f32[136,128]{1,0:T(8,128)S(1)}, f32[136,128]{1,0:T(8,128)S(1)}, u32[]{:S(2)}, u32[]{:S(2)}) collective-permute-start(f32[136,128]{1,0:T(8,128)S(1)} %get-tuple-element.134), channel_id=1, source_target_pairs={{0,6},{1,7},{2,4},{3,5},{4,2},{5,3},{6,0},{7,1},{8,14},{9,15},{10,... | collective-permute-start | bytes 208904 | tf_op jit(solution)/shard_map/ppermute | solution.py:283
  54.3 4.3 %collective-permute-start.11 = (f32[136,128]{1,0:T(8,128)S(1)}, f32[136,128]{1,0:T(8,128)S(1)}, u32[]{:S(2)}, u32[]{:S(2)}) collective-permute-start(f32[136,128]{1,0:T(8,128)S(1)} %get-tuple-element.135), channel_id=1, source_target_pairs={{0,2},{1,3},{2,0},{3,1},{4,6},{5,7},{6,4},{7,5},{8,10},{9,11},{10,... | collective-permute-start | bytes 208904 | tf_op jit(solution)/shard_map/ppermute | solution.py:275
  54.6 4.3 %collective-permute-start.10 = (f32[136,128]{1,0:T(8,128)S(1)}, f32[136,128]{1,0:T(8,128)S(1)}, u32[]{:S(2)}, u32[]{:S(2)}) collective-permute-start(f32[136,128]{1,0:T(8,128)S(1)} %get-tuple-element.136), channel_id=1, source_target_pairs={{0,4},{4,0},{8,12},{12,8},{16,20},{20,16},{24,28},{28,24},{1,5},{5... | collective-permute-start | bytes 208904 | tf_op jit(solution)/shard_map/ppermute | solution.py:277
  58.9 6.5 %collective-permute-start.15 = (f32[136,128]{1,0:T(8,128)S(1)}, f32[136,128]{1,0:T(8,128)S(1)}, u32[]{:S(2)}, u32[]{:S(2)}) collective-permute-start(f32[136,128]{1,0:T(8,128)S(1)} %fusion.37), channel_id=1, source_target_pairs={{0,24},{4,28},{8,16},{12,20},{16,8},{20,12},{24,0},{28,4},{1,25},{... | collective-permute-start | bytes 208904 | tf_op jit(solution)/shard_map/ppermute | solution.py:277
  62.0 5.7 %collective-permute-start.14 = (f32[136,128]{1,0:T(8,128)S(1)}, f32[136,128]{1,0:T(8,128)S(1)}, u32[]{:S(2)}, u32[]{:S(2)}) collective-permute-start(f32[136,128]{1,0:T(8,128)S(1)} %fusion.37), channel_id=1, source_target_pairs={{0,16},{4,20},{8,24},{12,28},{16,0},{20,4},{24,8},{28,12},{1,17},{... | collective-permute-start | bytes 208904 | tf_op jit(solution)/shard_map/ppermute | solution.py:277
  62.2 5.5 %collective-permute-start.13 = (f32[136,128]{1,0:T(8,128)S(1)}, f32[136,128]{1,0:T(8,128)S(1)}, u32[]{:S(2)}, u32[]{:S(2)}) collective-permute-start(f32[136,128]{1,0:T(8,128)S(1)} %fusion.37), channel_id=1, source_target_pairs={{0,8},{4,12},{8,0},{12,4},{16,24},{20,28},{24,16},{28,20},{1,9},{5... | collective-permute-start | bytes 208904 | tf_op jit(solution)/shard_map/ppermute | solution.py:277
  67.7 5.8 %collective-permute-start.18 = (f32[136,128]{1,0:T(8,128)S(1)}, f32[136,128]{1,0:T(8,128)S(1)}, u32[]{:S(2)}, u32[]{:S(2)}) collective-permute-start(f32[136,128]{1,0:T(8,128)S(1)} %add_add_fusion.refs_0_), channel_id=1, source_target_pairs={{0,6},{1,7},{2,4},{3,5},{4,2},{5,3},{6,0},{7,1},{8,14},{9,15},{10,... | collective-permute-start | bytes 208904 | tf_op jit(solution)/shard_map/ppermute | solution.py:283
  69.3 4.6 %collective-permute-start.17 = (f32[136,128]{1,0:T(8,128)S(1)}, f32[136,128]{1,0:T(8,128)S(1)}, u32[]{:S(2)}, u32[]{:S(2)}) collective-permute-start(f32[136,128]{1,0:T(8,128)S(1)} %add_add_fusion.refs_0_), channel_id=1, source_target_pairs={{0,2},{1,3},{2,0},{3,1},{4,6},{5,7},{6,4},{7,5},{8,10},{9,11},{10,... | collective-permute-start | bytes 208904 | tf_op jit(solution)/shard_map/ppermute | solution.py:275
  71.0 4.3 %collective-permute-start.16 = (f32[136,128]{1,0:T(8,128)S(1)}, f32[136,128]{1,0:T(8,128)S(1)}, u32[]{:S(2)}, u32[]{:S(2)}) collective-permute-start(f32[136,128]{1,0:T(8,128)S(1)} %add_add_fusion.refs_0_), channel_id=1, source_target_pairs={{0,4},{4,0},{8,12},{12,8},{16,20},{20,16},{24,28},{28,24},{1,5},{5... | collective-permute-start | bytes 208904 | tf_op jit(solution)/shard_map/ppermute | solution.py:277
  71.3 4.1 %collective-permute-start.19 = (f32[136,128]{1,0:T(8,128)S(1)}, f32[136,128]{1,0:T(8,128)S(1)}, u32[]{:S(2)}, u32[]{:S(2)}) collective-permute-start(f32[136,128]{1,0:T(8,128)S(1)} %add_add_fusion.refs_0_), channel_id=1, source_target_pairs={{0,1},{1,0},{2,3},{3,2},{4,5},{5,4},{6,7},{7,6},{8,9},{9,8},{10,11... | collective-permute-start | bytes 208904 | tf_op jit(solution)/shard_map/ppermute | solution.py:275
  73.5 1.8 collective-permute-start.22
  73.9 1.4 collective-permute-start.21
  75.3 1.3 collective-permute-start.20
  105.4 2.7 %copy-start = (f32[512,512]{1,0:T(8,128)S(1)}, f32[512,512]{1,0:T(8,128)}, u32[]{:S(2)}) copy-start(f32[512,512]{1,0:T(8,128)} %get-tuple-element.98) | copy-start | bytes 3145732 | tf_op jit(solution)/shard_map/cond
  109.5 1.0 copy-start.1

commit v5 on v4

--- a/solution.py
+++ b/solution.py
@@ -236,18 +236,23 @@
         for gram in earlier:
             acc[...] += gram[...]
     if last:
-        core_bit, me = place()
+        core_bit, me, partner = place()
         size = own.shape[1]
         half = acc.shape[0] // 2
         for d in range(own.shape[0]):
-            at = (me ^ d) * size
-            own[d] = acc[pl.ds(pl.multiple_of(core_bit * half + at, 8), size)]
-            send[d] = acc[pl.ds(pl.multiple_of((1 - core_bit) * half + at, 8), size)]
+            at = core_bit * half + (me ^ d) * size
+            own[d] = acc[pl.ds(pl.multiple_of(at, 8), size)]
+            at = (1 - core_bit) * half + (partner ^ d) * size
+            send[d] = acc[pl.ds(pl.multiple_of(at, 8), size)]
 
 
 def place():
     row, col = lax.axis_index("row"), lax.axis_index("col")
-    return col & 1, (row & 1) | (col & 2)
+    core_bit = col & 1
+    near, far = (row & 1) | (col & 2), (row >> 1) & 3
+    if lax.axis_size("row") < 8:
+        return core_bit, near, near
+    return core_bit, jnp.where(core_bit == 0, far, near), jnp.where(core_bit == 0, near, far)
 
 
 def gram_chunk(keep, core, across, earlier, last):
@@ -269,40 +274,41 @@
     )(*args)
 
 
+def routed(x, flips):
+    rows, cols = lax.axis_size("row"), lax.axis_size("col")
+    if flips[0] == flips[1] and not flips[0][0]:
+        return lax.ppermute(x, "col", [(c, c ^ flips[0][1]) for c in range(cols)])
+    route = []
+    for r in range(rows):
+        for c in range(cols):
+            row_flip, col_flip = flips[c & 1]
+            route.append((r * cols + c, (r ^ row_flip) * cols + (c ^ col_flip)))
+    return lax.ppermute(x, ("row", "col"), route)
+
+
 def swapped(x, row_flip, col_flip):
-    rows, cols = lax.axis_size("row"), lax.axis_size("col")
-    if not row_flip:
-        return lax.ppermute(x, "col", [(c, c ^ col_flip) for c in range(cols)])
-    if not col_flip:
-        return lax.ppermute(x, "row", [(r, r ^ row_flip) for r in range(rows)])
-    route = [
-        (r * cols + c, (r ^ row_flip) * cols + (c ^ col_flip))
-        for r in range(rows)
-        for c in range(cols)
-    ]
-    return lax.ppermute(x, ("row", "col"), route)
-
-
-FLIPS = ((1, 0), (0, 2), (1, 2))
+    return routed(x, ((row_flip, col_flip),) * 2)
+
+
+NEAR = ((1, 0), (0, 2), (1, 2))
+FAR = ((2, 0), (4, 0), (6, 0))
 
 
 def gram_sum(own, send):
     theirs = swapped(send, 0, 1)
+    bits = lax.axis_size("row").bit_length() - 1
+    if bits >= 3:
+        shared, added, rest = list(zip(FAR, NEAR)), [list(zip(NEAR, FAR))], range(3, bits)
+    else:
+        shared, added, rest = list(zip(NEAR, NEAR)), [], range(1, bits)
+    added += [[((1 << bit, 0),) * 2] for bit in rest]
     part = [own[d] + theirs[d] for d in range(4)]
-    got = [swapped(x, *flip) for x, flip in zip(part[1:], FLIPS)]
+    got = [routed(x, flips) for x, flips in zip(part[1:], shared)]
     piece = (part[0] + got[0]) + (got[1] + got[2])
-    bits = lax.axis_size("row").bit_length() - 1
-    bit = 1
-    while bit < bits:
-        if bit + 1 < bits:
-            a, b = 1 << bit, 2 << bit
-            got = [swapped(piece, flip, 0) for flip in (a, b, a | b)]
-            piece = (piece + got[0]) + (got[1] + got[2])
-            bit += 2
-        else:
-            piece = piece + swapped(piece, 1 << bit, 0)
-            bit += 1
-    mine = [piece] + [swapped(piece, *flip) for flip in FLIPS]
+    for stage in added:
+        got = [routed(piece, flips) for flips in stage]
+        piece = piece + got[0] if len(got) == 1 else (piece + got[0]) + (got[1] + got[2])
+    mine = [piece] + [routed(piece, flips) for flips in shared]
     return mine, [swapped(x, 0, 1) for x in mine]
 
 
@@ -334,10 +340,11 @@
     wb, gh, gl, yh, yl, ph, dh, dl = refs[19 + chunks :]
     size = gram.shape[0]
     order = size // BLOCK
-    core_bit, me = place()
+    core_bit, me, partner = place()
     half = blocks.shape[0] // 2
     for n, piece in enumerate(pieces):
-        at = (core_bit ^ (n // 4)) * half + (me ^ (n % 4)) * piece.shape[0]
+        first, number = (core_bit, me) if n < 4 else (1 - core_bit, partner)
+        at = first * half + (number ^ (n % 4)) * piece.shape[0]
         blocks[pl.ds(pl.multiple_of(at, 8), piece.shape[0])] = piece[...]
     at = [slice(i * BLOCK, (i + 1) * BLOCK) for i in range(order)]
 

time: 270 us -> 270 us (level)
  Pallas kernels: 42.6 us -> 45.9 us
    pallas_call x2, Pallas kernels: 13.1 us -> 16.3 us  [tile_products(): pl.pallas_call(functools.partial(tile_kernel, resident, spans, stride), o...]
  transfers between devices with their start and end apart: 23 -> 23, of which waited for: 16 -> 17; matrix products, arithmetic and copies ran while one was open for 0% -> 0% of each run, Pallas kernels for 3% -> 4%
where the time goes in v5:
time: 270 us; the launch traced here: 265 us
  other arithmetic  122 us (45%)
  Pallas kernels  45.9 us (17%)
  waiting for transfers between devices  37.1 us (14%)
  local copies, waits for them, and re-layouts  19.5 us (7%)
  starting transfers between devices  19.3 us (7%)
  matrix products  14.6 us (5%)
  loops' own time  3.5 us (1%)
  between operations  3.14 us (1%)
    another operation x14, other arithmetic, direct(): lower = jnp.linalg.cholesky(gram)  78.9 us
    another operation x2, other arithmetic, direct(): jax.scipy.linalg.solve_triangular(lower, own_rows.T, lower=True).T * scale  39.3 us
    pallas_call x1, Pallas kernels, factor(): pl.pallas_call(functools.partial(factor_kernel, len(rows), scale, 12), ou...  27.6 us
    ppermute x14, waiting for transfers between devices, routed(): return lax.ppermute(x, 'col', [(c, c ^ flips[0][1]) for c in range(cols)])  25.9 us
    pallas_call x2, Pallas kernels, tile_products(): pl.pallas_call(functools.partial(tile_kernel, resident, spans, stride), o...  16.3 us
    ppermute x9, starting transfers between devices, routed(): return lax.ppermute(x, ('row', 'col'), route)  14.3 us
    another operation x13, local copies, waits for them, and re-layouts  14.2 us
    ppermute x9, waiting for transfers between devices, routed(): return lax.ppermute(x, ('row', 'col'), route)  11.2 us
  transfers between devices with their start and end apart: 23, of which 17 were waited for; matrix products, arithmetic and copies ran while one was open for 0% of the time, Pallas kernels for 4%

profile of v5, /device:TPU:0, one launch (start us, length us, event | category | flops | bytes accessed | tf_op | source)
XLA Modules:
  0.0 264.7 jit_solution(13048182807259295206)
XLA Ops:
  1.3 7.7 %shard_map.63 = (f32[1,128,512]{2,1,0:T(8,128)S(1)}, f32[4,128,512]{2,1,0:T(8,128)S(1)}, f32[1,128,512]{2,1,0:T(8,128)S(1)}, f32[4,128,512]{2,1,0:T(8,128)S(1)}) custom-call(s32[1,1]{1,0:T(1,128)S(6)} %copy.38.counts, s32[2,360]{1,0:T(2,128)} %bitcast.74, bf16[360,128,128]{2,1,0:T(8,128)(2,1)} %bitcast.70, bf16[48,128,512]{2,1,0:T(8,128)(2,1)} %bitcast.72), custom_call_target="tpu_custom_call" | custom-call | tf_op jit(solution)/shard_map/pallas_call | solution.py:165
  9.0 1.5 collective-permute-done
  10.7 1.8 collective-permute-start.2
  13.4 1.8 collective-permute-start.8
  15.2 8.7 %shard_map.64 = (f32[1,128,512]{2,1,0:T(8,128)S(1)}, f32[1,128,512]{2,1,0:T(8,128)S(1)}, f32[4,128,512]{2,1,0:T(8,128)S(1)}, f32[1,128,512]{2,1,0:T(8,128)S(1)},...) custom-call(s32[1,1]{1,0:T(1,128)S(6)} %copy.38.counts, ...), custom_call_target="tpu_custom_call" | custom-call | tf_op jit(solution)/shard_map/pallas_call | solution.py:165
  25.0 2.0 collective-permute-done.4
  27.8 14.6 %collective-permute-done.8.refs_2_ = f32[4,128,512]{2,1,0:T(8,128)S(1)} collective-permute-done((f32[4,128,512]{2,1,0:T(8,128)S(1)}, f32[4,128,512]{2,1,0:T(8,128)S(1)}, u32[]{:S(2)}, u32[]{:S(2)}) %collective-permute-start.8) | collective-permute-done | bytes 1048608 | tf_op jit(solution)/shard_map/ppermute | solution.py:280
  42.4 1.1 shard_map.66
  43.5 4.0 %collective-permute-done.5.refs_2_ = f32[1,128,512]{2,1,0:T(8,128)S(1)} collective-permute-done((f32[1,128,512]{2,1,0:T(8,128)S(1)}, f32[1,128,512]{2,1,0:T(8,128)S(1)}, u32[]{:S(2)}, u32[]{:S(2)}) %collective-permute-start.5) | collective-permute-done | bytes 262176 | tf_op jit(solution)/shard_map/ppermute | solution.py:280
  48.0 1.5 collective-permute-done.9
  49.6 5.6 %collective-permute-start.12 = (f32[136,128]{1,0:T(8,128)S(1)}, f32[136,128]{1,0:T(8,128)S(1)}, u32[]{:S(2)}, u32[]{:S(2)}) collective-permute-start(f32[136,128]{1,0:T(8,128)S(1)} %get-tuple-element.134), channel_id=1, source_target_pairs={{0,24},{1,7},{2,26},{3,5},{4,28},{5,3},{6,30},{7,1},{8,16},{9,15},... | collective-permute-start | bytes 208904 | tf_op jit(solution)/shard_map/ppermute | solution.py:286
  55.8 1.7 collective-permute-done.12
  57.5 3.0 %collective-permute-done.11 = f32[136,128]{1,0:T(8,128)S(1)} collective-permute-done((f32[136,128]{1,0:T(8,128)S(1)}, f32[136,128]{1,0:T(8,128)S(1)}, u32[]{:S(2)}, u32[]{:S(2)}) %collective-permute-start.11) | collective-permute-done | bytes 69664 | tf_op jit(solution)/shard_map/ppermute | solution.py:286
  60.6 2.0 collective-permute-start.15
  63.1 1.0 collective-permute-start.13
  64.1 1.7 collective-permute-done.15
  65.9 1.1 collective-permute-done.14
  67.5 1.7 collective-permute-start.18
  70.1 1.8 collective-permute-start.16
  71.9 1.7 collective-permute-done.18.refs_3_
  76.4 27.6 %shard_map.68 = (f32[768,512]{1,0:T(8,128)}, f32[512,512]{1,0:T(8,128)}, f32[512,512]{1,0:T(8,128)}, s32[1]{0:T(128)}) custom-call(f32[136,128]{1,0:T(8,128)S(1)} %add_add_fusion.refs_0_, f32[136,128]{1,0:T(8,128)S(1)} %collective-permute-done.16.refs_1_, f32[136,128]{1,0:T(8,128)S(1)} %collective-permute-done.17.refs_2_, ...), custom_call_target="tpu_custom_call" | custom-call | tf_op jit(solution)/shard_map/pallas_call | solution.py:485
  104.6 159.0 %conditional.1 = ((f32[768,512]{1,0:T(8,128)}, f32[512,512]{1,0:T(8,128)})) conditional(s32[]{:T(128)} %bitcast.21, (f32[512,512]{1,0:T(8,128)}, f32[128,512]{1,0:T(8,128)S(1)}, f32[512,512]{1,0:T(8,128)S(1)}, f32[128,512]{1,0:T(8,128)S(1)}) %tuple.20, (f32[768,512]{1,0:T(8,128)}, f32[512,512]{1,0:T(8,128)}) %tuple.21), branch_computations={%region_0.9_spmd, %region_9.10_spmd} | conditional | flops 1918272000 | bytes 41947460 | solution.py:562
  105.2 2.6 copy.11
  107.9 1.4 fusion.6
  109.3 1.0 copy-done.1
  110.3 11.7 %cholesky.5 = f32[128,128]{1,0:T(8,128)S(1)} custom-call(f32[128,128]{1,0:T(8,128)S(1)} %cholesky.100), custom_call_target="Cholesky" | custom-call | tf_op jit(solution)/shard_map/cond/branch_0_fun/jit(cholesky)/cholesky | solution.py:510
  122.1 9.8 %custom-call.27 = f32[1,128,128]{1,2,0:T(8,128)S(1)} custom-call(f32[1,128,128]{2,1,0:T(8,128)S(1)} %get-tuple-element.129), custom_call_target="InvertDiagBlocksLowerTriangular" | custom-call | tf_op jit(solution)/shard_map/cond/branch_0_fun/jit(cholesky)/cholesky | solution.py:510
  132.0 1.2 constant_dynamic-update-slice_fusion.3
  133.3 1.3 convolution_subtract_fusion.3
  134.5 11.7 %cholesky.29 = f32[128,128]{1,0:T(8,128)S(1)} custom-call(f32[128,128]{1,0:T(8,128)S(1)} %cholesky.104), custom_call_target="Cholesky" | custom-call | tf_op jit(solution)/shard_map/cond/branch_0_fun/jit(cholesky)/cholesky | solution.py:510
  148.2 10.0 %custom-call.28 = f32[1,128,128]{1,2,0:T(8,128)S(1)} custom-call(f32[1,128,128]{2,1,0:T(8,128)S(1)} %get-tuple-element.126), custom_call_target="InvertDiagBlocksLowerTriangular" | custom-call | tf_op jit(solution)/shard_map/cond/branch_0_fun/jit(cholesky)/cholesky | solution.py:510
  158.5 1.3 convolution_subtract_fusion.4
  159.8 11.7 %cholesky.62 = f32[128,128]{1,0:T(8,128)S(1)} custom-call(f32[128,128]{1,0:T(8,128)S(1)} %cholesky.111), custom_call_target="Cholesky" | custom-call | tf_op jit(solution)/shard_map/cond/branch_0_fun/jit(cholesky)/cholesky | solution.py:510
  172.9 9.8 %custom-call.29 = f32[1,128,128]{1,2,0:T(8,128)S(1)} custom-call(f32[1,128,128]{2,1,0:T(8,128)S(1)} %get-tuple-element.123), custom_call_target="InvertDiagBlocksLowerTriangular" | custom-call | tf_op jit(solution)/shard_map/cond/branch_0_fun/jit(cholesky)/cholesky | solution.py:510
  182.9 1.2 convolution_subtract_fusion.5
  184.2 11.7 %cholesky.89 = f32[128,128]{1,0:T(8,128)S(1)} custom-call(f32[128,128]{1,0:T(8,128)S(1)} %convolution_subtract_fusion.5), custom_call_target="Cholesky" | custom-call | tf_op jit(solution)/shard_map/cond/branch_0_fun/jit(cholesky)/cholesky | solution.py:510
  197.4 1.6 multiply_bitcast_fusion
  199.0 2.5 copy.18
  201.5 11.6 %while.1 = (s32[]{:T(128)}, f32[512,512]{1,0:T(8,128)}, s32[4,2]{0,1:T(2,128)S(1)}, f32[4,128,128]{2,1,0:T(8,128)S(1)}, s32[]{:T(128)}) while((s32[]{:T(128)}, f32[512,512]{1,0:T(8,128)}, s32[4,2]{0,1:T(2,128)S(1)}, f32[4,128,128]{2,1,0:T(8,128)S(1)}, s32[]{:T(128)}) %tuple.58), condition=%wide.while_cond, body=%wide.while_body.sunk | while | flops 2 | bytes 131189 | solution.py:512
  202.2 2.2 bitcast_dynamic-update-slice_fusion.2
  205.1 2.2 bitcast_dynamic-update-slice_fusion.2
  208.1 2.2 bitcast_dynamic-update-slice_fusion.2
  211.0 2.2 bitcast_dynamic-update-slice_fusion.2
  213.2 39.3 %custom-call.30 = f32[4,128,128]{1,2,0:T(8,128)S(1)} custom-call(f32[4,128,128]{2,1,0:T(8,128)S(1)} %get-tuple-element.97), custom_call_target="InvertDiagBlocksLowerTriangular" | custom-call | tf_op jit(solution)/shard_map/cond/branch_0_fun/jit(_solve_triangular)/triangular_solve | solution.py:512
  253.0 1.6 convolution_subtract_fusion.1
  255.2 2.3 convolution_subtract_fusion.2
  258.1 3.0 %convolution_subtract_fusion = f32[128,768]{0,1:T(8,128)S(1)} fusion(f32[128,768]{1,0:T(8,128)S(1)} %fusion.22, f32[128,768]{1,0:T(8,128)S(1)} %fusion.24, f32[128,768]{1,0:T(8,128)S(1)} %fusion.11, f32[512,768]{0,1:T(8,128)S(1)} %maximum_bitcast_fusion, f32[512,512]{1,0:T(8,128)} %get-tuple-element.213), kind=kOutput, calls=%fused_computation.5 | convolution fusion | flops 453672960 | bytes 2162688 | tf_op jit(solution)/shard_map/cond/branch_0_fun/jit(_solve_triangular)/triangular_solve | solution.py:512
  261.8 1.6 copy.16
  (70 shorter events, 17.1 us)
Async XLA Ops:
  8.9 1.6 collective-permute-start
  10.5 2.7 %collective-permute-start.1 = (f32[4,128,512]{2,1,0:T(8,128)S(1)}, f32[4,128,512]{2,1,0:T(8,128)S(1)}, u32[]{:S(2)}, u32[]{:S(2)}) collective-permute-start(f32[4,128,512]{2,1,0:T(8,128)S(1)} %get-tuple-element.56), channel_id=1, source_target_pairs={{0,1},{1,0},{2,3},{3,2},{4,5},{5,4},{6,7},{7,6},{8,9},{9,8},{10,11... | collective-permute-start | bytes 3145736 | tf_op jit(solution)/shard_map/ppermute | solution.py:280
  10.7 13.2 %collective-permute-start.2 = (f32[1,128,512]{2,1,0:T(8,128)S(1)}, f32[1,128,512]{2,1,0:T(8,128)S(1)}, u32[]{:S(2)}, u32[]{:S(2)}) collective-permute-start(f32[1,128,512]{2,1,0:T(8,128)S(1)} %add.92), channel_id=1, source_target_pairs={{0,2},{1,3},{2,0},{3,1},{4,6},{5,7},{6,4},{7,5},{8,10},{9,11},{10,... | collective-permute-start | bytes 786440 | tf_op jit(solution)/shard_map/ppermute | solution.py:280
  13.4 29.0 %collective-permute-start.8 = (f32[4,128,512]{2,1,0:T(8,128)S(1)}, f32[4,128,512]{2,1,0:T(8,128)S(1)}, u32[]{:S(2)}, u32[]{:S(2)}) collective-permute-start(f32[4,128,512]{2,1,0:T(8,128)S(1)} %add.93), channel_id=1, source_target_pairs={{0,2},{1,3},{2,0},{3,1},{4,6},{5,7},{6,4},{7,5},{8,10},{9,11},{10,... | collective-permute-start | bytes 3145736 | tf_op jit(solution)/shard_map/ppermute | solution.py:280
  23.9 18.5 %collective-permute-start.7 = (f32[4,128,512]{2,1,0:T(8,128)S(1)}, f32[4,128,512]{2,1,0:T(8,128)S(1)}, u32[]{:S(2)}, u32[]{:S(2)}) collective-permute-start(f32[4,128,512]{2,1,0:T(8,128)S(1)} %get-tuple-element.75), channel_id=1, source_target_pairs={{0,1},{1,0},{2,3},{3,2},{4,5},{5,4},{6,7},{7,6},{8,9},{9,8},{10,11... | collective-permute-start | bytes 3145736 | tf_op jit(solution)/shard_map/ppermute | solution.py:280
  24.0 3.0 %collective-permute-start.4 = (f32[1,128,512]{2,1,0:T(8,128)S(1)}, f32[1,128,512]{2,1,0:T(8,128)S(1)}, u32[]{:S(2)}, u32[]{:S(2)}) collective-permute-start(f32[1,128,512]{2,1,0:T(8,128)S(1)} %get-tuple-element.69), channel_id=1, source_target_pairs={{0,1},{1,0},{2,3},{3,2},{4,5},{5,4},{6,7},{7,6},{8,9},{9,8},{10,11... | collective-permute-start | bytes 786440 | tf_op jit(solution)/shard_map/ppermute | solution.py:280
  24.5 2.9 %collective-permute-start.6 = (f32[1,128,512]{2,1,0:T(8,128)S(1)}, f32[1,128,512]{2,1,0:T(8,128)S(1)}, u32[]{:S(2)}, u32[]{:S(2)}) collective-permute-start(f32[1,128,512]{2,1,0:T(8,128)S(1)} %get-tuple-element.71), channel_id=1, source_target_pairs={{0,1},{1,0},{2,3},{3,2},{4,5},{5,4},{6,7},{7,6},{8,9},{9,8},{10,11... | collective-permute-start | bytes 786440 | tf_op jit(solution)/shard_map/ppermute | solution.py:280
  24.5 18.9 %collective-permute-start.3 = (f32[1,128,512]{2,1,0:T(8,128)S(1)}, f32[1,128,512]{2,1,0:T(8,128)S(1)}, u32[]{:S(2)}, u32[]{:S(2)}) collective-permute-start(f32[1,128,512]{2,1,0:T(8,128)S(1)} %get-tuple-element.67), channel_id=1, source_target_pairs={{0,1},{1,0},{2,3},{3,2},{4,5},{5,4},{6,7},{7,6},{8,9},{9,8},{10,11... | collective-permute-start | bytes 786440 | tf_op jit(solution)/shard_map/ppermute | solution.py:280
  27.0 20.4 %collective-permute-start.5 = (f32[1,128,512]{2,1,0:T(8,128)S(1)}, f32[1,128,512]{2,1,0:T(8,128)S(1)}, u32[]{:S(2)}, u32[]{:S(2)}) collective-permute-start(f32[1,128,512]{2,1,0:T(8,128)S(1)} %add.94), channel_id=1, source_target_pairs={{0,2},{1,3},{2,0},{3,1},{4,6},{5,7},{6,4},{7,5},{8,10},{9,11},{10,... | collective-permute-start | bytes 786440 | tf_op jit(solution)/shard_map/ppermute | solution.py:280
  47.9 1.6 collective-permute-start.9
  49.6 8.0 %collective-permute-start.12 = (f32[136,128]{1,0:T(8,128)S(1)}, f32[136,128]{1,0:T(8,128)S(1)}, u32[]{:S(2)}, u32[]{:S(2)}) collective-permute-start(f32[136,128]{1,0:T(8,128)S(1)} %get-tuple-element.134), channel_id=1, source_target_pairs={{0,24},{1,7},{2,26},{3,5},{4,28},{5,3},{6,30},{7,1},{8,16},{9,15},... | collective-permute-start | bytes 208904 | tf_op jit(solution)/shard_map/ppermute | solution.py:286
  55.2 5.4 %collective-permute-start.11 = (f32[136,128]{1,0:T(8,128)S(1)}, f32[136,128]{1,0:T(8,128)S(1)}, u32[]{:S(2)}, u32[]{:S(2)}) collective-permute-start(f32[136,128]{1,0:T(8,128)S(1)} %get-tuple-element.135), channel_id=1, source_target_pairs={{0,16},{1,3},{2,18},{3,1},{4,20},{5,7},{6,22},{7,5},{8,24},{9,11},... | collective-permute-start | bytes 208904 | tf_op jit(solution)/shard_map/ppermute | solution.py:286
  55.4 5.2 %collective-permute-start.10 = (f32[136,128]{1,0:T(8,128)S(1)}, f32[136,128]{1,0:T(8,128)S(1)}, u32[]{:S(2)}, u32[]{:S(2)}) collective-permute-start(f32[136,128]{1,0:T(8,128)S(1)} %get-tuple-element.136), channel_id=1, source_target_pairs={{0,8},{1,5},{2,10},{3,7},{4,12},{5,1},{6,14},{7,3},{8,0},{9,13},{1... | collective-permute-start | bytes 208904 | tf_op jit(solution)/shard_map/ppermute | solution.py:286
  60.6 5.3 %collective-permute-start.15 = (f32[136,128]{1,0:T(8,128)S(1)}, f32[136,128]{1,0:T(8,128)S(1)}, u32[]{:S(2)}, u32[]{:S(2)}) collective-permute-start(f32[136,128]{1,0:T(8,128)S(1)} %fusion.37), channel_id=1, source_target_pairs={{0,6},{1,25},{2,4},{3,27},{4,2},{5,29},{6,0},{7,31},{8,14},{9,17},... | collective-permute-start | bytes 208904 | tf_op jit(solution)/shard_map/ppermute | solution.py:286
  62.6 4.3 %collective-permute-start.14 = (f32[136,128]{1,0:T(8,128)S(1)}, f32[136,128]{1,0:T(8,128)S(1)}, u32[]{:S(2)}, u32[]{:S(2)}) collective-permute-start(f32[136,128]{1,0:T(8,128)S(1)} %fusion.37), channel_id=1, source_target_pairs={{0,2},{1,17},{2,0},{3,19},{4,6},{5,21},{6,4},{7,23},{8,10},{9,25},... | collective-permute-start | bytes 208904 | tf_op jit(solution)/shard_map/ppermute | solution.py:286
  63.1 4.3 %collective-permute-start.13 = (f32[136,128]{1,0:T(8,128)S(1)}, f32[136,128]{1,0:T(8,128)S(1)}, u32[]{:S(2)}, u32[]{:S(2)}) collective-permute-start(f32[136,128]{1,0:T(8,128)S(1)} %fusion.37), channel_id=1, source_target_pairs={{0,4},{1,9},{2,6},{3,11},{4,0},{5,13},{6,2},{7,15},{8,12},{9,1},{1... | collective-permute-start | bytes 208904 | tf_op jit(solution)/shard_map/ppermute | solution.py:286
  67.5 6.2 %collective-permute-start.18 = (f32[136,128]{1,0:T(8,128)S(1)}, f32[136,128]{1,0:T(8,128)S(1)}, u32[]{:S(2)}, u32[]{:S(2)}) collective-permute-start(f32[136,128]{1,0:T(8,128)S(1)} %add_add_fusion.refs_0_), channel_id=1, source_target_pairs={{0,24},{1,7},{2,26},{3,5},{4,28},{5,3},{6,30},{7,1},{8,16},{9,15},... | collective-permute-start | bytes 208904 | tf_op jit(solution)/shard_map/ppermute | solution.py:286
  69.2 5.3 %collective-permute-start.17 = (f32[136,128]{1,0:T(8,128)S(1)}, f32[136,128]{1,0:T(8,128)S(1)}, u32[]{:S(2)}, u32[]{:S(2)}) collective-permute-start(f32[136,128]{1,0:T(8,128)S(1)} %add_add_fusion.refs_0_), channel_id=1, source_target_pairs={{0,16},{1,3},{2,18},{3,1},{4,20},{5,7},{6,22},{7,5},{8,24},{9,11},... | collective-permute-start | bytes 208904 | tf_op jit(solution)/shard_map/ppermute | solution.py:286
  70.1 5.0 %collective-permute-start.16 = (f32[136,128]{1,0:T(8,128)S(1)}, f32[136,128]{1,0:T(8,128)S(1)}, u32[]{:S(2)}, u32[]{:S(2)}) collective-permute-start(f32[136,128]{1,0:T(8,128)S(1)} %add_add_fusion.refs_0_), channel_id=1, source_target_pairs={{0,8},{1,5},{2,10},{3,7},{4,12},{5,1},{6,14},{7,3},{8,0},{9,13},{1... | collective-permute-start | bytes 208904 | tf_op jit(solution)/shard_map/ppermute | solution.py:286
  71.9 3.2 %collective-permute-start.19 = (f32[136,128]{1,0:T(8,128)S(1)}, f32[136,128]{1,0:T(8,128)S(1)}, u32[]{:S(2)}, u32[]{:S(2)}) collective-permute-start(f32[136,128]{1,0:T(8,128)S(1)} %add_add_fusion.refs_0_), channel_id=1, source_target_pairs={{0,1},{1,0},{2,3},{3,2},{4,5},{5,4},{6,7},{7,6},{8,9},{9,8},{10,11... | collective-permute-start | bytes 208904 | tf_op jit(solution)/shard_map/ppermute | solution.py:280
  73.6 1.5 collective-permute-start.22
  74.5 1.3 collective-permute-start.21
  75.1 1.3 collective-permute-start.20
  105.2 2.7 %copy-start = (f32[512,512]{1,0:T(8,128)S(1)}, f32[512,512]{1,0:T(8,128)}, u32[]{:S(2)}) copy-start(f32[512,512]{1,0:T(8,128)} %get-tuple-element.98) | copy-start | bytes 3145732 | tf_op jit(solution)/shard_map/cond
  109.3 1.0 copy-start.1

commit v6 on v4

--- a/solution.py
+++ b/solution.py
@@ -329,9 +329,9 @@
 
 def factor_kernel(chunks, scale, rounds, *refs):
     pieces, rows = refs[:8], refs[8 : 8 + chunks]
-    basis_out, triangle_out, gram, flag = refs[8 + chunks : 12 + chunks]
-    blocks, half_mask, half_eye, w, basis, triangle, out_sem = refs[12 + chunks : 19 + chunks]
-    wb, gh, gl, yh, yl, ph, dh, dl = refs[19 + chunks :]
+    basis_out, triangle_out = refs[8 + chunks : 10 + chunks]
+    blocks, gram, half_mask, half_eye, w, basis, triangle, out_sem = refs[10 + chunks : 18 + chunks]
+    wb, gh, gl, yh, yl, ph, dh, dl = refs[18 + chunks :]
     size = gram.shape[0]
     order = size // BLOCK
     core_bit, me = place()
@@ -391,11 +391,11 @@
 
     def step(exact):
         for cols, k in ((top, wide), (low, size)):
-            y = dot_rows(both(gh[:, :k], gl[:, :k]), twice(wb[cols, :k]))
             if exact:
+                y = dot_rows(both(gh[:, :k], gl[:, :k]), twice(wb[cols, :k]))
                 yh[:, cols], yl[:, cols] = halves(y)
             else:
-                yh[:, cols] = y.astype(BF16)
+                yh[:, cols] = dot_rows(gh[:, :k], wb[cols, :k]).astype(BF16)
         norm = jnp.zeros((1, 1), F32)
         strips = []
         for part, k in ((top, wide), (low, size)):
@@ -442,32 +442,101 @@
         return state[0] + 1, step(True)
 
     _, norm = lax.while_loop(not_done, again, (jnp.int32(0), jnp.float32(1.0)))
-    flag[0] = jnp.where(norm < SMALL, 1, 0).astype(jnp.int32)
-    for part, k in ((top, wide), (low, size)):
-        wb[part, :k], dl[part, :k] = halves(w[part, :k])
-    for part, k in ((top, wide), (low, size)):
-        upper = times((wb[part, :k], dl[part, :k]), (gh[:k, k - wide :], gl[:k, k - wide :]))
-        corner = jnp.where(r <= c, upper[:, :wide], 0.0)
-        upper = both(corner, upper[:, wide:]) if k == wide else corner
-        triangle[part, k - wide :] = upper * (1.0 / scale)
-    triangle[low, top] = jnp.zeros((wide, wide), F32)
-    copies = [pltpu.make_async_copy(triangle, triangle_out, out_sem.at[0])]
-    copies[0].start()
-    first = 0
-    for part in rows:
-        for head in range(0, part.shape[0], wide):
-            count = min(wide, part.shape[0] - head)
-            sh, sl = halves(part[head : head + count])
-            here = pl.ds(first, count)
-            for cols, k in ((top, wide), (low, size)):
-                out = against((sh[:, :k], sl[:, :k]), (wb[cols, :k], dl[cols, :k]))
-                basis[here, cols] = out * scale
-            sem = out_sem.at[len(copies)]
-            copies.append(pltpu.make_async_copy(basis.at[here], basis_out.at[here], sem))
-            copies[-1].start()
-            first += count
-    for copy in copies:
-        copy.wait()
+    triangle_copy = pltpu.make_async_copy(triangle, triangle_out, out_sem.at[0])
+    found = norm < SMALL
+
+    @pl.when(found)
+    def _():
+        for part, k in ((top, wide), (low, size)):
+            wb[part, :k], dl[part, :k] = halves(w[part, :k])
+        for part, k in ((top, wide), (low, size)):
+            upper = times((wb[part, :k], dl[part, :k]), (gh[:k, k - wide :], gl[:k, k - wide :]))
+            corner = jnp.where(r <= c, upper[:, :wide], 0.0)
+            upper = both(corner, upper[:, wide:]) if k == wide else corner
+            triangle[part, k - wide :] = upper * (1.0 / scale)
+        triangle[low, top] = jnp.zeros((wide, wide), F32)
+        triangle_copy.start()
+        copies = [triangle_copy]
+        first = 0
+        for part in rows:
+            for head in range(0, part.shape[0], wide):
+                count = min(wide, part.shape[0] - head)
+                sh, sl = halves(part[head : head + count])
+                here = pl.ds(first, count)
+                for cols, k in ((top, wide), (low, size)):
+                    out = against((sh[:, :k], sl[:, :k]), (wb[cols, :k], dl[cols, :k]))
+                    basis[here, cols] = out * scale
+                sem = out_sem.at[len(copies)]
+                copies.append(pltpu.make_async_copy(basis.at[here], basis_out.at[here], sem))
+                copies[-1].start()
+                first += count
+        for copy in copies:
+            copy.wait()
+
+    @pl.when(jnp.logical_not(found))
+    def _():
+        eliminate(gram, triangle, w)
+        triangle[...] = triangle[...] * (1.0 / scale)
+        first = 0
+        for part in rows:
+
+            def strip(n, carry, part=part, first=first):
+                at = pl.ds(pl.multiple_of(n * BLOCK, BLOCK), BLOCK)
+                out = exact_dot(part[at, :], w[...], (((1,), (1,)), ((), ())))
+                here = pl.multiple_of(first + n * BLOCK, BLOCK)
+                basis[pl.ds(here, BLOCK), :] = out * scale
+                return carry
+
+            lax.fori_loop(0, part.shape[0] // BLOCK, strip, 0)
+            first += part.shape[0]
+        basis_copy = pltpu.make_async_copy(basis, basis_out, out_sem.at[1])
+        triangle_copy.start()
+        basis_copy.start()
+        triangle_copy.wait()
+        basis_copy.wait()
+
+
+def exact_dot(left, right, dims):
+    return lax.dot_general(
+        left, right, dims, precision=lax.Precision.HIGHEST, preferred_element_type=F32
+    )
+
+
+def eliminate(gram, upper, inverse):
+    size = gram.shape[0]
+    columns = lax.broadcasted_iota(jnp.int32, (BLOCK, size), 1)
+    lines = lax.broadcasted_iota(jnp.int32, (BLOCK, size), 0)
+    r, c = square_index()
+    line = r[:, :1]
+    for n in range(size // BLOCK):
+        here = slice(n * BLOCK, (n + 1) * BLOCK)
+        left = gram[here, :]
+        right = jnp.where(columns == lines + n * BLOCK, 1.0, 0.0)
+        if n:
+            above = upper[: n * BLOCK, here]
+            over = (((0,), (0,)), ((), ()))
+            left = left - exact_dot(above, upper[: n * BLOCK, :], over)
+            right = right - exact_dot(above, inverse[: n * BLOCK, :], over)
+        upper[here, :] = left
+        inverse[here, :] = right
+
+        def row(j, carry, n=n, here=here):
+            at = pl.ds(n * BLOCK + j, 1)
+            corner = upper[here, here]
+            column = jnp.sum(jnp.where(c == j, corner, 0.0), axis=1, keepdims=True)
+            pivot = jnp.sum(jnp.where(line == j, column, 0.0), axis=0, keepdims=True)
+            root = lax.rsqrt(pivot)
+            left = upper[at, :] * root
+            right = inverse[at, :] * root
+            factor_of = jnp.where(line > j, column * root, 0.0)
+            upper[here, :] = upper[here, :] - factor_of * left
+            inverse[here, :] = inverse[here, :] - factor_of * right
+            upper[at, :] = left
+            inverse[at, :] = right
+            return carry
+
+        lax.fori_loop(0, BLOCK, row, 0)
+        upper[here, :] = jnp.where(columns >= lines + n * BLOCK, upper[here, :], 0.0)
 
 
 def factor(pieces, rows, scale):
@@ -476,17 +545,16 @@
     local = sum(part.shape[0] for part in rows)
     number = gram_rows(width // BLOCK)[3]
     return pl.pallas_call(
-        functools.partial(factor_kernel, len(rows), scale, 12),
+        functools.partial(factor_kernel, len(rows), scale, 6),
         out_shape=[
             pltpu.HBM((local, width), F32),
             pltpu.HBM(square, F32),
-            jax.ShapeDtypeStruct(square, F32),
-            jax.ShapeDtypeStruct((1,), jnp.int32),
         ],
         in_specs=[VMEM] * (8 + len(rows)),
-        out_specs=[HBM, HBM, VMEM, SMEM],
+        out_specs=[HBM, HBM],
         scratch_shapes=[
             pltpu.VMEM((number, BLOCK), F32),
+            pltpu.VMEM(square, F32),
             pltpu.VMEM((width // 2, width // 2), F32),
             pltpu.VMEM((width // 2, width // 2), F32),
             pltpu.VMEM(square, F32),
@@ -497,13 +565,6 @@
         + [pltpu.VMEM(square, BF16)] * 8,
         compiler_params=params(24 << 20),
     )(*pieces, *rows)
-
-
-def direct(gram, rows, scale):
-    lower = jnp.linalg.cholesky(gram)
-    own_rows = jnp.concatenate(rows, axis=0)
-    basis = jax.scipy.linalg.solve_triangular(lower, own_rows.T, lower=True).T * scale
-    return basis, lower.T / scale
 
 
 def body(tile_values, tile_places, tile_counts, sketch):
@@ -551,11 +612,8 @@
         rows.append(out[0])
         grams.append(out[1])
     mine, theirs = gram_sum(*out[1:])
-    basis, triangle, gram, flag = factor(mine + theirs, rows, scale)
-    return lax.switch(
-        flag[0],
-        (lambda: direct(gram, rows, scale), lambda: (basis, triangle)),
-    )
+    basis, triangle = factor(mine + theirs, rows, scale)
+    return basis, triangle
 
 
 def solution(mesh):

time: 270 us -> 191 us (0.71); the launches traced: 265 us -> 191 us
  other arithmetic: 122 us -> 0.35 us
  Pallas kernels: 42.6 us -> 134 us
  local copies, waits for them, and re-layouts: 19.5 us -> 0 us
  matrix products: 14.6 us -> 0 us
  starting transfers between devices: 21.1 us -> 17.5 us
  loops' own time: 3.5 us -> 0 us
    another operation x16 -> x0, other arithmetic: 118 us -> none  [the longest x14 78.9 us: direct(): lower = jnp.linalg.cholesky(gram)]
    pallas_call x1, Pallas kernels: 27.6 us -> 114 us  [factor(): pl.pallas_call(functools.partial(factor_kernel, len(rows), scale, 6), out...]
    another operation x13 -> x0, matrix products: 14.6 us -> none  [the longest x7 9.11 us: direct(): jax.scipy.linalg.solve_triangular(lower, own_rows.T, lower=True).T * scale]
    another operation x18 -> x0, local copies, waits for them, and re-layouts: 14.3 us -> none
    pallas_call x2, Pallas kernels: 13.1 us -> 18.3 us  [tile_products(): pl.pallas_call(functools.partial(tile_kernel, resident, spans, stride), o...]
    cond x6 -> x0, local copies, waits for them, and re-layouts: 5.13 us -> none  [the longest x2 4.15 us: body(): lax.switch(flag[0], (lambda: direct(gram, rows, scale), lambda: (basis, t...]
    ppermute x16, starting transfers between devices: 11.3 us -> 7.01 us  [swapped(): return lax.ppermute(x, 'col', [(c, c ^ col_flip) for c in range(cols)])]
    another operation x2 -> x0, loops' own time: 3.5 us -> none  [the longest x1 3.44 us: body(): lax.switch(flag[0], (lambda: direct(gram, rows, scale), lambda: (basis, t...]
  transfers between devices with their start and end apart: 23 -> 23, of which waited for: 16 -> 17; matrix products, arithmetic and copies ran while one was open for 0% -> 0% of each run, Pallas kernels for 3% -> 6%
where the time goes in v6:
time: 191 us
  Pallas kernels  134 us (70%)
  waiting for transfers between devices  37.2 us (19%)
  starting transfers between devices  17.5 us (9%)
    pallas_call x1, Pallas kernels, factor(): pl.pallas_call(functools.partial(factor_kernel, len(rows), scale, 6), out...  114 us
    ppermute x16, waiting for transfers between devices, swapped(): return lax.ppermute(x, 'col', [(c, c ^ col_flip) for c in range(cols)])  26.6 us
    pallas_call x2, Pallas kernels, tile_products(): pl.pallas_call(functools.partial(tile_kernel, resident, spans, stride), o...  18.3 us
    ppermute x16, starting transfers between devices, swapped(): return lax.ppermute(x, 'col', [(c, c ^ col_flip) for c in range(cols)])  7.01 us
    ppermute x5, waiting for transfers between devices, swapped(): return lax.ppermute(x, 'row', [(r, r ^ row_flip) for r in range(rows)])  6.57 us
    ppermute x5, starting transfers between devices, swapped(): return lax.ppermute(x, 'row', [(r, r ^ row_flip) for r in range(rows)])  5.54 us
    ppermute x2, starting transfers between devices, swapped(): return lax.ppermute(x, ('row', 'col'), route)  4.95 us
    ppermute x2, waiting for transfers between devices, swapped(): return lax.ppermute(x, ('row', 'col'), route)  4.04 us
  transfers between devices with their start and end apart: 23, of which 17 were waited for; matrix products, arithmetic and copies ran while one was open for 0% of the time, Pallas kernels for 6%

profile of v6, /device:TPU:0, one launch (start us, length us, event | category | flops | bytes accessed | tf_op | source)
XLA Modules:
  0.0 191.0 jit_solution(14089121993542339159)
XLA Ops:
  1.3 8.4 %shard_map.59 = (f32[1,128,512]{2,1,0:T(8,128)S(1)}, f32[4,128,512]{2,1,0:T(8,128)S(1)}, f32[1,128,512]{2,1,0:T(8,128)S(1)}, f32[4,128,512]{2,1,0:T(8,128)S(1)}) custom-call(s32[1,1]{1,0:T(1,128)S(6)} %copy.6.counts, s32[2,360]{1,0:T(2,128)} %bitcast.19, bf16[360,128,128]{2,1,0:T(8,128)(2,1)} %bitcast.15, bf16[48,128,512]{2,1,0:T(8,128)(2,1)} %bitcast.17), custom_call_target="tpu_custom_call" | custom-call | tf_op jit(solution)/shard_map/pallas_call | solution.py:165
  9.7 0.5 collective-permute-start
  10.2 1.2 collective-permute-done
  11.4 0.4 collective-permute-start.1
  11.8 1.7 collective-permute-start.2
  13.5 0.6 collective-permute-done.1
  14.0 0.2 add.52
  14.2 1.7 collective-permute-start.8
  15.9 9.9 %shard_map.60 = (f32[1,128,512]{2,1,0:T(8,128)S(1)}, f32[1,128,512]{2,1,0:T(8,128)S(1)}, f32[4,128,512]{2,1,0:T(8,128)S(1)}, f32[1,128,512]{2,1,0:T(8,128)S(1)},...) custom-call(s32[1,1]{1,0:T(1,128)S(6)} %copy.6.counts, ...), custom_call_target="tpu_custom_call" | custom-call | tf_op jit(solution)/shard_map/pallas_call | solution.py:165
  25.9 0.0 collective-permute-done.2.refs_2_
  25.9 0.1 collective-permute-start.7
  26.0 0.4 collective-permute-start.4
  26.5 0.1 collective-permute-start.6
  26.5 0.4 collective-permute-start.3
  27.0 2.0 %collective-permute-done.4 = f32[1,128,512]{2,1,0:T(8,128)S(1)} collective-permute-done((f32[1,128,512]{2,1,0:T(8,128)S(1)}, f32[1,128,512]{2,1,0:T(8,128)S(1)}, u32[]{:S(2)}, u32[]{:S(2)}) %collective-permute-start.4) | collective-permute-done | bytes 262176 | tf_op jit(solution)/shard_map/ppermute | solution.py:275
  29.0 0.1 collective-permute-start.5
  29.1 0.3 collective-permute-done.6.refs_1_
  29.4 0.4 shard_map.61
  29.8 13.7 %collective-permute-done.8.refs_2_ = f32[4,128,512]{2,1,0:T(8,128)S(1)} collective-permute-done((f32[4,128,512]{2,1,0:T(8,128)S(1)}, f32[4,128,512]{2,1,0:T(8,128)S(1)}, u32[]{:S(2)}, u32[]{:S(2)}) %collective-permute-start.8) | collective-permute-done | bytes 1048608 | tf_op jit(solution)/shard_map/ppermute | solution.py:275
  43.5 0.0 collective-permute-done.7.refs_1_
  43.5 1.1 shard_map.62
  44.5 0.0 collective-permute-done.3.refs_1_
  44.5 3.7 %collective-permute-done.5.refs_2_ = f32[1,128,512]{2,1,0:T(8,128)S(1)} collective-permute-done((f32[1,128,512]{2,1,0:T(8,128)S(1)}, f32[1,128,512]{2,1,0:T(8,128)S(1)}, u32[]{:S(2)}, u32[]{:S(2)}) %collective-permute-start.5) | collective-permute-done | bytes 262176 | tf_op jit(solution)/shard_map/ppermute | solution.py:275
  48.3 0.5 shard_map.63
  48.7 0.1 collective-permute-start.9
  48.8 1.5 collective-permute-done.9
  50.4 3.3 %collective-permute-start.12 = (f32[136,128]{1,0:T(8,128)S(1)}, f32[136,128]{1,0:T(8,128)S(1)}, u32[]{:S(2)}, u32[]{:S(2)}) collective-permute-start(f32[136,128]{1,0:T(8,128)S(1)} %get-tuple-element.62), channel_id=1, source_target_pairs={{0,6},{1,7},{2,4},{3,5},{4,2},{5,3},{6,0},{7,1},{8,14},{9,15},{10,... | collective-permute-start | bytes 208904 | tf_op jit(solution)/shard_map/ppermute | solution.py:283
  53.7 0.3 collective-permute-start.11
  54.0 0.4 collective-permute-start.10
  54.4 1.9 collective-permute-done.12
  56.2 1.8 collective-permute-done.11
  58.0 0.3 collective-permute-done.10
  58.3 3.8 %collective-permute-start.15 = (f32[136,128]{1,0:T(8,128)S(1)}, f32[136,128]{1,0:T(8,128)S(1)}, u32[]{:S(2)}, u32[]{:S(2)}) collective-permute-start(f32[136,128]{1,0:T(8,128)S(1)} %fusion.5), channel_id=1, source_target_pairs={{0,24},{4,28},{8,16},{12,20},{16,8},{20,12},{24,0},{28,4},{1,25},{... | collective-permute-start | bytes 208904 | tf_op jit(solution)/shard_map/ppermute | solution.py:277
  62.1 0.2 collective-permute-start.14
  62.4 0.4 collective-permute-start.13
  62.8 2.1 %collective-permute-done.15 = f32[136,128]{1,0:T(8,128)S(1)} collective-permute-done((f32[136,128]{1,0:T(8,128)S(1)}, f32[136,128]{1,0:T(8,128)S(1)}, u32[]{:S(2)}, u32[]{:S(2)}) %collective-permute-start.15) | collective-permute-done | bytes 69664 | tf_op jit(solution)/shard_map/ppermute | solution.py:277
  64.9 3.3 %collective-permute-done.14 = f32[136,128]{1,0:T(8,128)S(1)} collective-permute-done((f32[136,128]{1,0:T(8,128)S(1)}, f32[136,128]{1,0:T(8,128)S(1)}, u32[]{:S(2)}, u32[]{:S(2)}) %collective-permute-start.14) | collective-permute-done | bytes 69664 | tf_op jit(solution)/shard_map/ppermute | solution.py:277
  68.3 1.6 collective-permute-start.18
  69.9 1.2 collective-permute-start.17
  71.1 0.7 collective-permute-start.16
  71.8 0.0 collective-permute-start.19
  71.8 2.2 %collective-permute-done.18.refs_3_ = f32[136,128]{1,0:T(8,128)S(1)} collective-permute-done((f32[136,128]{1,0:T(8,128)S(1)}, f32[136,128]{1,0:T(8,128)S(1)}, u32[]{:S(2)}, u32[]{:S(2)}) %collective-permute-start.18) | collective-permute-done | bytes 69664 | tf_op jit(solution)/shard_map/ppermute | solution.py:283
  74.0 0.6 collective-permute-done.17.refs_2_
  74.6 0.8 collective-permute-done.16.refs_1_
  75.4 0.0 collective-permute-start.20
  75.4 0.4 collective-permute-done.21.refs_6_
  75.8 0.8 collective-permute-done.20.refs_5_
  76.7 114.1 %shard_map.64 = (f32[768,512]{1,0:T(8,128)}, f32[512,512]{1,0:T(8,128)}) custom-call(f32[136,128]{1,0:T(8,128)S(1)} %add_add_fusion.refs_0_, f32[136,128]{1,0:T(8,128)S(1)} %collective-permute-done.16.refs_1_, f32[136,128]{1,0:T(8,128)S(1)} %collective-permute-done.17.refs_2_, f32[136,128]{1,0:T(8,128)S(1)} %collective-permute-done.18.refs_3_, ...), custom_call_target="tpu_custom_call" | custom-call | tf_op jit(solution)/shard_map/pallas_call | solution.py:547
  (10 shorter events, 0.1 us)
Async XLA Ops:
  9.7 1.7 collective-permute-start
  11.4 2.7 %collective-permute-start.1 = (f32[4,128,512]{2,1,0:T(8,128)S(1)}, f32[4,128,512]{2,1,0:T(8,128)S(1)}, u32[]{:S(2)}, u32[]{:S(2)}) collective-permute-start(f32[4,128,512]{2,1,0:T(8,128)S(1)} %get-tuple-element.36), channel_id=1, source_target_pairs={{0,1},{1,0},{2,3},{3,2},{4,5},{5,4},{6,7},{7,6},{8,9},{9,8},{10,11... | collective-permute-start | bytes 3145736 | tf_op jit(solution)/shard_map/ppermute | solution.py:275
  11.8 14.1 %collective-permute-start.2 = (f32[1,128,512]{2,1,0:T(8,128)S(1)}, f32[1,128,512]{2,1,0:T(8,128)S(1)}, u32[]{:S(2)}, u32[]{:S(2)}) collective-permute-start(f32[1,128,512]{2,1,0:T(8,128)S(1)} %add.51), channel_id=1, source_target_pairs={{0,2},{1,3},{2,0},{3,1},{4,6},{5,7},{6,4},{7,5},{8,10},{9,11},{10,... | collective-permute-start | bytes 786440 | tf_op jit(solution)/shard_map/ppermute | solution.py:275
  14.2 29.2 %collective-permute-start.8 = (f32[4,128,512]{2,1,0:T(8,128)S(1)}, f32[4,128,512]{2,1,0:T(8,128)S(1)}, u32[]{:S(2)}, u32[]{:S(2)}) collective-permute-start(f32[4,128,512]{2,1,0:T(8,128)S(1)} %add.52), channel_id=1, source_target_pairs={{0,2},{1,3},{2,0},{3,1},{4,6},{5,7},{6,4},{7,5},{8,10},{9,11},{10,... | collective-permute-start | bytes 3145736 | tf_op jit(solution)/shard_map/ppermute | solution.py:275
  25.9 17.6 %collective-permute-start.7 = (f32[4,128,512]{2,1,0:T(8,128)S(1)}, f32[4,128,512]{2,1,0:T(8,128)S(1)}, u32[]{:S(2)}, u32[]{:S(2)}) collective-permute-start(f32[4,128,512]{2,1,0:T(8,128)S(1)} %get-tuple-element.55), channel_id=1, source_target_pairs={{0,1},{1,0},{2,3},{3,2},{4,5},{5,4},{6,7},{7,6},{8,9},{9,8},{10,11... | collective-permute-start | bytes 3145736 | tf_op jit(solution)/shard_map/ppermute | solution.py:275
  26.0 3.0 %collective-permute-start.4 = (f32[1,128,512]{2,1,0:T(8,128)S(1)}, f32[1,128,512]{2,1,0:T(8,128)S(1)}, u32[]{:S(2)}, u32[]{:S(2)}) collective-permute-start(f32[1,128,512]{2,1,0:T(8,128)S(1)} %get-tuple-element.49), channel_id=1, source_target_pairs={{0,1},{1,0},{2,3},{3,2},{4,5},{5,4},{6,7},{7,6},{8,9},{9,8},{10,11... | collective-permute-start | bytes 786440 | tf_op jit(solution)/shard_map/ppermute | solution.py:275
  26.5 2.9 %collective-permute-start.6 = (f32[1,128,512]{2,1,0:T(8,128)S(1)}, f32[1,128,512]{2,1,0:T(8,128)S(1)}, u32[]{:S(2)}, u32[]{:S(2)}) collective-permute-start(f32[1,128,512]{2,1,0:T(8,128)S(1)} %get-tuple-element.51), channel_id=1, source_target_pairs={{0,1},{1,0},{2,3},{3,2},{4,5},{5,4},{6,7},{7,6},{8,9},{9,8},{10,11... | collective-permute-start | bytes 786440 | tf_op jit(solution)/shard_map/ppermute | solution.py:275
  26.5 18.0 %collective-permute-start.3 = (f32[1,128,512]{2,1,0:T(8,128)S(1)}, f32[1,128,512]{2,1,0:T(8,128)S(1)}, u32[]{:S(2)}, u32[]{:S(2)}) collective-permute-start(f32[1,128,512]{2,1,0:T(8,128)S(1)} %get-tuple-element.47), channel_id=1, source_target_pairs={{0,1},{1,0},{2,3},{3,2},{4,5},{5,4},{6,7},{7,6},{8,9},{9,8},{10,11... | collective-permute-start | bytes 786440 | tf_op jit(solution)/shard_map/ppermute | solution.py:275
  29.0 19.2 %collective-permute-start.5 = (f32[1,128,512]{2,1,0:T(8,128)S(1)}, f32[1,128,512]{2,1,0:T(8,128)S(1)}, u32[]{:S(2)}, u32[]{:S(2)}) collective-permute-start(f32[1,128,512]{2,1,0:T(8,128)S(1)} %add.53), channel_id=1, source_target_pairs={{0,2},{1,3},{2,0},{3,1},{4,6},{5,7},{6,4},{7,5},{8,10},{9,11},{10,... | collective-permute-start | bytes 786440 | tf_op jit(solution)/shard_map/ppermute | solution.py:275
  48.7 1.6 collective-permute-start.9
  50.4 5.9 %collective-permute-start.12 = (f32[136,128]{1,0:T(8,128)S(1)}, f32[136,128]{1,0:T(8,128)S(1)}, u32[]{:S(2)}, u32[]{:S(2)}) collective-permute-start(f32[136,128]{1,0:T(8,128)S(1)} %get-tuple-element.62), channel_id=1, source_target_pairs={{0,6},{1,7},{2,4},{3,5},{4,2},{5,3},{6,0},{7,1},{8,14},{9,15},{10,... | collective-permute-start | bytes 208904 | tf_op jit(solution)/shard_map/ppermute | solution.py:283
  53.7 4.3 %collective-permute-start.11 = (f32[136,128]{1,0:T(8,128)S(1)}, f32[136,128]{1,0:T(8,128)S(1)}, u32[]{:S(2)}, u32[]{:S(2)}) collective-permute-start(f32[136,128]{1,0:T(8,128)S(1)} %get-tuple-element.63), channel_id=1, source_target_pairs={{0,2},{1,3},{2,0},{3,1},{4,6},{5,7},{6,4},{7,5},{8,10},{9,11},{10,... | collective-permute-start | bytes 208904 | tf_op jit(solution)/shard_map/ppermute | solution.py:275
  54.0 4.3 %collective-permute-start.10 = (f32[136,128]{1,0:T(8,128)S(1)}, f32[136,128]{1,0:T(8,128)S(1)}, u32[]{:S(2)}, u32[]{:S(2)}) collective-permute-start(f32[136,128]{1,0:T(8,128)S(1)} %get-tuple-element.64), channel_id=1, source_target_pairs={{0,4},{4,0},{8,12},{12,8},{16,20},{20,16},{24,28},{28,24},{1,5},{5... | collective-permute-start | bytes 208904 | tf_op jit(solution)/shard_map/ppermute | solution.py:277
  58.3 6.6 %collective-permute-start.15 = (f32[136,128]{1,0:T(8,128)S(1)}, f32[136,128]{1,0:T(8,128)S(1)}, u32[]{:S(2)}, u32[]{:S(2)}) collective-permute-start(f32[136,128]{1,0:T(8,128)S(1)} %fusion.5), channel_id=1, source_target_pairs={{0,24},{4,28},{8,16},{12,20},{16,8},{20,12},{24,0},{28,4},{1,25},{... | collective-permute-start | bytes 208904 | tf_op jit(solution)/shard_map/ppermute | solution.py:277
  62.1 6.1 %collective-permute-start.14 = (f32[136,128]{1,0:T(8,128)S(1)}, f32[136,128]{1,0:T(8,128)S(1)}, u32[]{:S(2)}, u32[]{:S(2)}) collective-permute-start(f32[136,128]{1,0:T(8,128)S(1)} %fusion.5), channel_id=1, source_target_pairs={{0,16},{4,20},{8,24},{12,28},{16,0},{20,4},{24,8},{28,12},{1,17},{... | collective-permute-start | bytes 208904 | tf_op jit(solution)/shard_map/ppermute | solution.py:277
  62.4 5.9 %collective-permute-start.13 = (f32[136,128]{1,0:T(8,128)S(1)}, f32[136,128]{1,0:T(8,128)S(1)}, u32[]{:S(2)}, u32[]{:S(2)}) collective-permute-start(f32[136,128]{1,0:T(8,128)S(1)} %fusion.5), channel_id=1, source_target_pairs={{0,8},{4,12},{8,0},{12,4},{16,24},{20,28},{24,16},{28,20},{1,9},{5... | collective-permute-start | bytes 208904 | tf_op jit(solution)/shard_map/ppermute | solution.py:277
  68.3 5.7 %collective-permute-start.18 = (f32[136,128]{1,0:T(8,128)S(1)}, f32[136,128]{1,0:T(8,128)S(1)}, u32[]{:S(2)}, u32[]{:S(2)}) collective-permute-start(f32[136,128]{1,0:T(8,128)S(1)} %add_add_fusion.refs_0_), channel_id=1, source_target_pairs={{0,6},{1,7},{2,4},{3,5},{4,2},{5,3},{6,0},{7,1},{8,14},{9,15},{10,... | collective-permute-start | bytes 208904 | tf_op jit(solution)/shard_map/ppermute | solution.py:283
  69.9 4.7 %collective-permute-start.17 = (f32[136,128]{1,0:T(8,128)S(1)}, f32[136,128]{1,0:T(8,128)S(1)}, u32[]{:S(2)}, u32[]{:S(2)}) collective-permute-start(f32[136,128]{1,0:T(8,128)S(1)} %add_add_fusion.refs_0_), channel_id=1, source_target_pairs={{0,2},{1,3},{2,0},{3,1},{4,6},{5,7},{6,4},{7,5},{8,10},{9,11},{10,... | collective-permute-start | bytes 208904 | tf_op jit(solution)/shard_map/ppermute | solution.py:275
  71.1 4.3 %collective-permute-start.16 = (f32[136,128]{1,0:T(8,128)S(1)}, f32[136,128]{1,0:T(8,128)S(1)}, u32[]{:S(2)}, u32[]{:S(2)}) collective-permute-start(f32[136,128]{1,0:T(8,128)S(1)} %add_add_fusion.refs_0_), channel_id=1, source_target_pairs={{0,4},{4,0},{8,12},{12,8},{16,20},{20,16},{24,28},{28,24},{1,5},{5... | collective-permute-start | bytes 208904 | tf_op jit(solution)/shard_map/ppermute | solution.py:277
  71.8 3.6 %collective-permute-start.19 = (f32[136,128]{1,0:T(8,128)S(1)}, f32[136,128]{1,0:T(8,128)S(1)}, u32[]{:S(2)}, u32[]{:S(2)}) collective-permute-start(f32[136,128]{1,0:T(8,128)S(1)} %add_add_fusion.refs_0_), channel_id=1, source_target_pairs={{0,1},{1,0},{2,3},{3,2},{4,5},{5,4},{6,7},{7,6},{8,9},{9,8},{10,11... | collective-permute-start | bytes 208904 | tf_op jit(solution)/shard_map/ppermute | solution.py:275
  74.0 1.4 collective-permute-start.22
  74.6 1.3 collective-permute-start.21
  75.4 1.3 collective-permute-start.20

commit v7 on v6

--- a/solution.py
+++ b/solution.py
@@ -11,7 +11,7 @@
 BF16 = jnp.bfloat16
 F32 = jnp.float32
 PAIR = 2
-TURN = 16
+TURN = 20
 PARTS = 2
 BLOCK = 128
 SMALL = 0.01
@@ -35,7 +35,7 @@
 def tile_kernel(resident, spans, stride, counts, places, tiles, panels, *refs):
     outs, refs = refs[: 2 * len(spans)], refs[2 * len(spans) :]
     tile_buf, panel_buf, place_of, key, first_of, key_of, acc, load_sem, panel_sem = refs[:9]
-    fill, entry = refs[9 : 9 + PARTS], refs[9 + PARTS :]
+    fill, entry = refs[9:-1], refs[-1]
     slots = tiles.shape[0]
     blocks = acc.shape[0]
     per_owner = key.shape[0] // lax.axis_size("col")
@@ -62,9 +62,10 @@
         for inside in range(per_owner):
             name = [base + heads[f, inside] if (f, inside) in heads else blocks for f in (0, 1)]
             key[owner * per_owner + inside] = jnp.where(flipped, name[1], name[0])
+    base = [n * (blocks * stride + cuts[1]) for n in range(PARTS + 1)]
     for n in range(PARTS):
         for k in range(blocks + 1):
-            fill[n][k] = k * stride
+            fill[n][k] = base[n] + k * stride
     place_load.wait()
     live = counts[0, 0]
     shift = panels.shape[0].bit_length()
@@ -82,42 +83,42 @@
             spots = [fill[n][k] for n, k in enumerate(lists)]
             for n in range(PARTS):
                 fill[n][lists[n]] = spots[n] + 1
-                entry[n][spots[n]] = made[n]
+                entry[spots[n]] = made[n]
         return carry
 
     lax.fori_loop(0, (jnp.minimum(live, cuts[1]) + unroll - 1) // unroll, put, 0)
 
-    empty = blocks * stride + cuts[1]
+    for i in range(PAIR):
+        entry[base[-1] + i] = slots << shift
     number, bounds = 0, [0]
     for n in range(PARTS):
-        for i in range(PAIR):
-            entry[n][empty + i] = slots << shift
         for k in range(blocks):
-            size = fill[n][k] - k * stride
+            head = base[n] + k * stride
+            end = fill[n][k]
             for i in range(PAIR - 1):
-                entry[n][fill[n][k] + i] = slots << shift
-
-            def add_pair(j, at, k=k):
-                first_of[at + j] = k * stride + j * PAIR
+                entry[end + i] = slots << shift
+
+            def add_pair(j, at, head=head, k=k):
+                first_of[at + j] = head + j * PAIR
                 key_of[at + j] = k
                 return at
 
-            pairs = (size + PAIR - 1) // PAIR
+            pairs = (end - head + PAIR - 1) // PAIR
             lax.fori_loop(0, pairs, add_pair, number)
             number += pairs
-        for i in range(TURN - 1):
-            first_of[number + i] = empty
-            key_of[number + i] = 0
-        number = (number + TURN - 1) // TURN * TURN
         bounds.append(number // TURN)
+    for i in range(TURN - 1):
+        first_of[number + i] = base[-1]
+        key_of[number + i] = 0
+    bounds[-1] = (number + TURN - 1) // TURN
     acc[...] = jnp.zeros_like(acc)
     tile_buf[slots] = jnp.zeros_like(tile_buf[slots])
     for load in panel_loads:
         load.wait()
 
-    def turn(n, g, carry):
+    def turn(g, carry):
         firsts = [first_of[g * TURN + i] for i in range(TURN)]
-        entries = [[entry[n][at + j] for j in range(PAIR)] for at in firsts]
+        entries = [[entry[at + j] for j in range(PAIR)] for at in firsts]
         slot = [[e >> shift for e in pair] for pair in entries]
         column = [[e & ((1 << shift) - 1) for e in pair] for pair in entries]
         if not resident:
@@ -145,7 +146,7 @@
 
     for n, load in enumerate(tile_loads):
         load.wait()
-        lax.fori_loop(bounds[n], bounds[n + 1], functools.partial(turn, n), 0)
+        lax.fori_loop(bounds[n], bounds[n + 1], turn, 0)
     first = 0
     for out in outs:
         out[...] = acc[first : first + out.shape[0]]
@@ -159,7 +160,7 @@
     blocks = sum(sizes)
     part = -(-slots // PARTS)
     stride = (min(part, panels.shape[0]) // PAIR + 1) * PAIR
-    pairs = PARTS * blocks * stride // PAIR + TURN * (PARTS + 1)
+    pairs = PARTS * blocks * stride // PAIR + TURN
     resident = panels.size * 2 <= 16 << 20
     panel_shape = (panels.shape[0] if resident else PAIR * TURN, size, width)
     return pl.pallas_call(
@@ -179,7 +180,7 @@
             pltpu.SemaphoreType.DMA((1 if resident else PAIR * TURN,)),
         ]
         + [pltpu.SMEM((blocks + 1,), jnp.int32)] * PARTS
-        + [pltpu.SMEM((blocks * stride + part + PAIR,), jnp.int32)] * PARTS,
+        + [pltpu.SMEM((PARTS * (blocks * stride + part) + PAIR,), jnp.int32)],
         compiler_params=params(50 << 20),
     )(counts, in_hbm(places), tiles, panels)
 
@@ -374,8 +375,7 @@
     c = lax.broadcasted_iota(jnp.int32, (wide, wide), 1)
     half_mask[...] = jnp.where(r > c, 1.0, jnp.where(r == c, 0.5, 0.0))
     half_eye[...] = jnp.where(r == c, 0.5, 0.0)
-    for ref in (ph, dh, dl):
-        ref[top, low] = jnp.zeros((wide, wide), BF16)
+    ph[top, low] = jnp.zeros((wide, wide), BF16)
 
     def dot(left, right):
         return jnp.dot(left, right, preferred_element_type=F32)
@@ -410,21 +410,15 @@
             if exact:
                 norm = norm + jnp.sum(p * p, keepdims=True)
         for p, part, k in zip(strips, (top, low), (wide, size)):
-            square = dot(ph[part, :k], ph[:k, :k])
-            cross = dot_rows(ph[part, :k], ph[:k, :k])
-            corner = cross[:, k - wide :] * half_mask[...]
-            cross = corner if k == wide else both(cross[:, :wide], corner)
-            d = p - square - cross
-            if exact:
-                dh[part, :k], dl[part, :k] = halves(d)
-            else:
-                dh[part, :k] = d.astype(BF16)
-        for part, k in ((top, wide), (low, size)):
-            if exact:
-                change = dot(both(dh[part, :k], dl[part, :k]), twice(wb[:k, :k], 0))
-            else:
-                change = dot(dh[part, :k], wb[:k, :k])
-            w[part, :k] = wb[part, :k].astype(F32) - change
+            corner = dot_rows(ph[part, :k], ph[part, :k]) * half_mask[...]
+            corner = p[:, k - wide :] - dot(ph[part, part], ph[part, part]) - corner
+            dh[part, part] = corner.astype(BF16)
+            if k == size:
+                side = dot(ph[low, :], ph[:, top]) + dot_rows(ph[low, top], ph[top, top])
+                dh[low, top] = (p[:, :wide] - side).astype(BF16)
+        for part in (top, low):
+            w[part, part] = wb[part, part].astype(F32) - dot(dh[part, part], wb[part, part])
+        w[low, top] = wb[low, top].astype(F32) - dot(dh[low, :], wb[:, top])
         return jnp.sum(norm)
 
     def rounded():
@@ -442,34 +436,37 @@
         return state[0] + 1, step(True)
 
     _, norm = lax.while_loop(not_done, again, (jnp.int32(0), jnp.float32(1.0)))
-    triangle_copy = pltpu.make_async_copy(triangle, triangle_out, out_sem.at[0])
     found = norm < SMALL
 
     @pl.when(found)
     def _():
         for part, k in ((top, wide), (low, size)):
             wb[part, :k], dl[part, :k] = halves(w[part, :k])
-        for part, k in ((top, wide), (low, size)):
-            upper = times((wb[part, :k], dl[part, :k]), (gh[:k, k - wide :], gl[:k, k - wide :]))
-            corner = jnp.where(r <= c, upper[:, :wide], 0.0)
-            upper = both(corner, upper[:, wide:]) if k == wide else corner
-            triangle[part, k - wide :] = upper * (1.0 / scale)
-        triangle[low, top] = jnp.zeros((wide, wide), F32)
-        triangle_copy.start()
-        copies = [triangle_copy]
-        first = 0
-        for part in rows:
-            for head in range(0, part.shape[0], wide):
-                count = min(wide, part.shape[0] - head)
-                sh, sl = halves(part[head : head + count])
-                here = pl.ds(first, count)
-                for cols, k in ((top, wide), (low, size)):
-                    out = against((sh[:, :k], sl[:, :k]), (wb[cols, :k], dl[cols, :k]))
-                    basis[here, cols] = out * scale
-                sem = out_sem.at[len(copies)]
-                copies.append(pltpu.make_async_copy(basis.at[here], basis_out.at[here], sem))
-                copies[-1].start()
-                first += count
+        copies = []
+
+        def send(source, target):
+            copies.append(pltpu.make_async_copy(source, target, out_sem.at[len(copies)]))
+            copies[-1].start()
+
+        own_rows = jnp.concatenate([part[...] for part in rows], axis=0)
+        count = own_rows.shape[0] // 2
+        for n in range(2):
+            here = pl.ds(n * count, count)
+            sh, sl = halves(own_rows[n * count : (n + 1) * count])
+            for cols, k in ((low, size), (top, wide)):
+                out = against((sh[:, :k], sl[:, :k]), (wb[cols, :k], dl[cols, :k]))
+                basis[here, cols] = out * scale
+                send(basis.at[here, cols], basis_out.at[here, cols])
+            if n == 1:
+                for part, k in ((top, wide), (low, size)):
+                    upper = times(
+                        (wb[part, :k], dl[part, :k]), (gh[:k, k - wide :], gl[:k, k - wide :])
+                    )
+                    corner = jnp.where(r <= c, upper[:, :wide], 0.0)
+                    upper = both(corner, upper[:, wide:]) if k == wide else corner
+                    triangle[part, k - wide :] = upper * (1.0 / scale)
+                triangle[low, top] = jnp.zeros((wide, wide), F32)
+                send(triangle, triangle_out)
         for copy in copies:
             copy.wait()
 
@@ -489,11 +486,14 @@
 
             lax.fori_loop(0, part.shape[0] // BLOCK, strip, 0)
             first += part.shape[0]
-        basis_copy = pltpu.make_async_copy(basis, basis_out, out_sem.at[1])
-        triangle_copy.start()
-        basis_copy.start()
-        triangle_copy.wait()
-        basis_copy.wait()
+        copies = [
+            pltpu.make_async_copy(triangle, triangle_out, out_sem.at[0]),
+            pltpu.make_async_copy(basis, basis_out, out_sem.at[1]),
+        ]
+        for copy in copies:
+            copy.start()
+        for copy in copies:
+            copy.wait()
 
 
 def exact_dot(left, right, dims):
@@ -560,7 +560,7 @@
             pltpu.VMEM(square, F32),
             pltpu.VMEM((local, width), F32),
             pltpu.VMEM(square, F32),
-            pltpu.SemaphoreType.DMA((1 + sum(-(-part.shape[0] * 2 // width) for part in rows),)),
+            pltpu.SemaphoreType.DMA((5,)),
         ]
         + [pltpu.VMEM(square, BF16)] * 8,
         compiler_params=params(24 << 20),
@@ -603,7 +603,7 @@
     places, own = lax.optimization_barrier((places, own))
     send, keep = products([(1, *chunk) for chunk in late] + [(0, *chunk) for chunk in chunks])
     send, keep, across[0] = lax.optimization_barrier((send, keep, across[0]))
-    across += [swapped(x, 0, 2) for x in across_cores(send[: len(late)], keep[: len(late)])]
+    across += [swapped(x, 0, 2) for x in across_cores(list(send[: len(late)]), keep[: len(late)])]
     send, keep = send[len(late) :], keep[len(late) :]
     chunks = len(chunks)
     rows, grams = [], []

time: 191 us -> 191 us (level)
  Pallas kernels: 134 us -> 130 us
  starting transfers between devices: 17.5 us -> 20.8 us
    pallas_call x2, Pallas kernels: 18.3 us -> 14.8 us  [tile_products(): pl.pallas_call(functools.partial(tile_kernel, resident, spans, stride), o...]
  transfers between devices with their start and end apart: 23 -> 23, of which waited for: 17 -> 18; matrix products, arithmetic and copies ran while one was open for 0% -> 0% of each run, Pallas kernels for 6% -> 5%
where the time goes in v7:
time: 191 us
  Pallas kernels  130 us (68%)
  waiting for transfers between devices  37.5 us (20%)
  starting transfers between devices  20.8 us (11%)
    pallas_call x1, Pallas kernels, factor(): pl.pallas_call(functools.partial(factor_kernel, len(rows), scale, 6), out...  114 us
    ppermute x16, waiting for transfers between devices, swapped(): return lax.ppermute(x, 'col', [(c, c ^ col_flip) for c in range(cols)])  28.3 us
    pallas_call x2, Pallas kernels, tile_products(): pl.pallas_call(functools.partial(tile_kernel, resident, spans, stride), o...  14.8 us
    ppermute x16, starting transfers between devices, swapped(): return lax.ppermute(x, 'col', [(c, c ^ col_flip) for c in range(cols)])  8.84 us
    ppermute x5, starting transfers between devices, swapped(): return lax.ppermute(x, 'row', [(r, r ^ row_flip) for r in range(rows)])  7.3 us
    ppermute x5, waiting for transfers between devices, swapped(): return lax.ppermute(x, 'row', [(r, r ^ row_flip) for r in range(rows)])  5.56 us
    ppermute x2, starting transfers between devices, swapped(): return lax.ppermute(x, ('row', 'col'), route)  4.61 us
  transfers between devices with their start and end apart: 23, of which 18 were waited for; matrix products, arithmetic and copies ran while one was open for 0% of the time, Pallas kernels for 5%

profile of v7, /device:TPU:0, one launch (start us, length us, event | category | flops | bytes accessed | tf_op | source)
XLA Modules:
  0.0 190.6 jit_solution(15041285590370825827)
XLA Ops:
  1.3 7.3 %shard_map.59 = (f32[1,128,512]{2,1,0:T(8,128)S(1)}, f32[4,128,512]{2,1,0:T(8,128)S(1)}, f32[1,128,512]{2,1,0:T(8,128)S(1)}, f32[4,128,512]{2,1,0:T(8,128)S(1)}) custom-call(s32[1,1]{1,0:T(1,128)S(6)} %copy.6.counts, s32[2,360]{1,0:T(2,128)} %bitcast.19, bf16[360,128,128]{2,1,0:T(8,128)(2,1)} %bitcast.15, bf16[48,128,512]{2,1,0:T(8,128)(2,1)} %bitcast.17), custom_call_target="tpu_custom_call" | custom-call | tf_op jit(solution)/shard_map/pallas_call | solution.py:166
  8.6 0.5 collective-permute-start
  9.1 1.2 collective-permute-done
  10.2 0.4 collective-permute-start.1
  10.6 2.7 %collective-permute-start.2 = (f32[1,128,512]{2,1,0:T(8,128)S(1)}, f32[1,128,512]{2,1,0:T(8,128)S(1)}, u32[]{:S(2)}, u32[]{:S(2)}) collective-permute-start(f32[1,128,512]{2,1,0:T(8,128)S(1)} %add.51), channel_id=1, source_target_pairs={{0,2},{1,3},{2,0},{3,1},{4,6},{5,7},{6,4},{7,5},{8,10},{9,11},{10,... | collective-permute-start | bytes 786440 | tf_op jit(solution)/shard_map/ppermute | solution.py:276
  13.4 0.0 collective-permute-done.1
  13.4 0.2 add.52
  13.6 2.5 %collective-permute-start.8 = (f32[4,128,512]{2,1,0:T(8,128)S(1)}, f32[4,128,512]{2,1,0:T(8,128)S(1)}, u32[]{:S(2)}, u32[]{:S(2)}) collective-permute-start(f32[4,128,512]{2,1,0:T(8,128)S(1)} %add.52), channel_id=1, source_target_pairs={{0,2},{1,3},{2,0},{3,1},{4,6},{5,7},{6,4},{7,5},{8,10},{9,11},{10,... | collective-permute-start | bytes 3145736 | tf_op jit(solution)/shard_map/ppermute | solution.py:276
  16.1 7.5 %shard_map.60 = (f32[1,128,512]{2,1,0:T(8,128)S(1)}, f32[1,128,512]{2,1,0:T(8,128)S(1)}, f32[4,128,512]{2,1,0:T(8,128)S(1)}, f32[1,128,512]{2,1,0:T(8,128)S(1)},...) custom-call(s32[1,1]{1,0:T(1,128)S(6)} %copy.6.counts, ...), custom_call_target="tpu_custom_call" | custom-call | tf_op jit(solution)/shard_map/pallas_call | solution.py:166
  23.6 0.0 collective-permute-done.2.refs_2_
  23.6 0.1 collective-permute-start.7
  23.7 0.5 collective-permute-start.4
  24.2 0.1 collective-permute-start.6
  24.2 0.4 collective-permute-start.3
  24.7 2.0 %collective-permute-done.4 = f32[1,128,512]{2,1,0:T(8,128)S(1)} collective-permute-done((f32[1,128,512]{2,1,0:T(8,128)S(1)}, f32[1,128,512]{2,1,0:T(8,128)S(1)}, u32[]{:S(2)}, u32[]{:S(2)}) %collective-permute-start.4) | collective-permute-done | bytes 262176 | tf_op jit(solution)/shard_map/ppermute | solution.py:276
  26.7 0.1 collective-permute-start.5
  26.8 0.2 collective-permute-done.6.refs_1_
  27.1 0.4 shard_map.61
  27.5 15.5 %collective-permute-done.8.refs_2_ = f32[4,128,512]{2,1,0:T(8,128)S(1)} collective-permute-done((f32[4,128,512]{2,1,0:T(8,128)S(1)}, f32[4,128,512]{2,1,0:T(8,128)S(1)}, u32[]{:S(2)}, u32[]{:S(2)}) %collective-permute-start.8) | collective-permute-done | bytes 1048608 | tf_op jit(solution)/shard_map/ppermute | solution.py:276
  43.0 1.1 shard_map.62
  44.1 0.0 collective-permute-done.3.refs_1_
  44.1 4.2 %collective-permute-done.5.refs_2_ = f32[1,128,512]{2,1,0:T(8,128)S(1)} collective-permute-done((f32[1,128,512]{2,1,0:T(8,128)S(1)}, f32[1,128,512]{2,1,0:T(8,128)S(1)}, u32[]{:S(2)}, u32[]{:S(2)}) %collective-permute-start.5) | collective-permute-done | bytes 262176 | tf_op jit(solution)/shard_map/ppermute | solution.py:276
  48.3 0.5 shard_map.63
  48.8 0.1 collective-permute-start.9
  48.8 1.5 collective-permute-done.9
  50.4 3.6 %collective-permute-start.12 = (f32[136,128]{1,0:T(8,128)S(1)}, f32[136,128]{1,0:T(8,128)S(1)}, u32[]{:S(2)}, u32[]{:S(2)}) collective-permute-start(f32[136,128]{1,0:T(8,128)S(1)} %get-tuple-element.62), channel_id=1, source_target_pairs={{0,6},{1,7},{2,4},{3,5},{4,2},{5,3},{6,0},{7,1},{8,14},{9,15},{10,... | collective-permute-start | bytes 208904 | tf_op jit(solution)/shard_map/ppermute | solution.py:284
  54.0 0.3 collective-permute-start.11
  54.3 0.4 collective-permute-start.10
  54.7 1.9 collective-permute-done.12
  56.5 1.8 collective-permute-done.11
  58.3 0.3 collective-permute-done.10
  58.6 4.8 %collective-permute-start.15 = (f32[136,128]{1,0:T(8,128)S(1)}, f32[136,128]{1,0:T(8,128)S(1)}, u32[]{:S(2)}, u32[]{:S(2)}) collective-permute-start(f32[136,128]{1,0:T(8,128)S(1)} %fusion.5), channel_id=1, source_target_pairs={{0,24},{4,28},{8,16},{12,20},{16,8},{20,12},{24,0},{28,4},{1,25},{... | collective-permute-start | bytes 208904 | tf_op jit(solution)/shard_map/ppermute | solution.py:278
  63.5 0.0 collective-permute-start.14
  63.5 0.6 collective-permute-start.13
  64.1 1.8 collective-permute-done.15
  65.9 2.8 %collective-permute-done.14 = f32[136,128]{1,0:T(8,128)S(1)} collective-permute-done((f32[136,128]{1,0:T(8,128)S(1)}, f32[136,128]{1,0:T(8,128)S(1)}, u32[]{:S(2)}, u32[]{:S(2)}) %collective-permute-start.14) | collective-permute-done | bytes 69664 | tf_op jit(solution)/shard_map/ppermute | solution.py:278
  68.7 0.3 collective-permute-done.13
  69.0 1.0 collective-permute-start.18
  70.0 1.1 collective-permute-start.17
  71.1 1.5 collective-permute-start.16
  72.6 1.8 collective-permute-done.18.refs_3_
  74.4 0.7 collective-permute-done.17.refs_2_
  75.1 0.4 collective-permute-done.16.refs_1_
  75.4 0.1 collective-permute-start.20
  75.6 0.1 collective-permute-done.22.refs_7_
  75.7 0.7 collective-permute-done.21.refs_6_
  76.3 0.4 collective-permute-done.20.refs_5_
  76.7 113.7 %shard_map.64 = (f32[768,512]{1,0:T(8,128)}, f32[512,512]{1,0:T(8,128)}) custom-call(f32[136,128]{1,0:T(8,128)S(1)} %add_add_fusion.refs_0_, f32[136,128]{1,0:T(8,128)S(1)} %collective-permute-done.16.refs_1_, f32[136,128]{1,0:T(8,128)S(1)} %collective-permute-done.17.refs_2_, f32[136,128]{1,0:T(8,128)S(1)} %collective-permute-done.18.refs_3_, ...), custom_call_target="tpu_custom_call" | custom-call | tf_op jit(solution)/shard_map/pallas_call | solution.py:547
  (10 shorter events, 0.1 us)
Async XLA Ops:
  8.6 1.7 collective-permute-start
  10.2 3.1 %collective-permute-start.1 = (f32[4,128,512]{2,1,0:T(8,128)S(1)}, f32[4,128,512]{2,1,0:T(8,128)S(1)}, u32[]{:S(2)}, u32[]{:S(2)}) collective-permute-start(f32[4,128,512]{2,1,0:T(8,128)S(1)} %get-tuple-element.36), channel_id=1, source_target_pairs={{0,1},{1,0},{2,3},{3,2},{4,5},{5,4},{6,7},{7,6},{8,9},{9,8},{10,11... | collective-permute-start | bytes 3145736 | tf_op jit(solution)/shard_map/ppermute | solution.py:276
  10.6 12.9 %collective-permute-start.2 = (f32[1,128,512]{2,1,0:T(8,128)S(1)}, f32[1,128,512]{2,1,0:T(8,128)S(1)}, u32[]{:S(2)}, u32[]{:S(2)}) collective-permute-start(f32[1,128,512]{2,1,0:T(8,128)S(1)} %add.51), channel_id=1, source_target_pairs={{0,2},{1,3},{2,0},{3,1},{4,6},{5,7},{6,4},{7,5},{8,10},{9,11},{10,... | collective-permute-start | bytes 786440 | tf_op jit(solution)/shard_map/ppermute | solution.py:276
  13.6 29.4 %collective-permute-start.8 = (f32[4,128,512]{2,1,0:T(8,128)S(1)}, f32[4,128,512]{2,1,0:T(8,128)S(1)}, u32[]{:S(2)}, u32[]{:S(2)}) collective-permute-start(f32[4,128,512]{2,1,0:T(8,128)S(1)} %add.52), channel_id=1, source_target_pairs={{0,2},{1,3},{2,0},{3,1},{4,6},{5,7},{6,4},{7,5},{8,10},{9,11},{10,... | collective-permute-start | bytes 3145736 | tf_op jit(solution)/shard_map/ppermute | solution.py:276
  23.6 19.4 %collective-permute-start.7 = (f32[4,128,512]{2,1,0:T(8,128)S(1)}, f32[4,128,512]{2,1,0:T(8,128)S(1)}, u32[]{:S(2)}, u32[]{:S(2)}) collective-permute-start(f32[4,128,512]{2,1,0:T(8,128)S(1)} %get-tuple-element.55), channel_id=1, source_target_pairs={{0,1},{1,0},{2,3},{3,2},{4,5},{5,4},{6,7},{7,6},{8,9},{9,8},{10,11... | collective-permute-start | bytes 3145736 | tf_op jit(solution)/shard_map/ppermute | solution.py:276
  23.7 3.0 %collective-permute-start.4 = (f32[1,128,512]{2,1,0:T(8,128)S(1)}, f32[1,128,512]{2,1,0:T(8,128)S(1)}, u32[]{:S(2)}, u32[]{:S(2)}) collective-permute-start(f32[1,128,512]{2,1,0:T(8,128)S(1)} %get-tuple-element.49), channel_id=1, source_target_pairs={{0,1},{1,0},{2,3},{3,2},{4,5},{5,4},{6,7},{7,6},{8,9},{9,8},{10,11... | collective-permute-start | bytes 786440 | tf_op jit(solution)/shard_map/ppermute | solution.py:276
  24.2 2.9 %collective-permute-start.6 = (f32[1,128,512]{2,1,0:T(8,128)S(1)}, f32[1,128,512]{2,1,0:T(8,128)S(1)}, u32[]{:S(2)}, u32[]{:S(2)}) collective-permute-start(f32[1,128,512]{2,1,0:T(8,128)S(1)} %get-tuple-element.51), channel_id=1, source_target_pairs={{0,1},{1,0},{2,3},{3,2},{4,5},{5,4},{6,7},{7,6},{8,9},{9,8},{10,11... | collective-permute-start | bytes 786440 | tf_op jit(solution)/shard_map/ppermute | solution.py:276
  24.2 19.8 %collective-permute-start.3 = (f32[1,128,512]{2,1,0:T(8,128)S(1)}, f32[1,128,512]{2,1,0:T(8,128)S(1)}, u32[]{:S(2)}, u32[]{:S(2)}) collective-permute-start(f32[1,128,512]{2,1,0:T(8,128)S(1)} %get-tuple-element.47), channel_id=1, source_target_pairs={{0,1},{1,0},{2,3},{3,2},{4,5},{5,4},{6,7},{7,6},{8,9},{9,8},{10,11... | collective-permute-start | bytes 786440 | tf_op jit(solution)/shard_map/ppermute | solution.py:276
  26.7 21.6 %collective-permute-start.5 = (f32[1,128,512]{2,1,0:T(8,128)S(1)}, f32[1,128,512]{2,1,0:T(8,128)S(1)}, u32[]{:S(2)}, u32[]{:S(2)}) collective-permute-start(f32[1,128,512]{2,1,0:T(8,128)S(1)} %add.53), channel_id=1, source_target_pairs={{0,2},{1,3},{2,0},{3,1},{4,6},{5,7},{6,4},{7,5},{8,10},{9,11},{10,... | collective-permute-start | bytes 786440 | tf_op jit(solution)/shard_map/ppermute | solution.py:276
  48.8 1.6 collective-permute-start.9
  50.4 6.1 %collective-permute-start.12 = (f32[136,128]{1,0:T(8,128)S(1)}, f32[136,128]{1,0:T(8,128)S(1)}, u32[]{:S(2)}, u32[]{:S(2)}) collective-permute-start(f32[136,128]{1,0:T(8,128)S(1)} %get-tuple-element.62), channel_id=1, source_target_pairs={{0,6},{1,7},{2,4},{3,5},{4,2},{5,3},{6,0},{7,1},{8,14},{9,15},{10,... | collective-permute-start | bytes 208904 | tf_op jit(solution)/shard_map/ppermute | solution.py:284
  54.0 4.3 %collective-permute-start.11 = (f32[136,128]{1,0:T(8,128)S(1)}, f32[136,128]{1,0:T(8,128)S(1)}, u32[]{:S(2)}, u32[]{:S(2)}) collective-permute-start(f32[136,128]{1,0:T(8,128)S(1)} %get-tuple-element.63), channel_id=1, source_target_pairs={{0,2},{1,3},{2,0},{3,1},{4,6},{5,7},{6,4},{7,5},{8,10},{9,11},{10,... | collective-permute-start | bytes 208904 | tf_op jit(solution)/shard_map/ppermute | solution.py:276
  54.3 4.3 %collective-permute-start.10 = (f32[136,128]{1,0:T(8,128)S(1)}, f32[136,128]{1,0:T(8,128)S(1)}, u32[]{:S(2)}, u32[]{:S(2)}) collective-permute-start(f32[136,128]{1,0:T(8,128)S(1)} %get-tuple-element.64), channel_id=1, source_target_pairs={{0,4},{4,0},{8,12},{12,8},{16,20},{20,16},{24,28},{28,24},{1,5},{5... | collective-permute-start | bytes 208904 | tf_op jit(solution)/shard_map/ppermute | solution.py:278
  58.6 7.3 %collective-permute-start.15 = (f32[136,128]{1,0:T(8,128)S(1)}, f32[136,128]{1,0:T(8,128)S(1)}, u32[]{:S(2)}, u32[]{:S(2)}) collective-permute-start(f32[136,128]{1,0:T(8,128)S(1)} %fusion.5), channel_id=1, source_target_pairs={{0,24},{4,28},{8,16},{12,20},{16,8},{20,12},{24,0},{28,4},{1,25},{... | collective-permute-start | bytes 208904 | tf_op jit(solution)/shard_map/ppermute | solution.py:278
  63.5 5.3 %collective-permute-start.14 = (f32[136,128]{1,0:T(8,128)S(1)}, f32[136,128]{1,0:T(8,128)S(1)}, u32[]{:S(2)}, u32[]{:S(2)}) collective-permute-start(f32[136,128]{1,0:T(8,128)S(1)} %fusion.5), channel_id=1, source_target_pairs={{0,16},{4,20},{8,24},{12,28},{16,0},{20,4},{24,8},{28,12},{1,17},{... | collective-permute-start | bytes 208904 | tf_op jit(solution)/shard_map/ppermute | solution.py:278
  63.5 5.5 %collective-permute-start.13 = (f32[136,128]{1,0:T(8,128)S(1)}, f32[136,128]{1,0:T(8,128)S(1)}, u32[]{:S(2)}, u32[]{:S(2)}) collective-permute-start(f32[136,128]{1,0:T(8,128)S(1)} %fusion.5), channel_id=1, source_target_pairs={{0,8},{4,12},{8,0},{12,4},{16,24},{20,28},{24,16},{28,20},{1,9},{5... | collective-permute-start | bytes 208904 | tf_op jit(solution)/shard_map/ppermute | solution.py:278
  69.0 5.4 %collective-permute-start.18 = (f32[136,128]{1,0:T(8,128)S(1)}, f32[136,128]{1,0:T(8,128)S(1)}, u32[]{:S(2)}, u32[]{:S(2)}) collective-permute-start(f32[136,128]{1,0:T(8,128)S(1)} %add_add_fusion.refs_0_), channel_id=1, source_target_pairs={{0,6},{1,7},{2,4},{3,5},{4,2},{5,3},{6,0},{7,1},{8,14},{9,15},{10,... | collective-permute-start | bytes 208904 | tf_op jit(solution)/shard_map/ppermute | solution.py:284
  70.0 5.0 %collective-permute-start.17 = (f32[136,128]{1,0:T(8,128)S(1)}, f32[136,128]{1,0:T(8,128)S(1)}, u32[]{:S(2)}, u32[]{:S(2)}) collective-permute-start(f32[136,128]{1,0:T(8,128)S(1)} %add_add_fusion.refs_0_), channel_id=1, source_target_pairs={{0,2},{1,3},{2,0},{3,1},{4,6},{5,7},{6,4},{7,5},{8,10},{9,11},{10,... | collective-permute-start | bytes 208904 | tf_op jit(solution)/shard_map/ppermute | solution.py:276
  71.1 4.3 %collective-permute-start.16 = (f32[136,128]{1,0:T(8,128)S(1)}, f32[136,128]{1,0:T(8,128)S(1)}, u32[]{:S(2)}, u32[]{:S(2)}) collective-permute-start(f32[136,128]{1,0:T(8,128)S(1)} %add_add_fusion.refs_0_), channel_id=1, source_target_pairs={{0,4},{4,0},{8,12},{12,8},{16,20},{20,16},{24,28},{28,24},{1,5},{5... | collective-permute-start | bytes 208904 | tf_op jit(solution)/shard_map/ppermute | solution.py:278
  72.6 3.0 %collective-permute-start.19 = (f32[136,128]{1,0:T(8,128)S(1)}, f32[136,128]{1,0:T(8,128)S(1)}, u32[]{:S(2)}, u32[]{:S(2)}) collective-permute-start(f32[136,128]{1,0:T(8,128)S(1)} %add_add_fusion.refs_0_), channel_id=1, source_target_pairs={{0,1},{1,0},{2,3},{3,2},{4,5},{5,4},{6,7},{7,6},{8,9},{9,8},{10,11... | collective-permute-start | bytes 208904 | tf_op jit(solution)/shard_map/ppermute | solution.py:276
  74.4 1.3 collective-permute-start.22
  75.1 1.3 collective-permute-start.21
  75.4 1.3 collective-permute-start.20

commit v8 on v7

--- a/solution.py
+++ b/solution.py
@@ -68,14 +68,14 @@
             fill[n][k] = base[n] + k * stride
     place_load.wait()
     live = counts[0, 0]
-    shift = panels.shape[0].bit_length()
     unroll = math.gcd(cuts[1], 6)
 
     def put(g, carry):
         for i in range(unroll):
-            mine = [jnp.minimum(cut + g * unroll + i, slots - 1) for cut in cuts[:-1]]
+            mine = [cut + g * unroll + i for cut in cuts[:-1]]
+            if slots % PARTS:
+                mine = [jnp.minimum(t, slots - 1) for t in mine]
             names = [key[place_of[0, t]] for t in mine]
-            made = [(t << shift) | place_of[1, t] for t in mine]
             lists = [
                 jnp.where(cut + g * unroll + i < live, name, blocks)
                 for cut, name in zip(cuts, names)
@@ -83,20 +83,20 @@
             spots = [fill[n][k] for n, k in enumerate(lists)]
             for n in range(PARTS):
                 fill[n][lists[n]] = spots[n] + 1
-                entry[spots[n]] = made[n]
+                entry[spots[n]] = mine[n]
         return carry
 
     lax.fori_loop(0, (jnp.minimum(live, cuts[1]) + unroll - 1) // unroll, put, 0)
 
     for i in range(PAIR):
-        entry[base[-1] + i] = slots << shift
+        entry[base[-1] + i] = slots
     number, bounds = 0, [0]
     for n in range(PARTS):
         for k in range(blocks):
             head = base[n] + k * stride
             end = fill[n][k]
             for i in range(PAIR - 1):
-                entry[end + i] = slots << shift
+                entry[end + i] = slots
 
             def add_pair(j, at, head=head, k=k):
                 first_of[at + j] = head + j * PAIR
@@ -118,9 +118,8 @@
 
     def turn(g, carry):
         firsts = [first_of[g * TURN + i] for i in range(TURN)]
-        entries = [[entry[at + j] for j in range(PAIR)] for at in firsts]
-        slot = [[e >> shift for e in pair] for pair in entries]
-        column = [[e & ((1 << shift) - 1) for e in pair] for pair in entries]
+        slot = [[entry[at + j] for j in range(PAIR)] for at in firsts]
+        column = [[place_of[1, jnp.minimum(t, slots - 1)] for t in pair] for pair in slot]
         if not resident:
             copies = [
                 pltpu.make_async_copy(

time: 191 us -> 191 us (level)
    ppermute x16, starting transfers between devices: 8.84 us -> 10.8 us  [swapped(): return lax.ppermute(x, 'col', [(c, c ^ col_flip) for c in range(cols)])]
  transfers between devices with their start and end apart: 23 -> 23, of which waited for: 18 -> 15; matrix products, arithmetic and copies ran while one was open for 0% -> 0% of each run, Pallas kernels for 5% -> 5%
where the time goes in v8:
time: 191 us
  Pallas kernels  130 us (68%)
  waiting for transfers between devices  36.9 us (19%)
  starting transfers between devices  21.5 us (11%)
    pallas_call x1, Pallas kernels, factor(): pl.pallas_call(functools.partial(factor_kernel, len(rows), scale, 6), out...  114 us
    ppermute x16, waiting for transfers between devices, swapped(): return lax.ppermute(x, 'col', [(c, c ^ col_flip) for c in range(cols)])  27.5 us
    pallas_call x2, Pallas kernels, tile_products(): pl.pallas_call(functools.partial(tile_kernel, resident, spans, stride), o...  14.8 us
    ppermute x16, starting transfers between devices, swapped(): return lax.ppermute(x, 'col', [(c, c ^ col_flip) for c in range(cols)])  10.8 us
    ppermute x5, waiting for transfers between devices, swapped(): return lax.ppermute(x, 'row', [(r, r ^ row_flip) for r in range(rows)])  5.77 us
    ppermute x5, starting transfers between devices, swapped(): return lax.ppermute(x, 'row', [(r, r ^ row_flip) for r in range(rows)])  5.49 us
    ppermute x2, starting transfers between devices, swapped(): return lax.ppermute(x, ('row', 'col'), route)  5.28 us
  transfers between devices with their start and end apart: 23, of which 15 were waited for; matrix products, arithmetic and copies ran while one was open for 0% of the time, Pallas kernels for 5%

profile of v8, /device:TPU:0, one launch (start us, length us, event | category | flops | bytes accessed | tf_op | source)
XLA Modules:
  0.0 190.8 jit_solution(16983009548131524862)
XLA Ops:
  1.3 7.3 %shard_map.59 = (f32[1,128,512]{2,1,0:T(8,128)S(1)}, f32[4,128,512]{2,1,0:T(8,128)S(1)}, f32[1,128,512]{2,1,0:T(8,128)S(1)}, f32[4,128,512]{2,1,0:T(8,128)S(1)}) custom-call(s32[1,1]{1,0:T(1,128)S(6)} %copy.6.counts, s32[2,360]{1,0:T(2,128)} %bitcast.19, bf16[360,128,128]{2,1,0:T(8,128)(2,1)} %bitcast.15, bf16[48,128,512]{2,1,0:T(8,128)(2,1)} %bitcast.17), custom_call_target="tpu_custom_call" | custom-call | tf_op jit(solution)/shard_map/pallas_call | solution.py:165
  8.6 0.5 collective-permute-start
  9.1 1.2 collective-permute-done
  10.2 0.4 collective-permute-start.1
  10.7 3.6 %collective-permute-start.2 = (f32[1,128,512]{2,1,0:T(8,128)S(1)}, f32[1,128,512]{2,1,0:T(8,128)S(1)}, u32[]{:S(2)}, u32[]{:S(2)}) collective-permute-start(f32[1,128,512]{2,1,0:T(8,128)S(1)} %add.51), channel_id=1, source_target_pairs={{0,2},{1,3},{2,0},{3,1},{4,6},{5,7},{6,4},{7,5},{8,10},{9,11},{10,... | collective-permute-start | bytes 786440 | tf_op jit(solution)/shard_map/ppermute | solution.py:275
  14.3 0.2 add.52
  14.5 2.5 %collective-permute-start.8 = (f32[4,128,512]{2,1,0:T(8,128)S(1)}, f32[4,128,512]{2,1,0:T(8,128)S(1)}, u32[]{:S(2)}, u32[]{:S(2)}) collective-permute-start(f32[4,128,512]{2,1,0:T(8,128)S(1)} %add.52), channel_id=1, source_target_pairs={{0,2},{1,3},{2,0},{3,1},{4,6},{5,7},{6,4},{7,5},{8,10},{9,11},{10,... | collective-permute-start | bytes 3145736 | tf_op jit(solution)/shard_map/ppermute | solution.py:275
  16.9 7.5 %shard_map.60 = (f32[1,128,512]{2,1,0:T(8,128)S(1)}, f32[1,128,512]{2,1,0:T(8,128)S(1)}, f32[4,128,512]{2,1,0:T(8,128)S(1)}, f32[1,128,512]{2,1,0:T(8,128)S(1)},...) custom-call(s32[1,1]{1,0:T(1,128)S(6)} %copy.6.counts, ...), custom_call_target="tpu_custom_call" | custom-call | tf_op jit(solution)/shard_map/pallas_call | solution.py:165
  24.5 0.0 collective-permute-done.2.refs_2_
  24.5 0.1 collective-permute-start.7
  24.6 0.5 collective-permute-start.4
  25.0 0.1 collective-permute-start.6
  25.1 0.4 collective-permute-start.3
  25.6 2.0 %collective-permute-done.4 = f32[1,128,512]{2,1,0:T(8,128)S(1)} collective-permute-done((f32[1,128,512]{2,1,0:T(8,128)S(1)}, f32[1,128,512]{2,1,0:T(8,128)S(1)}, u32[]{:S(2)}, u32[]{:S(2)}) %collective-permute-start.4) | collective-permute-done | bytes 262176 | tf_op jit(solution)/shard_map/ppermute | solution.py:275
  27.6 1.1 collective-permute-start.5
  28.7 0.0 collective-permute-done.6.refs_1_
  28.7 0.4 shard_map.61
  29.1 14.8 %collective-permute-done.8.refs_2_ = f32[4,128,512]{2,1,0:T(8,128)S(1)} collective-permute-done((f32[4,128,512]{2,1,0:T(8,128)S(1)}, f32[4,128,512]{2,1,0:T(8,128)S(1)}, u32[]{:S(2)}, u32[]{:S(2)}) %collective-permute-start.8) | collective-permute-done | bytes 1048608 | tf_op jit(solution)/shard_map/ppermute | solution.py:275
  43.9 0.0 collective-permute-done.7.refs_1_
  43.9 1.1 shard_map.62
  45.0 0.0 collective-permute-done.3.refs_1_
  45.0 4.2 %collective-permute-done.5.refs_2_ = f32[1,128,512]{2,1,0:T(8,128)S(1)} collective-permute-done((f32[1,128,512]{2,1,0:T(8,128)S(1)}, f32[1,128,512]{2,1,0:T(8,128)S(1)}, u32[]{:S(2)}, u32[]{:S(2)}) %collective-permute-start.5) | collective-permute-done | bytes 262176 | tf_op jit(solution)/shard_map/ppermute | solution.py:275
  49.2 0.5 shard_map.63
  49.6 0.1 collective-permute-start.9
  49.7 1.5 collective-permute-done.9
  51.3 3.7 %collective-permute-start.12 = (f32[136,128]{1,0:T(8,128)S(1)}, f32[136,128]{1,0:T(8,128)S(1)}, u32[]{:S(2)}, u32[]{:S(2)}) collective-permute-start(f32[136,128]{1,0:T(8,128)S(1)} %get-tuple-element.62), channel_id=1, source_target_pairs={{0,6},{1,7},{2,4},{3,5},{4,2},{5,3},{6,0},{7,1},{8,14},{9,15},{10,... | collective-permute-start | bytes 208904 | tf_op jit(solution)/shard_map/ppermute | solution.py:283
  55.0 0.3 collective-permute-start.11
  55.3 0.4 collective-permute-start.10
  55.6 1.9 collective-permute-done.12
  57.5 1.8 collective-permute-done.11
  59.3 0.3 collective-permute-done.10
  59.6 3.6 %collective-permute-start.15 = (f32[136,128]{1,0:T(8,128)S(1)}, f32[136,128]{1,0:T(8,128)S(1)}, u32[]{:S(2)}, u32[]{:S(2)}) collective-permute-start(f32[136,128]{1,0:T(8,128)S(1)} %fusion.5), channel_id=1, source_target_pairs={{0,24},{4,28},{8,16},{12,20},{16,8},{20,12},{24,0},{28,4},{1,25},{... | collective-permute-start | bytes 208904 | tf_op jit(solution)/shard_map/ppermute | solution.py:277
  63.2 0.0 collective-permute-start.14
  63.2 0.9 collective-permute-start.13
  64.1 1.7 collective-permute-done.15
  65.8 2.6 %collective-permute-done.14 = f32[136,128]{1,0:T(8,128)S(1)} collective-permute-done((f32[136,128]{1,0:T(8,128)S(1)}, f32[136,128]{1,0:T(8,128)S(1)}, u32[]{:S(2)}, u32[]{:S(2)}) %collective-permute-start.14) | collective-permute-done | bytes 69664 | tf_op jit(solution)/shard_map/ppermute | solution.py:277
  68.4 0.0 collective-permute-done.13
  68.4 1.6 collective-permute-start.18
  70.0 1.3 collective-permute-start.17
  71.3 0.7 collective-permute-start.16
  72.0 0.0 collective-permute-start.19
  72.0 1.7 collective-permute-done.18.refs_3_
  73.7 0.0 collective-permute-start.22
  73.7 0.7 collective-permute-done.17.refs_2_
  74.4 1.2 collective-permute-done.16.refs_1_
  75.6 0.1 collective-permute-done.21.refs_6_
  75.7 1.2 collective-permute-done.20.refs_5_
  76.9 113.7 %shard_map.64 = (f32[768,512]{1,0:T(8,128)}, f32[512,512]{1,0:T(8,128)}) custom-call(f32[136,128]{1,0:T(8,128)S(1)} %add_add_fusion.refs_0_, f32[136,128]{1,0:T(8,128)S(1)} %collective-permute-done.16.refs_1_, f32[136,128]{1,0:T(8,128)S(1)} %collective-permute-done.17.refs_2_, f32[136,128]{1,0:T(8,128)S(1)} %collective-permute-done.18.refs_3_, ...), custom_call_target="tpu_custom_call" | custom-call | tf_op jit(solution)/shard_map/pallas_call | solution.py:546
  (10 shorter events, 0.2 us)
Async XLA Ops:
  8.6 1.7 collective-permute-start
  10.2 4.0 %collective-permute-start.1 = (f32[4,128,512]{2,1,0:T(8,128)S(1)}, f32[4,128,512]{2,1,0:T(8,128)S(1)}, u32[]{:S(2)}, u32[]{:S(2)}) collective-permute-start(f32[4,128,512]{2,1,0:T(8,128)S(1)} %get-tuple-element.36), channel_id=1, source_target_pairs={{0,1},{1,0},{2,3},{3,2},{4,5},{5,4},{6,7},{7,6},{8,9},{9,8},{10,11... | collective-permute-start | bytes 3145736 | tf_op jit(solution)/shard_map/ppermute | solution.py:275
  10.7 13.8 %collective-permute-start.2 = (f32[1,128,512]{2,1,0:T(8,128)S(1)}, f32[1,128,512]{2,1,0:T(8,128)S(1)}, u32[]{:S(2)}, u32[]{:S(2)}) collective-permute-start(f32[1,128,512]{2,1,0:T(8,128)S(1)} %add.51), channel_id=1, source_target_pairs={{0,2},{1,3},{2,0},{3,1},{4,6},{5,7},{6,4},{7,5},{8,10},{9,11},{10,... | collective-permute-start | bytes 786440 | tf_op jit(solution)/shard_map/ppermute | solution.py:275
  14.5 29.4 %collective-permute-start.8 = (f32[4,128,512]{2,1,0:T(8,128)S(1)}, f32[4,128,512]{2,1,0:T(8,128)S(1)}, u32[]{:S(2)}, u32[]{:S(2)}) collective-permute-start(f32[4,128,512]{2,1,0:T(8,128)S(1)} %add.52), channel_id=1, source_target_pairs={{0,2},{1,3},{2,0},{3,1},{4,6},{5,7},{6,4},{7,5},{8,10},{9,11},{10,... | collective-permute-start | bytes 3145736 | tf_op jit(solution)/shard_map/ppermute | solution.py:275
  24.5 19.4 %collective-permute-start.7 = (f32[4,128,512]{2,1,0:T(8,128)S(1)}, f32[4,128,512]{2,1,0:T(8,128)S(1)}, u32[]{:S(2)}, u32[]{:S(2)}) collective-permute-start(f32[4,128,512]{2,1,0:T(8,128)S(1)} %get-tuple-element.55), channel_id=1, source_target_pairs={{0,1},{1,0},{2,3},{3,2},{4,5},{5,4},{6,7},{7,6},{8,9},{9,8},{10,11... | collective-permute-start | bytes 3145736 | tf_op jit(solution)/shard_map/ppermute | solution.py:275
  24.6 3.0 %collective-permute-start.4 = (f32[1,128,512]{2,1,0:T(8,128)S(1)}, f32[1,128,512]{2,1,0:T(8,128)S(1)}, u32[]{:S(2)}, u32[]{:S(2)}) collective-permute-start(f32[1,128,512]{2,1,0:T(8,128)S(1)} %get-tuple-element.49), channel_id=1, source_target_pairs={{0,1},{1,0},{2,3},{3,2},{4,5},{5,4},{6,7},{7,6},{8,9},{9,8},{10,11... | collective-permute-start | bytes 786440 | tf_op jit(solution)/shard_map/ppermute | solution.py:275
  25.0 3.6 %collective-permute-start.6 = (f32[1,128,512]{2,1,0:T(8,128)S(1)}, f32[1,128,512]{2,1,0:T(8,128)S(1)}, u32[]{:S(2)}, u32[]{:S(2)}) collective-permute-start(f32[1,128,512]{2,1,0:T(8,128)S(1)} %get-tuple-element.51), channel_id=1, source_target_pairs={{0,1},{1,0},{2,3},{3,2},{4,5},{5,4},{6,7},{7,6},{8,9},{9,8},{10,11... | collective-permute-start | bytes 786440 | tf_op jit(solution)/shard_map/ppermute | solution.py:275
  25.1 19.8 %collective-permute-start.3 = (f32[1,128,512]{2,1,0:T(8,128)S(1)}, f32[1,128,512]{2,1,0:T(8,128)S(1)}, u32[]{:S(2)}, u32[]{:S(2)}) collective-permute-start(f32[1,128,512]{2,1,0:T(8,128)S(1)} %get-tuple-element.47), channel_id=1, source_target_pairs={{0,1},{1,0},{2,3},{3,2},{4,5},{5,4},{6,7},{7,6},{8,9},{9,8},{10,11... | collective-permute-start | bytes 786440 | tf_op jit(solution)/shard_map/ppermute | solution.py:275
  27.6 21.6 %collective-permute-start.5 = (f32[1,128,512]{2,1,0:T(8,128)S(1)}, f32[1,128,512]{2,1,0:T(8,128)S(1)}, u32[]{:S(2)}, u32[]{:S(2)}) collective-permute-start(f32[1,128,512]{2,1,0:T(8,128)S(1)} %add.53), channel_id=1, source_target_pairs={{0,2},{1,3},{2,0},{3,1},{4,6},{5,7},{6,4},{7,5},{8,10},{9,11},{10,... | collective-permute-start | bytes 786440 | tf_op jit(solution)/shard_map/ppermute | solution.py:275
  49.6 1.6 collective-permute-start.9
  51.3 6.2 %collective-permute-start.12 = (f32[136,128]{1,0:T(8,128)S(1)}, f32[136,128]{1,0:T(8,128)S(1)}, u32[]{:S(2)}, u32[]{:S(2)}) collective-permute-start(f32[136,128]{1,0:T(8,128)S(1)} %get-tuple-element.62), channel_id=1, source_target_pairs={{0,6},{1,7},{2,4},{3,5},{4,2},{5,3},{6,0},{7,1},{8,14},{9,15},{10,... | collective-permute-start | bytes 208904 | tf_op jit(solution)/shard_map/ppermute | solution.py:283
  55.0 4.3 %collective-permute-start.11 = (f32[136,128]{1,0:T(8,128)S(1)}, f32[136,128]{1,0:T(8,128)S(1)}, u32[]{:S(2)}, u32[]{:S(2)}) collective-permute-start(f32[136,128]{1,0:T(8,128)S(1)} %get-tuple-element.63), channel_id=1, source_target_pairs={{0,2},{1,3},{2,0},{3,1},{4,6},{5,7},{6,4},{7,5},{8,10},{9,11},{10,... | collective-permute-start | bytes 208904 | tf_op jit(solution)/shard_map/ppermute | solution.py:275
  55.3 4.3 %collective-permute-start.10 = (f32[136,128]{1,0:T(8,128)S(1)}, f32[136,128]{1,0:T(8,128)S(1)}, u32[]{:S(2)}, u32[]{:S(2)}) collective-permute-start(f32[136,128]{1,0:T(8,128)S(1)} %get-tuple-element.64), channel_id=1, source_target_pairs={{0,4},{4,0},{8,12},{12,8},{16,20},{20,16},{24,28},{28,24},{1,5},{5... | collective-permute-start | bytes 208904 | tf_op jit(solution)/shard_map/ppermute | solution.py:277
  59.6 6.2 %collective-permute-start.15 = (f32[136,128]{1,0:T(8,128)S(1)}, f32[136,128]{1,0:T(8,128)S(1)}, u32[]{:S(2)}, u32[]{:S(2)}) collective-permute-start(f32[136,128]{1,0:T(8,128)S(1)} %fusion.5), channel_id=1, source_target_pairs={{0,24},{4,28},{8,16},{12,20},{16,8},{20,12},{24,0},{28,4},{1,25},{... | collective-permute-start | bytes 208904 | tf_op jit(solution)/shard_map/ppermute | solution.py:277
  63.2 5.2 %collective-permute-start.14 = (f32[136,128]{1,0:T(8,128)S(1)}, f32[136,128]{1,0:T(8,128)S(1)}, u32[]{:S(2)}, u32[]{:S(2)}) collective-permute-start(f32[136,128]{1,0:T(8,128)S(1)} %fusion.5), channel_id=1, source_target_pairs={{0,16},{4,20},{8,24},{12,28},{16,0},{20,4},{24,8},{28,12},{1,17},{... | collective-permute-start | bytes 208904 | tf_op jit(solution)/shard_map/ppermute | solution.py:277
  63.2 5.2 %collective-permute-start.13 = (f32[136,128]{1,0:T(8,128)S(1)}, f32[136,128]{1,0:T(8,128)S(1)}, u32[]{:S(2)}, u32[]{:S(2)}) collective-permute-start(f32[136,128]{1,0:T(8,128)S(1)} %fusion.5), channel_id=1, source_target_pairs={{0,8},{4,12},{8,0},{12,4},{16,24},{20,28},{24,16},{28,20},{1,9},{5... | collective-permute-start | bytes 208904 | tf_op jit(solution)/shard_map/ppermute | solution.py:277
  68.4 5.3 %collective-permute-start.18 = (f32[136,128]{1,0:T(8,128)S(1)}, f32[136,128]{1,0:T(8,128)S(1)}, u32[]{:S(2)}, u32[]{:S(2)}) collective-permute-start(f32[136,128]{1,0:T(8,128)S(1)} %add_add_fusion.refs_0_), channel_id=1, source_target_pairs={{0,6},{1,7},{2,4},{3,5},{4,2},{5,3},{6,0},{7,1},{8,14},{9,15},{10,... | collective-permute-start | bytes 208904 | tf_op jit(solution)/shard_map/ppermute | solution.py:283
  70.0 4.4 %collective-permute-start.17 = (f32[136,128]{1,0:T(8,128)S(1)}, f32[136,128]{1,0:T(8,128)S(1)}, u32[]{:S(2)}, u32[]{:S(2)}) collective-permute-start(f32[136,128]{1,0:T(8,128)S(1)} %add_add_fusion.refs_0_), channel_id=1, source_target_pairs={{0,2},{1,3},{2,0},{3,1},{4,6},{5,7},{6,4},{7,5},{8,10},{9,11},{10,... | collective-permute-start | bytes 208904 | tf_op jit(solution)/shard_map/ppermute | solution.py:275
  71.3 4.3 %collective-permute-start.16 = (f32[136,128]{1,0:T(8,128)S(1)}, f32[136,128]{1,0:T(8,128)S(1)}, u32[]{:S(2)}, u32[]{:S(2)}) collective-permute-start(f32[136,128]{1,0:T(8,128)S(1)} %add_add_fusion.refs_0_), channel_id=1, source_target_pairs={{0,4},{4,0},{8,12},{12,8},{16,20},{20,16},{24,28},{28,24},{1,5},{5... | collective-permute-start | bytes 208904 | tf_op jit(solution)/shard_map/ppermute | solution.py:277
  72.0 3.6 %collective-permute-start.19 = (f32[136,128]{1,0:T(8,128)S(1)}, f32[136,128]{1,0:T(8,128)S(1)}, u32[]{:S(2)}, u32[]{:S(2)}) collective-permute-start(f32[136,128]{1,0:T(8,128)S(1)} %add_add_fusion.refs_0_), channel_id=1, source_target_pairs={{0,1},{1,0},{2,3},{3,2},{4,5},{5,4},{6,7},{7,6},{8,9},{9,8},{10,11... | collective-permute-start | bytes 208904 | tf_op jit(solution)/shard_map/ppermute | solution.py:275
  73.7 1.9 collective-permute-start.22
  74.4 1.3 collective-permute-start.21
  75.6 1.3 collective-permute-start.20

commit v9 on v8

--- a/solution.py
+++ b/solution.py
@@ -409,11 +409,14 @@
             if exact:
                 norm = norm + jnp.sum(p * p, keepdims=True)
         for p, part, k in zip(strips, (top, low), (wide, size)):
-            corner = dot_rows(ph[part, :k], ph[part, :k]) * half_mask[...]
-            corner = p[:, k - wide :] - dot(ph[part, part], ph[part, part]) - corner
+            corner = p[:, k - wide :] - dot(ph[part, part], ph[part, part])
+            if exact:
+                corner = corner - dot_rows(ph[part, :k], ph[part, :k]) * half_mask[...]
             dh[part, part] = corner.astype(BF16)
             if k == size:
-                side = dot(ph[low, :], ph[:, top]) + dot_rows(ph[low, top], ph[top, top])
+                side = dot(ph[low, :], ph[:, top])
+                if exact:
+                    side = side + dot_rows(ph[low, top], ph[top, top])
                 dh[low, top] = (p[:, :wide] - side).astype(BF16)
         for part in (top, low):
             w[part, part] = wb[part, part].astype(F32) - dot(dh[part, part], wb[part, part])

time: 191 us -> 191 us (level)
    ppermute x16, starting transfers between devices: 10.8 us -> 8.27 us  [swapped(): return lax.ppermute(x, 'col', [(c, c ^ col_flip) for c in range(cols)])]
  transfers between devices with their start and end apart: 23 -> 23, of which waited for: 15 -> 17; matrix products, arithmetic and copies ran while one was open for 0% -> 0% of each run, Pallas kernels for 5% -> 5%
where the time goes in v9:
time: 191 us; the launch traced here: 190 us
  Pallas kernels  130 us (68%)
  waiting for transfers between devices  38.4 us (20%)
  starting transfers between devices  20.1 us (11%)
    pallas_call x1, Pallas kernels, factor(): pl.pallas_call(functools.partial(factor_kernel, len(rows), scale, 6), out...  113 us
    ppermute x16, waiting for transfers between devices, swapped(): return lax.ppermute(x, 'col', [(c, c ^ col_flip) for c in range(cols)])  28.2 us
    pallas_call x2, Pallas kernels, tile_products(): pl.pallas_call(functools.partial(tile_kernel, resident, spans, stride), o...  14.7 us
    ppermute x16, starting transfers between devices, swapped(): return lax.ppermute(x, 'col', [(c, c ^ col_flip) for c in range(cols)])  8.27 us
    ppermute x5, starting transfers between devices, swapped(): return lax.ppermute(x, 'row', [(r, r ^ row_flip) for r in range(rows)])  6.19 us
    ppermute x5, waiting for transfers between devices, swapped(): return lax.ppermute(x, 'row', [(r, r ^ row_flip) for r in range(rows)])  6.1 us
    ppermute x2, starting transfers between devices, swapped(): return lax.ppermute(x, ('row', 'col'), route)  5.64 us
    ppermute x2, waiting for transfers between devices, swapped(): return lax.ppermute(x, ('row', 'col'), route)  4.1 us
  transfers between devices with their start and end apart: 23, of which 17 were waited for; matrix products, arithmetic and copies ran while one was open for 0% of the time, Pallas kernels for 5%

profile of v9, /device:TPU:0, one launch (start us, length us, event | category | flops | bytes accessed | tf_op | source)
XLA Modules:
  0.0 190.5 jit_solution(2358680205544337962)
XLA Ops:
  1.3 7.3 %shard_map.59 = (f32[1,128,512]{2,1,0:T(8,128)S(1)}, f32[4,128,512]{2,1,0:T(8,128)S(1)}, f32[1,128,512]{2,1,0:T(8,128)S(1)}, f32[4,128,512]{2,1,0:T(8,128)S(1)}) custom-call(s32[1,1]{1,0:T(1,128)S(6)} %copy.6.counts, s32[2,360]{1,0:T(2,128)} %bitcast.19, bf16[360,128,128]{2,1,0:T(8,128)(2,1)} %bitcast.15, bf16[48,128,512]{2,1,0:T(8,128)(2,1)} %bitcast.17), custom_call_target="tpu_custom_call" | custom-call | tf_op jit(solution)/shard_map/pallas_call | solution.py:165
  8.6 0.5 collective-permute-start
  9.1 1.2 collective-permute-done
  10.2 0.4 collective-permute-start.1
  10.7 2.4 %collective-permute-start.2 = (f32[1,128,512]{2,1,0:T(8,128)S(1)}, f32[1,128,512]{2,1,0:T(8,128)S(1)}, u32[]{:S(2)}, u32[]{:S(2)}) collective-permute-start(f32[1,128,512]{2,1,0:T(8,128)S(1)} %add.51), channel_id=1, source_target_pairs={{0,2},{1,3},{2,0},{3,1},{4,6},{5,7},{6,4},{7,5},{8,10},{9,11},{10,... | collective-permute-start | bytes 786440 | tf_op jit(solution)/shard_map/ppermute | solution.py:275
  13.1 0.0 collective-permute-done.1
  13.1 0.2 add.52
  13.3 2.3 %collective-permute-start.8 = (f32[4,128,512]{2,1,0:T(8,128)S(1)}, f32[4,128,512]{2,1,0:T(8,128)S(1)}, u32[]{:S(2)}, u32[]{:S(2)}) collective-permute-start(f32[4,128,512]{2,1,0:T(8,128)S(1)} %add.52), channel_id=1, source_target_pairs={{0,2},{1,3},{2,0},{3,1},{4,6},{5,7},{6,4},{7,5},{8,10},{9,11},{10,... | collective-permute-start | bytes 3145736 | tf_op jit(solution)/shard_map/ppermute | solution.py:275
  15.5 7.4 %shard_map.60 = (f32[1,128,512]{2,1,0:T(8,128)S(1)}, f32[1,128,512]{2,1,0:T(8,128)S(1)}, f32[4,128,512]{2,1,0:T(8,128)S(1)}, f32[1,128,512]{2,1,0:T(8,128)S(1)},...) custom-call(s32[1,1]{1,0:T(1,128)S(6)} %copy.6.counts, ...), custom_call_target="tpu_custom_call" | custom-call | tf_op jit(solution)/shard_map/pallas_call | solution.py:165
  23.0 0.0 collective-permute-done.2.refs_2_
  23.0 0.1 collective-permute-start.7
  23.1 0.4 collective-permute-start.4
  23.6 0.1 collective-permute-start.6
  23.6 0.4 collective-permute-start.3
  24.1 2.0 %collective-permute-done.4 = f32[1,128,512]{2,1,0:T(8,128)S(1)} collective-permute-done((f32[1,128,512]{2,1,0:T(8,128)S(1)}, f32[1,128,512]{2,1,0:T(8,128)S(1)}, u32[]{:S(2)}, u32[]{:S(2)}) %collective-permute-start.4) | collective-permute-done | bytes 262176 | tf_op jit(solution)/shard_map/ppermute | solution.py:275
  26.1 0.1 collective-permute-start.5
  26.2 0.3 collective-permute-done.6.refs_1_
  26.5 0.4 shard_map.61
  26.9 15.8 %collective-permute-done.8.refs_2_ = f32[4,128,512]{2,1,0:T(8,128)S(1)} collective-permute-done((f32[4,128,512]{2,1,0:T(8,128)S(1)}, f32[4,128,512]{2,1,0:T(8,128)S(1)}, u32[]{:S(2)}, u32[]{:S(2)}) %collective-permute-start.8) | collective-permute-done | bytes 1048608 | tf_op jit(solution)/shard_map/ppermute | solution.py:275
  42.6 0.0 collective-permute-done.7.refs_1_
  42.6 1.1 shard_map.62
  43.7 4.0 %collective-permute-done.5.refs_2_ = f32[1,128,512]{2,1,0:T(8,128)S(1)} collective-permute-done((f32[1,128,512]{2,1,0:T(8,128)S(1)}, f32[1,128,512]{2,1,0:T(8,128)S(1)}, u32[]{:S(2)}, u32[]{:S(2)}) %collective-permute-start.5) | collective-permute-done | bytes 262176 | tf_op jit(solution)/shard_map/ppermute | solution.py:275
  47.8 0.5 shard_map.63
  48.2 0.1 collective-permute-start.9
  48.3 1.5 collective-permute-done.9
  49.9 4.2 %collective-permute-start.12 = (f32[136,128]{1,0:T(8,128)S(1)}, f32[136,128]{1,0:T(8,128)S(1)}, u32[]{:S(2)}, u32[]{:S(2)}) collective-permute-start(f32[136,128]{1,0:T(8,128)S(1)} %get-tuple-element.62), channel_id=1, source_target_pairs={{0,6},{1,7},{2,4},{3,5},{4,2},{5,3},{6,0},{7,1},{8,14},{9,15},{10,... | collective-permute-start | bytes 208904 | tf_op jit(solution)/shard_map/ppermute | solution.py:283
  54.1 0.3 collective-permute-start.11
  54.4 0.4 collective-permute-start.10
  54.7 1.9 collective-permute-done.12
  56.6 1.8 collective-permute-done.11
  58.4 0.3 collective-permute-done.10
  58.7 4.0 %collective-permute-start.15 = (f32[136,128]{1,0:T(8,128)S(1)}, f32[136,128]{1,0:T(8,128)S(1)}, u32[]{:S(2)}, u32[]{:S(2)}) collective-permute-start(f32[136,128]{1,0:T(8,128)S(1)} %fusion.5), channel_id=1, source_target_pairs={{0,24},{4,28},{8,16},{12,20},{16,8},{20,12},{24,0},{28,4},{1,25},{... | collective-permute-start | bytes 208904 | tf_op jit(solution)/shard_map/ppermute | solution.py:277
  62.8 0.6 collective-permute-start.13
  63.4 2.4 %collective-permute-done.15 = f32[136,128]{1,0:T(8,128)S(1)} collective-permute-done((f32[136,128]{1,0:T(8,128)S(1)}, f32[136,128]{1,0:T(8,128)S(1)}, u32[]{:S(2)}, u32[]{:S(2)}) %collective-permute-start.15) | collective-permute-done | bytes 69664 | tf_op jit(solution)/shard_map/ppermute | solution.py:277
  65.8 3.0 %collective-permute-done.14 = f32[136,128]{1,0:T(8,128)S(1)} collective-permute-done((f32[136,128]{1,0:T(8,128)S(1)}, f32[136,128]{1,0:T(8,128)S(1)}, u32[]{:S(2)}, u32[]{:S(2)}) %collective-permute-start.14) | collective-permute-done | bytes 69664 | tf_op jit(solution)/shard_map/ppermute | solution.py:277
  68.8 0.0 collective-permute-done.13
  68.8 1.4 collective-permute-start.18
  70.2 1.0 collective-permute-start.17
  71.2 1.2 collective-permute-start.16
  72.4 2.2 %collective-permute-done.18.refs_3_ = f32[136,128]{1,0:T(8,128)S(1)} collective-permute-done((f32[136,128]{1,0:T(8,128)S(1)}, f32[136,128]{1,0:T(8,128)S(1)}, u32[]{:S(2)}, u32[]{:S(2)}) %collective-permute-start.18) | collective-permute-done | bytes 69664 | tf_op jit(solution)/shard_map/ppermute | solution.py:283
  74.6 0.0 collective-permute-start.22
  74.6 0.3 collective-permute-done.17.refs_2_
  75.0 0.2 collective-permute-start.21
  75.1 0.4 collective-permute-done.16.refs_1_
  75.6 0.3 collective-permute-done.22.refs_7_
  75.9 0.3 collective-permute-done.21.refs_6_
  76.2 0.6 collective-permute-done.20.refs_5_
  76.8 113.5 %shard_map.64 = (f32[768,512]{1,0:T(8,128)}, f32[512,512]{1,0:T(8,128)}) custom-call(f32[136,128]{1,0:T(8,128)S(1)} %add_add_fusion.refs_0_, f32[136,128]{1,0:T(8,128)S(1)} %collective-permute-done.16.refs_1_, f32[136,128]{1,0:T(8,128)S(1)} %collective-permute-done.17.refs_2_, f32[136,128]{1,0:T(8,128)S(1)} %collective-permute-done.18.refs_3_, ...), custom_call_target="tpu_custom_call" | custom-call | tf_op jit(solution)/shard_map/pallas_call | solution.py:549
  (10 shorter events, 0.1 us)
Async XLA Ops:
  8.6 1.7 collective-permute-start
  10.2 2.8 %collective-permute-start.1 = (f32[4,128,512]{2,1,0:T(8,128)S(1)}, f32[4,128,512]{2,1,0:T(8,128)S(1)}, u32[]{:S(2)}, u32[]{:S(2)}) collective-permute-start(f32[4,128,512]{2,1,0:T(8,128)S(1)} %get-tuple-element.36), channel_id=1, source_target_pairs={{0,1},{1,0},{2,3},{3,2},{4,5},{5,4},{6,7},{7,6},{8,9},{9,8},{10,11... | collective-permute-start | bytes 3145736 | tf_op jit(solution)/shard_map/ppermute | solution.py:275
  10.7 12.3 %collective-permute-start.2 = (f32[1,128,512]{2,1,0:T(8,128)S(1)}, f32[1,128,512]{2,1,0:T(8,128)S(1)}, u32[]{:S(2)}, u32[]{:S(2)}) collective-permute-start(f32[1,128,512]{2,1,0:T(8,128)S(1)} %add.51), channel_id=1, source_target_pairs={{0,2},{1,3},{2,0},{3,1},{4,6},{5,7},{6,4},{7,5},{8,10},{9,11},{10,... | collective-permute-start | bytes 786440 | tf_op jit(solution)/shard_map/ppermute | solution.py:275
  13.3 29.3 %collective-permute-start.8 = (f32[4,128,512]{2,1,0:T(8,128)S(1)}, f32[4,128,512]{2,1,0:T(8,128)S(1)}, u32[]{:S(2)}, u32[]{:S(2)}) collective-permute-start(f32[4,128,512]{2,1,0:T(8,128)S(1)} %add.52), channel_id=1, source_target_pairs={{0,2},{1,3},{2,0},{3,1},{4,6},{5,7},{6,4},{7,5},{8,10},{9,11},{10,... | collective-permute-start | bytes 3145736 | tf_op jit(solution)/shard_map/ppermute | solution.py:275
  23.0 19.7 %collective-permute-start.7 = (f32[4,128,512]{2,1,0:T(8,128)S(1)}, f32[4,128,512]{2,1,0:T(8,128)S(1)}, u32[]{:S(2)}, u32[]{:S(2)}) collective-permute-start(f32[4,128,512]{2,1,0:T(8,128)S(1)} %get-tuple-element.55), channel_id=1, source_target_pairs={{0,1},{1,0},{2,3},{3,2},{4,5},{5,4},{6,7},{7,6},{8,9},{9,8},{10,11... | collective-permute-start | bytes 3145736 | tf_op jit(solution)/shard_map/ppermute | solution.py:275
  23.1 3.0 %collective-permute-start.4 = (f32[1,128,512]{2,1,0:T(8,128)S(1)}, f32[1,128,512]{2,1,0:T(8,128)S(1)}, u32[]{:S(2)}, u32[]{:S(2)}) collective-permute-start(f32[1,128,512]{2,1,0:T(8,128)S(1)} %get-tuple-element.49), channel_id=1, source_target_pairs={{0,1},{1,0},{2,3},{3,2},{4,5},{5,4},{6,7},{7,6},{8,9},{9,8},{10,11... | collective-permute-start | bytes 786440 | tf_op jit(solution)/shard_map/ppermute | solution.py:275
  23.6 2.9 %collective-permute-start.6 = (f32[1,128,512]{2,1,0:T(8,128)S(1)}, f32[1,128,512]{2,1,0:T(8,128)S(1)}, u32[]{:S(2)}, u32[]{:S(2)}) collective-permute-start(f32[1,128,512]{2,1,0:T(8,128)S(1)} %get-tuple-element.51), channel_id=1, source_target_pairs={{0,1},{1,0},{2,3},{3,2},{4,5},{5,4},{6,7},{7,6},{8,9},{9,8},{10,11... | collective-permute-start | bytes 786440 | tf_op jit(solution)/shard_map/ppermute | solution.py:275
  23.6 20.1 %collective-permute-start.3 = (f32[1,128,512]{2,1,0:T(8,128)S(1)}, f32[1,128,512]{2,1,0:T(8,128)S(1)}, u32[]{:S(2)}, u32[]{:S(2)}) collective-permute-start(f32[1,128,512]{2,1,0:T(8,128)S(1)} %get-tuple-element.47), channel_id=1, source_target_pairs={{0,1},{1,0},{2,3},{3,2},{4,5},{5,4},{6,7},{7,6},{8,9},{9,8},{10,11... | collective-permute-start | bytes 786440 | tf_op jit(solution)/shard_map/ppermute | solution.py:275
  26.1 21.6 %collective-permute-start.5 = (f32[1,128,512]{2,1,0:T(8,128)S(1)}, f32[1,128,512]{2,1,0:T(8,128)S(1)}, u32[]{:S(2)}, u32[]{:S(2)}) collective-permute-start(f32[1,128,512]{2,1,0:T(8,128)S(1)} %add.53), channel_id=1, source_target_pairs={{0,2},{1,3},{2,0},{3,1},{4,6},{5,7},{6,4},{7,5},{8,10},{9,11},{10,... | collective-permute-start | bytes 786440 | tf_op jit(solution)/shard_map/ppermute | solution.py:275
  48.2 1.6 collective-permute-start.9
  49.9 6.7 %collective-permute-start.12 = (f32[136,128]{1,0:T(8,128)S(1)}, f32[136,128]{1,0:T(8,128)S(1)}, u32[]{:S(2)}, u32[]{:S(2)}) collective-permute-start(f32[136,128]{1,0:T(8,128)S(1)} %get-tuple-element.62), channel_id=1, source_target_pairs={{0,6},{1,7},{2,4},{3,5},{4,2},{5,3},{6,0},{7,1},{8,14},{9,15},{10,... | collective-permute-start | bytes 208904 | tf_op jit(solution)/shard_map/ppermute | solution.py:283
  54.1 4.3 %collective-permute-start.11 = (f32[136,128]{1,0:T(8,128)S(1)}, f32[136,128]{1,0:T(8,128)S(1)}, u32[]{:S(2)}, u32[]{:S(2)}) collective-permute-start(f32[136,128]{1,0:T(8,128)S(1)} %get-tuple-element.63), channel_id=1, source_target_pairs={{0,2},{1,3},{2,0},{3,1},{4,6},{5,7},{6,4},{7,5},{8,10},{9,11},{10,... | collective-permute-start | bytes 208904 | tf_op jit(solution)/shard_map/ppermute | solution.py:275
  54.4 4.3 %collective-permute-start.10 = (f32[136,128]{1,0:T(8,128)S(1)}, f32[136,128]{1,0:T(8,128)S(1)}, u32[]{:S(2)}, u32[]{:S(2)}) collective-permute-start(f32[136,128]{1,0:T(8,128)S(1)} %get-tuple-element.64), channel_id=1, source_target_pairs={{0,4},{4,0},{8,12},{12,8},{16,20},{20,16},{24,28},{28,24},{1,5},{5... | collective-permute-start | bytes 208904 | tf_op jit(solution)/shard_map/ppermute | solution.py:277
  58.7 7.1 %collective-permute-start.15 = (f32[136,128]{1,0:T(8,128)S(1)}, f32[136,128]{1,0:T(8,128)S(1)}, u32[]{:S(2)}, u32[]{:S(2)}) collective-permute-start(f32[136,128]{1,0:T(8,128)S(1)} %fusion.5), channel_id=1, source_target_pairs={{0,24},{4,28},{8,16},{12,20},{16,8},{20,12},{24,0},{28,4},{1,25},{... | collective-permute-start | bytes 208904 | tf_op jit(solution)/shard_map/ppermute | solution.py:277
  62.8 6.1 %collective-permute-start.14 = (f32[136,128]{1,0:T(8,128)S(1)}, f32[136,128]{1,0:T(8,128)S(1)}, u32[]{:S(2)}, u32[]{:S(2)}) collective-permute-start(f32[136,128]{1,0:T(8,128)S(1)} %fusion.5), channel_id=1, source_target_pairs={{0,16},{4,20},{8,24},{12,28},{16,0},{20,4},{24,8},{28,12},{1,17},{... | collective-permute-start | bytes 208904 | tf_op jit(solution)/shard_map/ppermute | solution.py:277
  62.8 6.1 %collective-permute-start.13 = (f32[136,128]{1,0:T(8,128)S(1)}, f32[136,128]{1,0:T(8,128)S(1)}, u32[]{:S(2)}, u32[]{:S(2)}) collective-permute-start(f32[136,128]{1,0:T(8,128)S(1)} %fusion.5), channel_id=1, source_target_pairs={{0,8},{4,12},{8,0},{12,4},{16,24},{20,28},{24,16},{28,20},{1,9},{5... | collective-permute-start | bytes 208904 | tf_op jit(solution)/shard_map/ppermute | solution.py:277
  68.8 5.8 %collective-permute-start.18 = (f32[136,128]{1,0:T(8,128)S(1)}, f32[136,128]{1,0:T(8,128)S(1)}, u32[]{:S(2)}, u32[]{:S(2)}) collective-permute-start(f32[136,128]{1,0:T(8,128)S(1)} %add_add_fusion.refs_0_), channel_id=1, source_target_pairs={{0,6},{1,7},{2,4},{3,5},{4,2},{5,3},{6,0},{7,1},{8,14},{9,15},{10,... | collective-permute-start | bytes 208904 | tf_op jit(solution)/shard_map/ppermute | solution.py:283
  70.2 4.7 %collective-permute-start.17 = (f32[136,128]{1,0:T(8,128)S(1)}, f32[136,128]{1,0:T(8,128)S(1)}, u32[]{:S(2)}, u32[]{:S(2)}) collective-permute-start(f32[136,128]{1,0:T(8,128)S(1)} %add_add_fusion.refs_0_), channel_id=1, source_target_pairs={{0,2},{1,3},{2,0},{3,1},{4,6},{5,7},{6,4},{7,5},{8,10},{9,11},{10,... | collective-permute-start | bytes 208904 | tf_op jit(solution)/shard_map/ppermute | solution.py:275
  71.2 4.3 %collective-permute-start.16 = (f32[136,128]{1,0:T(8,128)S(1)}, f32[136,128]{1,0:T(8,128)S(1)}, u32[]{:S(2)}, u32[]{:S(2)}) collective-permute-start(f32[136,128]{1,0:T(8,128)S(1)} %add_add_fusion.refs_0_), channel_id=1, source_target_pairs={{0,4},{4,0},{8,12},{12,8},{16,20},{20,16},{24,28},{28,24},{1,5},{5... | collective-permute-start | bytes 208904 | tf_op jit(solution)/shard_map/ppermute | solution.py:277
  72.4 3.2 %collective-permute-start.19 = (f32[136,128]{1,0:T(8,128)S(1)}, f32[136,128]{1,0:T(8,128)S(1)}, u32[]{:S(2)}, u32[]{:S(2)}) collective-permute-start(f32[136,128]{1,0:T(8,128)S(1)} %add_add_fusion.refs_0_), channel_id=1, source_target_pairs={{0,1},{1,0},{2,3},{3,2},{4,5},{5,4},{6,7},{7,6},{8,9},{9,8},{10,11... | collective-permute-start | bytes 208904 | tf_op jit(solution)/shard_map/ppermute | solution.py:275
  74.6 1.3 collective-permute-start.22
  75.0 1.3 collective-permute-start.21
  75.5 1.3 collective-permute-start.20

commit v10 on v8

--- a/solution.py
+++ b/solution.py
@@ -448,8 +448,9 @@
             copies[-1].start()
 
         own_rows = jnp.concatenate([part[...] for part in rows], axis=0)
-        count = own_rows.shape[0] // 2
-        for n in range(2):
+        strips = 3 if own_rows.shape[0] % (3 * BLOCK) == 0 else 2
+        count = own_rows.shape[0] // strips
+        for n in range(strips):
             here = pl.ds(n * count, count)
             sh, sl = halves(own_rows[n * count : (n + 1) * count])
             for cols, k in ((low, size), (top, wide)):
@@ -559,7 +560,7 @@
             pltpu.VMEM(square, F32),
             pltpu.VMEM((local, width), F32),
             pltpu.VMEM(square, F32),
-            pltpu.SemaphoreType.DMA((5,)),
+            pltpu.SemaphoreType.DMA((7,)),
         ]
         + [pltpu.VMEM(square, BF16)] * 8,
         compiler_params=params(24 << 20),

time: 191 us -> 191 us (level)
  transfers between devices with their start and end apart: 23 -> 23, of which waited for: 15 -> 17; matrix products, arithmetic and copies ran while one was open for 0% -> 0% of each run, Pallas kernels for 5% -> 5%
where the time goes in v10:
time: 191 us
  Pallas kernels  131 us (69%)
  waiting for transfers between devices  38.1 us (20%)
  starting transfers between devices  20 us (10%)
    pallas_call x1, Pallas kernels, factor(): pl.pallas_call(functools.partial(factor_kernel, len(rows), scale, 6), out...  114 us
    ppermute x16, waiting for transfers between devices, swapped(): return lax.ppermute(x, 'col', [(c, c ^ col_flip) for c in range(cols)])  27.9 us
    pallas_call x2, Pallas kernels, tile_products(): pl.pallas_call(functools.partial(tile_kernel, resident, spans, stride), o...  15 us
    ppermute x16, starting transfers between devices, swapped(): return lax.ppermute(x, 'col', [(c, c ^ col_flip) for c in range(cols)])  9.42 us
    ppermute x5, waiting for transfers between devices, swapped(): return lax.ppermute(x, 'row', [(r, r ^ row_flip) for r in range(rows)])  6.36 us
    ppermute x5, starting transfers between devices, swapped(): return lax.ppermute(x, 'row', [(r, r ^ row_flip) for r in range(rows)])  6.27 us
    ppermute x2, starting transfers between devices, swapped(): return lax.ppermute(x, ('row', 'col'), route)  4.26 us
    ppermute x2, waiting for transfers between devices, swapped(): return lax.ppermute(x, ('row', 'col'), route)  3.86 us
  transfers between devices with their start and end apart: 23, of which 17 were waited for; matrix products, arithmetic and copies ran while one was open for 0% of the time, Pallas kernels for 5%

profile of v10, /device:TPU:0, one launch (start us, length us, event | category | flops | bytes accessed | tf_op | source)
XLA Modules:
  0.0 190.6 jit_solution(5133728681891998616)
XLA Ops:
  1.3 7.4 %shard_map.59 = (f32[1,128,512]{2,1,0:T(8,128)S(1)}, f32[4,128,512]{2,1,0:T(8,128)S(1)}, f32[1,128,512]{2,1,0:T(8,128)S(1)}, f32[4,128,512]{2,1,0:T(8,128)S(1)}) custom-call(s32[1,1]{1,0:T(1,128)S(6)} %copy.6.counts, s32[2,360]{1,0:T(2,128)} %bitcast.19, bf16[360,128,128]{2,1,0:T(8,128)(2,1)} %bitcast.15, bf16[48,128,512]{2,1,0:T(8,128)(2,1)} %bitcast.17), custom_call_target="tpu_custom_call" | custom-call | tf_op jit(solution)/shard_map/pallas_call | solution.py:165
  8.6 0.5 collective-permute-start
  9.2 1.2 collective-permute-done
  10.3 0.4 collective-permute-start.1
  10.7 2.6 %collective-permute-start.2 = (f32[1,128,512]{2,1,0:T(8,128)S(1)}, f32[1,128,512]{2,1,0:T(8,128)S(1)}, u32[]{:S(2)}, u32[]{:S(2)}) collective-permute-start(f32[1,128,512]{2,1,0:T(8,128)S(1)} %add.51), channel_id=1, source_target_pairs={{0,2},{1,3},{2,0},{3,1},{4,6},{5,7},{6,4},{7,5},{8,10},{9,11},{10,... | collective-permute-start | bytes 786440 | tf_op jit(solution)/shard_map/ppermute | solution.py:275
  13.4 0.0 collective-permute-done.1
  13.4 0.2 add.52
  13.6 2.5 %collective-permute-start.8 = (f32[4,128,512]{2,1,0:T(8,128)S(1)}, f32[4,128,512]{2,1,0:T(8,128)S(1)}, u32[]{:S(2)}, u32[]{:S(2)}) collective-permute-start(f32[4,128,512]{2,1,0:T(8,128)S(1)} %add.52), channel_id=1, source_target_pairs={{0,2},{1,3},{2,0},{3,1},{4,6},{5,7},{6,4},{7,5},{8,10},{9,11},{10,... | collective-permute-start | bytes 3145736 | tf_op jit(solution)/shard_map/ppermute | solution.py:275
  16.1 7.6 %shard_map.60 = (f32[1,128,512]{2,1,0:T(8,128)S(1)}, f32[1,128,512]{2,1,0:T(8,128)S(1)}, f32[4,128,512]{2,1,0:T(8,128)S(1)}, f32[1,128,512]{2,1,0:T(8,128)S(1)},...) custom-call(s32[1,1]{1,0:T(1,128)S(6)} %copy.6.counts, ...), custom_call_target="tpu_custom_call" | custom-call | tf_op jit(solution)/shard_map/pallas_call | solution.py:165
  23.7 0.0 collective-permute-done.2.refs_2_
  23.7 0.8 collective-permute-start.7
  24.5 0.1 collective-permute-start.4
  24.6 0.4 collective-permute-start.6
  25.0 0.1 collective-permute-start.3
  25.1 2.1 %collective-permute-done.4 = f32[1,128,512]{2,1,0:T(8,128)S(1)} collective-permute-done((f32[1,128,512]{2,1,0:T(8,128)S(1)}, f32[1,128,512]{2,1,0:T(8,128)S(1)}, u32[]{:S(2)}, u32[]{:S(2)}) %collective-permute-start.4) | collective-permute-done | bytes 262176 | tf_op jit(solution)/shard_map/ppermute | solution.py:275
  27.2 0.1 collective-permute-start.5
  27.3 0.3 collective-permute-done.6.refs_1_
  27.5 0.4 shard_map.61
  27.9 15.1 %collective-permute-done.8.refs_2_ = f32[4,128,512]{2,1,0:T(8,128)S(1)} collective-permute-done((f32[4,128,512]{2,1,0:T(8,128)S(1)}, f32[4,128,512]{2,1,0:T(8,128)S(1)}, u32[]{:S(2)}, u32[]{:S(2)}) %collective-permute-start.8) | collective-permute-done | bytes 1048608 | tf_op jit(solution)/shard_map/ppermute | solution.py:275
  43.0 0.0 collective-permute-done.7.refs_1_
  43.0 1.1 shard_map.62
  44.1 4.2 %collective-permute-done.5.refs_2_ = f32[1,128,512]{2,1,0:T(8,128)S(1)} collective-permute-done((f32[1,128,512]{2,1,0:T(8,128)S(1)}, f32[1,128,512]{2,1,0:T(8,128)S(1)}, u32[]{:S(2)}, u32[]{:S(2)}) %collective-permute-start.5) | collective-permute-done | bytes 262176 | tf_op jit(solution)/shard_map/ppermute | solution.py:275
  48.3 0.5 shard_map.63
  48.8 0.1 collective-permute-start.9
  48.8 1.5 collective-permute-done.9
  50.4 2.7 %collective-permute-start.12 = (f32[136,128]{1,0:T(8,128)S(1)}, f32[136,128]{1,0:T(8,128)S(1)}, u32[]{:S(2)}, u32[]{:S(2)}) collective-permute-start(f32[136,128]{1,0:T(8,128)S(1)} %get-tuple-element.62), channel_id=1, source_target_pairs={{0,6},{1,7},{2,4},{3,5},{4,2},{5,3},{6,0},{7,1},{8,14},{9,15},{10,... | collective-permute-start | bytes 208904 | tf_op jit(solution)/shard_map/ppermute | solution.py:283
  53.1 0.5 collective-permute-start.11
  53.7 0.3 collective-permute-start.10
  54.0 1.7 collective-permute-done.12
  55.7 1.8 collective-permute-done.11
  57.5 0.5 collective-permute-done.10
  58.0 4.7 %collective-permute-start.15 = (f32[136,128]{1,0:T(8,128)S(1)}, f32[136,128]{1,0:T(8,128)S(1)}, u32[]{:S(2)}, u32[]{:S(2)}) collective-permute-start(f32[136,128]{1,0:T(8,128)S(1)} %fusion.5), channel_id=1, source_target_pairs={{0,24},{4,28},{8,16},{12,20},{16,8},{20,12},{24,0},{28,4},{1,25},{... | collective-permute-start | bytes 208904 | tf_op jit(solution)/shard_map/ppermute | solution.py:277
  62.7 0.0 collective-permute-start.14
  62.7 0.6 collective-permute-start.13
  63.3 1.7 collective-permute-done.15
  65.0 2.9 %collective-permute-done.14 = f32[136,128]{1,0:T(8,128)S(1)} collective-permute-done((f32[136,128]{1,0:T(8,128)S(1)}, f32[136,128]{1,0:T(8,128)S(1)}, u32[]{:S(2)}, u32[]{:S(2)}) %collective-permute-start.14) | collective-permute-done | bytes 69664 | tf_op jit(solution)/shard_map/ppermute | solution.py:277
  67.9 0.3 collective-permute-done.13
  68.2 1.5 collective-permute-start.18
  69.8 1.4 collective-permute-start.17
  71.1 0.7 collective-permute-start.16
  71.8 2.1 %collective-permute-done.18.refs_3_ = f32[136,128]{1,0:T(8,128)S(1)} collective-permute-done((f32[136,128]{1,0:T(8,128)S(1)}, f32[136,128]{1,0:T(8,128)S(1)}, u32[]{:S(2)}, u32[]{:S(2)}) %collective-permute-start.18) | collective-permute-done | bytes 69664 | tf_op jit(solution)/shard_map/ppermute | solution.py:283
  73.9 0.0 collective-permute-start.22
  73.9 0.6 collective-permute-done.17.refs_2_
  74.5 0.9 collective-permute-done.16.refs_1_
  75.4 0.0 collective-permute-done.22.refs_7_
  75.5 0.3 collective-permute-done.21.refs_6_
  75.7 1.0 collective-permute-done.20.refs_5_
  76.7 113.7 %shard_map.64 = (f32[768,512]{1,0:T(8,128)}, f32[512,512]{1,0:T(8,128)}) custom-call(f32[136,128]{1,0:T(8,128)S(1)} %add_add_fusion.refs_0_, f32[136,128]{1,0:T(8,128)S(1)} %collective-permute-done.16.refs_1_, f32[136,128]{1,0:T(8,128)S(1)} %collective-permute-done.17.refs_2_, f32[136,128]{1,0:T(8,128)S(1)} %collective-permute-done.18.refs_3_, ...), custom_call_target="tpu_custom_call" | custom-call | tf_op jit(solution)/shard_map/pallas_call | solution.py:547
  (10 shorter events, 0.1 us)
Async XLA Ops:
  8.6 1.7 collective-permute-start
  10.3 3.1 %collective-permute-start.1 = (f32[4,128,512]{2,1,0:T(8,128)S(1)}, f32[4,128,512]{2,1,0:T(8,128)S(1)}, u32[]{:S(2)}, u32[]{:S(2)}) collective-permute-start(f32[4,128,512]{2,1,0:T(8,128)S(1)} %get-tuple-element.36), channel_id=1, source_target_pairs={{0,1},{1,0},{2,3},{3,2},{4,5},{5,4},{6,7},{7,6},{8,9},{9,8},{10,11... | collective-permute-start | bytes 3145736 | tf_op jit(solution)/shard_map/ppermute | solution.py:275
  10.7 12.9 %collective-permute-start.2 = (f32[1,128,512]{2,1,0:T(8,128)S(1)}, f32[1,128,512]{2,1,0:T(8,128)S(1)}, u32[]{:S(2)}, u32[]{:S(2)}) collective-permute-start(f32[1,128,512]{2,1,0:T(8,128)S(1)} %add.51), channel_id=1, source_target_pairs={{0,2},{1,3},{2,0},{3,1},{4,6},{5,7},{6,4},{7,5},{8,10},{9,11},{10,... | collective-permute-start | bytes 786440 | tf_op jit(solution)/shard_map/ppermute | solution.py:275
  13.6 29.4 %collective-permute-start.8 = (f32[4,128,512]{2,1,0:T(8,128)S(1)}, f32[4,128,512]{2,1,0:T(8,128)S(1)}, u32[]{:S(2)}, u32[]{:S(2)}) collective-permute-start(f32[4,128,512]{2,1,0:T(8,128)S(1)} %add.52), channel_id=1, source_target_pairs={{0,2},{1,3},{2,0},{3,1},{4,6},{5,7},{6,4},{7,5},{8,10},{9,11},{10,... | collective-permute-start | bytes 3145736 | tf_op jit(solution)/shard_map/ppermute | solution.py:275
  23.7 19.3 %collective-permute-start.7 = (f32[4,128,512]{2,1,0:T(8,128)S(1)}, f32[4,128,512]{2,1,0:T(8,128)S(1)}, u32[]{:S(2)}, u32[]{:S(2)}) collective-permute-start(f32[4,128,512]{2,1,0:T(8,128)S(1)} %get-tuple-element.55), channel_id=1, source_target_pairs={{0,1},{1,0},{2,3},{3,2},{4,5},{5,4},{6,7},{7,6},{8,9},{9,8},{10,11... | collective-permute-start | bytes 3145736 | tf_op jit(solution)/shard_map/ppermute | solution.py:275
  24.5 2.7 %collective-permute-start.4 = (f32[1,128,512]{2,1,0:T(8,128)S(1)}, f32[1,128,512]{2,1,0:T(8,128)S(1)}, u32[]{:S(2)}, u32[]{:S(2)}) collective-permute-start(f32[1,128,512]{2,1,0:T(8,128)S(1)} %get-tuple-element.49), channel_id=1, source_target_pairs={{0,1},{1,0},{2,3},{3,2},{4,5},{5,4},{6,7},{7,6},{8,9},{9,8},{10,11... | collective-permute-start | bytes 786440 | tf_op jit(solution)/shard_map/ppermute | solution.py:275
  24.6 3.0 %collective-permute-start.6 = (f32[1,128,512]{2,1,0:T(8,128)S(1)}, f32[1,128,512]{2,1,0:T(8,128)S(1)}, u32[]{:S(2)}, u32[]{:S(2)}) collective-permute-start(f32[1,128,512]{2,1,0:T(8,128)S(1)} %get-tuple-element.51), channel_id=1, source_target_pairs={{0,1},{1,0},{2,3},{3,2},{4,5},{5,4},{6,7},{7,6},{8,9},{9,8},{10,11... | collective-permute-start | bytes 786440 | tf_op jit(solution)/shard_map/ppermute | solution.py:275
  25.0 19.1 %collective-permute-start.3 = (f32[1,128,512]{2,1,0:T(8,128)S(1)}, f32[1,128,512]{2,1,0:T(8,128)S(1)}, u32[]{:S(2)}, u32[]{:S(2)}) collective-permute-start(f32[1,128,512]{2,1,0:T(8,128)S(1)} %get-tuple-element.47), channel_id=1, source_target_pairs={{0,1},{1,0},{2,3},{3,2},{4,5},{5,4},{6,7},{7,6},{8,9},{9,8},{10,11... | collective-permute-start | bytes 786440 | tf_op jit(solution)/shard_map/ppermute | solution.py:275
  27.2 21.1 %collective-permute-start.5 = (f32[1,128,512]{2,1,0:T(8,128)S(1)}, f32[1,128,512]{2,1,0:T(8,128)S(1)}, u32[]{:S(2)}, u32[]{:S(2)}) collective-permute-start(f32[1,128,512]{2,1,0:T(8,128)S(1)} %add.53), channel_id=1, source_target_pairs={{0,2},{1,3},{2,0},{3,1},{4,6},{5,7},{6,4},{7,5},{8,10},{9,11},{10,... | collective-permute-start | bytes 786440 | tf_op jit(solution)/shard_map/ppermute | solution.py:275
  48.8 1.6 collective-permute-start.9
  50.4 5.3 %collective-permute-start.12 = (f32[136,128]{1,0:T(8,128)S(1)}, f32[136,128]{1,0:T(8,128)S(1)}, u32[]{:S(2)}, u32[]{:S(2)}) collective-permute-start(f32[136,128]{1,0:T(8,128)S(1)} %get-tuple-element.62), channel_id=1, source_target_pairs={{0,6},{1,7},{2,4},{3,5},{4,2},{5,3},{6,0},{7,1},{8,14},{9,15},{10,... | collective-permute-start | bytes 208904 | tf_op jit(solution)/shard_map/ppermute | solution.py:283
  53.1 4.3 %collective-permute-start.11 = (f32[136,128]{1,0:T(8,128)S(1)}, f32[136,128]{1,0:T(8,128)S(1)}, u32[]{:S(2)}, u32[]{:S(2)}) collective-permute-start(f32[136,128]{1,0:T(8,128)S(1)} %get-tuple-element.63), channel_id=1, source_target_pairs={{0,2},{1,3},{2,0},{3,1},{4,6},{5,7},{6,4},{7,5},{8,10},{9,11},{10,... | collective-permute-start | bytes 208904 | tf_op jit(solution)/shard_map/ppermute | solution.py:275
  53.7 4.3 %collective-permute-start.10 = (f32[136,128]{1,0:T(8,128)S(1)}, f32[136,128]{1,0:T(8,128)S(1)}, u32[]{:S(2)}, u32[]{:S(2)}) collective-permute-start(f32[136,128]{1,0:T(8,128)S(1)} %get-tuple-element.64), channel_id=1, source_target_pairs={{0,4},{4,0},{8,12},{12,8},{16,20},{20,16},{24,28},{28,24},{1,5},{5... | collective-permute-start | bytes 208904 | tf_op jit(solution)/shard_map/ppermute | solution.py:277
  58.0 7.1 %collective-permute-start.15 = (f32[136,128]{1,0:T(8,128)S(1)}, f32[136,128]{1,0:T(8,128)S(1)}, u32[]{:S(2)}, u32[]{:S(2)}) collective-permute-start(f32[136,128]{1,0:T(8,128)S(1)} %fusion.5), channel_id=1, source_target_pairs={{0,24},{4,28},{8,16},{12,20},{16,8},{20,12},{24,0},{28,4},{1,25},{... | collective-permute-start | bytes 208904 | tf_op jit(solution)/shard_map/ppermute | solution.py:277
  62.7 5.3 %collective-permute-start.14 = (f32[136,128]{1,0:T(8,128)S(1)}, f32[136,128]{1,0:T(8,128)S(1)}, u32[]{:S(2)}, u32[]{:S(2)}) collective-permute-start(f32[136,128]{1,0:T(8,128)S(1)} %fusion.5), channel_id=1, source_target_pairs={{0,16},{4,20},{8,24},{12,28},{16,0},{20,4},{24,8},{28,12},{1,17},{... | collective-permute-start | bytes 208904 | tf_op jit(solution)/shard_map/ppermute | solution.py:277
  62.7 5.5 %collective-permute-start.13 = (f32[136,128]{1,0:T(8,128)S(1)}, f32[136,128]{1,0:T(8,128)S(1)}, u32[]{:S(2)}, u32[]{:S(2)}) collective-permute-start(f32[136,128]{1,0:T(8,128)S(1)} %fusion.5), channel_id=1, source_target_pairs={{0,8},{4,12},{8,0},{12,4},{16,24},{20,28},{24,16},{28,20},{1,9},{5... | collective-permute-start | bytes 208904 | tf_op jit(solution)/shard_map/ppermute | solution.py:277
  68.2 5.7 %collective-permute-start.18 = (f32[136,128]{1,0:T(8,128)S(1)}, f32[136,128]{1,0:T(8,128)S(1)}, u32[]{:S(2)}, u32[]{:S(2)}) collective-permute-start(f32[136,128]{1,0:T(8,128)S(1)} %add_add_fusion.refs_0_), channel_id=1, source_target_pairs={{0,6},{1,7},{2,4},{3,5},{4,2},{5,3},{6,0},{7,1},{8,14},{9,15},{10,... | collective-permute-start | bytes 208904 | tf_op jit(solution)/shard_map/ppermute | solution.py:283
  69.8 4.7 %collective-permute-start.17 = (f32[136,128]{1,0:T(8,128)S(1)}, f32[136,128]{1,0:T(8,128)S(1)}, u32[]{:S(2)}, u32[]{:S(2)}) collective-permute-start(f32[136,128]{1,0:T(8,128)S(1)} %add_add_fusion.refs_0_), channel_id=1, source_target_pairs={{0,2},{1,3},{2,0},{3,1},{4,6},{5,7},{6,4},{7,5},{8,10},{9,11},{10,... | collective-permute-start | bytes 208904 | tf_op jit(solution)/shard_map/ppermute | solution.py:275
  71.1 4.3 %collective-permute-start.16 = (f32[136,128]{1,0:T(8,128)S(1)}, f32[136,128]{1,0:T(8,128)S(1)}, u32[]{:S(2)}, u32[]{:S(2)}) collective-permute-start(f32[136,128]{1,0:T(8,128)S(1)} %add_add_fusion.refs_0_), channel_id=1, source_target_pairs={{0,4},{4,0},{8,12},{12,8},{16,20},{20,16},{24,28},{28,24},{1,5},{5... | collective-permute-start | bytes 208904 | tf_op jit(solution)/shard_map/ppermute | solution.py:277
  71.8 3.7 %collective-permute-start.19 = (f32[136,128]{1,0:T(8,128)S(1)}, f32[136,128]{1,0:T(8,128)S(1)}, u32[]{:S(2)}, u32[]{:S(2)}) collective-permute-start(f32[136,128]{1,0:T(8,128)S(1)} %add_add_fusion.refs_0_), channel_id=1, source_target_pairs={{0,1},{1,0},{2,3},{3,2},{4,5},{5,4},{6,7},{7,6},{8,9},{9,8},{10,11... | collective-permute-start | bytes 208904 | tf_op jit(solution)/shard_map/ppermute | solution.py:275
  73.9 1.5 collective-permute-start.22
  74.5 1.3 collective-permute-start.21
  75.4 1.3 collective-permute-start.20
